TPU v7x, 32 devices: a whole 2x2x4 slice. The times are simulated.
32 devices in a mesh: crop: 2 (over core), row: 4 (over y, x), col: 4 (over z).
Axes of the slice: x: 2, y: 2, z: 4, core: 2. Of those that a mesh axis runs over, the one named last changes fastest.
Arguments:
- pair_state: bfloat16 [192, 96, 128], P(('crop', 'row'), 'col'), parts along dimension 0, may hold values from -6 to 6
- token_mask: int32 [192], P('crop'), parts along dimension 0, may hold values from 0 to 1, as said below
- block_pattern: int32 [8, 4], P('crop'), parts along dimension 0, may hold values from 0 to 1, as said below
- triangle_norm: float32 [128], replicated, may hold values from 0.1 to 1.9
- triangle_input: bfloat16 [128, 512], replicated, may hold values from -0.5 to 0.5
- triangle_gate: bfloat16 [128, 128], replicated, may hold values from -0.5 to 0.5
- product_norm: float32 [128], replicated, may hold values from 0.1 to 1.9
- triangle_output: bfloat16 [128, 128], replicated, may hold values from -0.5 to 0.5
- attend_norm: float32 [128], replicated, may hold values from 0.1 to 1.9
- attend_inputs: bfloat16 [128, 384], replicated, may hold values from -4 to 4
- attend_gate: bfloat16 [128, 128], replicated, may hold values from -0.5 to 0.5
- attend_bias: bfloat16 [128, 4], replicated, may hold values from -0.5 to 0.5
- attend_output: bfloat16 [128, 128], replicated, may hold values from -0.5 to 0.5
Outputs:
- pair_output: bfloat16 [192, 96, 128], P(('crop', 'row'), 'col'), parts along dimension 0
There are 2 independent parts, one for each index of `crop`. A program takes and returns all parts, laid end to end along the dimension named above; an argument that names none is the same for every part. Nothing has to cross between parts.
Inputs may be any that keep to these rules, and one draw needn't show every extreme that they name: `token_mask`: 1 on a prefix of 24 or more tokens and 0 after it. `block_pattern`: every row allows its own block and block 0.
All inputs are finite; a program needn't handle non-finite values.
Results may differ from a plain program's by a relative error of at most 0.02.
Values may be sent and summed in bfloat16 or wider, within the bound.
No kernel may reach another device: no remote copies, remote signals or barrier semaphores. Data moves between devices by JAX's collectives and lax.ppermute only.
A program may use at most 64 MiB of HBM per device.

v0:
```python
import math

import jax
import jax.numpy as jnp
from jax import lax
from jax.sharding import PartitionSpec as P

norm_epsilon = 1e-05


def layer_norm(inputs, gain):
    average = jnp.mean(inputs, axis=-1, keepdims=True)
    centered = inputs - average
    variance = jnp.mean(centered * centered, axis=-1, keepdims=True)
    return centered * lax.rsqrt(variance + norm_epsilon) * gain


def project_rows(pair_rows, attend_inputs, attend_gate, head_count):
    row_count, token_count, channels = pair_rows.shape
    head_width = channels // head_count
    combined = jnp.dot(pair_rows, attend_inputs, preferred_element_type=jnp.float32)
    queries = (
        combined[..., :channels]
        .astype(jnp.bfloat16)
        .reshape(row_count, token_count, head_count, head_width)
    )
    key_rows = (
        combined[..., channels : 2 * channels]
        .astype(jnp.bfloat16)
        .reshape(row_count, token_count, head_count, head_width)
    )
    values = (
        combined[..., 2 * channels :]
        .astype(jnp.bfloat16)
        .reshape(row_count, token_count, head_count, head_width)
    )
    gate_values = jax.nn.sigmoid(
        jnp.dot(pair_rows, attend_gate, preferred_element_type=jnp.float32)
    )
    return (queries, key_rows, values, gate_values)


def attend_dense(pair_rows, attend_inputs, attend_gate, head_bias, allowed):
    row_count, token_count, channels = pair_rows.shape
    head_count = head_bias.shape[0]
    queries, key_rows, values, gate_values = project_rows(
        pair_rows, attend_inputs, attend_gate, head_count
    )
    scores = jnp.einsum(
        "rjhd,rkhd->rhjk", queries, key_rows, preferred_element_type=jnp.float32
    ) / math.sqrt(channels // head_count)
    scores = scores + head_bias.astype(jnp.float32)[None]
    scores = jnp.where(allowed[None, None], scores, -jnp.inf)
    row_max = jnp.max(scores, axis=-1, keepdims=True)
    weights = jnp.exp(scores - row_max)
    probabilities = (weights / jnp.sum(weights, axis=-1, keepdims=True)).astype(jnp.bfloat16)
    attended = jnp.einsum(
        "rhjk,rkhd->rjhd", probabilities, values, preferred_element_type=jnp.float32
    ).reshape(row_count, token_count, channels)
    return (gate_values * attended).astype(jnp.bfloat16)


def shards(
    pair_state,
    token_mask,
    block_pattern,
    triangle_norm,
    triangle_input,
    triangle_gate,
    product_norm,
    triangle_output,
    attend_norm,
    attend_inputs,
    attend_gate,
    attend_bias,
    attend_output,
):
    tile_rows, tile_columns, channels = pair_state.shape
    row_devices = lax.axis_size("row")
    column_devices = lax.axis_size("col")
    token_count = tile_columns * column_devices
    row_index = lax.axis_index("row")
    column_index = lax.axis_index("col")
    valid_tokens = token_mask.astype(jnp.float32)
    row_valid = lax.dynamic_slice_in_dim(valid_tokens, row_index * tile_rows, tile_rows)
    column_valid = lax.dynamic_slice_in_dim(valid_tokens, column_index * tile_columns, tile_columns)
    state_float = pair_state.astype(jnp.float32)
    normed = layer_norm(state_float, triangle_norm).astype(jnp.bfloat16)
    projected = jnp.dot(normed, triangle_input, preferred_element_type=jnp.float32)
    pair_valid = (row_valid[:, None] * column_valid[None, :])[:, :, None]
    left_factor = (
        pair_valid
        * jax.nn.sigmoid(projected[..., :channels])
        * projected[..., channels : 2 * channels]
    ).astype(jnp.bfloat16)
    right_factor = (
        pair_valid
        * jax.nn.sigmoid(projected[..., 2 * channels : 3 * channels])
        * projected[..., 3 * channels :]
    ).astype(jnp.bfloat16)
    left_panel = lax.all_gather(left_factor, "col", axis=1, tiled=True)
    right_stacked = lax.all_gather(right_factor, "row", axis=0, tiled=True)
    right_rows = lax.all_to_all(right_stacked, "col", split_axis=0, concat_axis=1, tiled=True)
    summed = lax.dot_general(
        left_panel, right_rows, (((1,), (1,)), ((2,), (2,))), preferred_element_type=jnp.float32
    )
    product = jnp.transpose(summed, (1, 2, 0))
    product_normed = layer_norm(product, product_norm).astype(jnp.bfloat16)
    gate_values = jax.nn.sigmoid(jnp.dot(normed, triangle_gate, preferred_element_type=jnp.float32))
    middle = (
        state_float
        + gate_values * jnp.dot(product_normed, triangle_output, preferred_element_type=jnp.float32)
    ).astype(jnp.bfloat16)
    attend_normed = layer_norm(middle.astype(jnp.float32), attend_norm).astype(jnp.bfloat16)
    head_count = attend_bias.shape[1]
    bias_tile = jnp.dot(attend_normed, attend_bias, preferred_element_type=jnp.float32).astype(
        jnp.bfloat16
    )
    flat_bias = jnp.transpose(bias_tile, (2, 0, 1)).reshape(head_count, tile_rows * tile_columns)
    gathered = lax.all_gather(flat_bias, ("row", "col"), axis=1, tiled=True)
    head_bias = gathered.reshape(head_count, row_devices, column_devices, tile_rows, tile_columns)
    head_bias = jnp.transpose(head_bias, (0, 1, 3, 2, 4)).reshape(
        head_count, token_count, token_count
    )
    blocks = block_pattern.shape[0]
    block_width = token_count // blocks
    pattern_ok = block_pattern[:, None, :, None] > 0
    allowed = jnp.broadcast_to(pattern_ok, (blocks, block_width, blocks, block_width)).reshape(
        token_count, token_count
    ) & (token_mask[None, :] > 0)
    rows_each = tile_rows // column_devices
    grouped = attend_normed.reshape(column_devices, rows_each, tile_columns, channels)
    received = lax.all_to_all(grouped, "col", split_axis=0, concat_axis=2, tiled=True)
    outer, inner, tokens_here, width_here = received.shape
    flat = received.reshape(outer * inner, tokens_here, width_here)
    attended_rows = attend_dense(flat, attend_inputs, attend_gate, head_bias, allowed).reshape(
        outer, inner, tokens_here, width_here
    )
    returned = lax.all_to_all(attended_rows, "col", split_axis=2, concat_axis=0, tiled=True)
    returned = returned.reshape(tile_rows, tile_columns, channels)
    update = jnp.dot(returned, attend_output, preferred_element_type=jnp.float32)
    return (middle.astype(jnp.float32) + update).astype(jnp.bfloat16)


def solution(mesh):
    return jax.shard_map(
        shards,
        mesh=mesh,
        in_specs=(
            P(("crop", "row"), "col", None),
            P("crop"),
            P("crop", None),
            P(),
            P(),
            P(),
            P(),
            P(),
            P(),
            P(),
            P(),
            P(),
            P(),
        ),
        out_specs=P(("crop", "row"), "col", None),
        check_vma=False,
    )
```

profile of v0, /device:TPU:0, one launch (start us, length us, event | category | flops | bytes accessed | tf_op | source)
XLA Modules:
  0.0 119.5 jit_solution(7626349759795496379)
XLA Ops:
  0.0 0.7 convert_element_type.65
  0.7 1.1 convert_reduce_fusion
  1.8 1.2 fusion.22
  3.1 1.3 %fusion.38 = f32[24,24,512]{2,1,0:T(8,128)S(1)} fusion(bf16[128,512]{1,0:T(8,128)(2,1)S(1)} %copy-done, bf16[24,24,128]{2,1,0:T(8,128)(2,1)} %param.13, f32[128]{0:T(128)} %param.16, f32[24,24]{1,0:T(8,128)S(1)} %add_rsqrt_fusion.2, f32[24,24]{1,0:T(8,128)S(1)} %broadcast_multiply_fusion.3), kind=kOutput, calls=%fused_computation.58 | convolution fusion | flops 75866112 | bytes 1463296 | tf_op jit(solution)/shard_map/dot_general | solution.py:89
  4.6 12.6 %all_gather.10 = bf16[96,24,128]{2,1,0:T(8,128)(2,1)} all-gather(bf16[24,24,128]{2,1,0:T(8,128)(2,1)S(1)} %get-tuple-element.5), channel_id=1, replica_groups=mesh['crop'=2,'row'=4,'col'=4] {'row'}, dimensions={0}, use_global_device_ids=true | all-gather | bytes 737280 | tf_op jit(solution)/shard_map/all_gather | solution.py:102
  17.3 4.9 %all-to-all-start = ((bf16[96,24,128]{2,1,0:T(8,128)(2,1)}), bf16[96,24,128]{2,1,0:T(8,128)(2,1)S(1)}, u32[]{:S(2)}, u32[]{:S(2)}) async-start(bf16[96,24,128]{2,1,0:T(8,128)(2,1)} %all_gather.10), calls=%async_computation | async-start | bytes 1179648 | tf_op jit(solution)/shard_map/all_to_all | solution.py:103
  22.2 26.3 %all_gather.9 = bf16[24,96,128]{2,1,0:T(8,128)(2,1)S(1)} all-gather(bf16[24,24,128]{2,1,0:T(8,128)(2,1)S(1)} %get-tuple-element.6), channel_id=1, replica_groups=mesh['crop'=2,'row'=4,'col'=4] {'col'}, dimensions={1}, use_global_device_ids=true | all-gather | bytes 737280 | tf_op jit(solution)/shard_map/all_gather | solution.py:101
  48.5 0.4 copy.89
  49.4 1.1 fusion.12
  50.6 0.4 copy.90
  51.0 0.5 fusion.55
  51.6 0.5 copy.91
  52.6 0.4 fusion.53
  53.3 0.9 multiply_convert_fusion
  54.2 1.3 %fusion.18 = bf16[4,24,24]{2,0,1:T(4,128)(2,1)S(1)} fusion(bf16[24,24,128]{2,1,0:T(8,128)(2,1)} %multiply_convert_fusion, bf16[128,4]{0,1:T(4,128)(2,1)S(1)} %copy-done.7), kind=kOutput, calls=%fused_computation.26 | convolution fusion | flops 592128 | bytes 153088 | tf_op jit(solution)/shard_map/dot_general | solution.py:116
  55.6 41.3 %all-gather = bf16[16,576,4]{1,2,0:T(4,128)(2,1)S(1)} all-gather(bf16[1,576,4]{1,2,0:T(4,128)(2,1)S(1)} %bitcast.94), channel_id=1, replica_groups=mesh['crop'=2,'row'=4,'col'=4] {'row','col'}, dimensions={0}, use_global_device_ids=true | all-gather | bytes 78336 | tf_op jit(solution)/shard_map/all_gather | solution.py:120
  96.8 3.3 %all-to-all-start.1 = ((bf16[4,6,24,128]{3,2,1,0:T(8,128)(2,1)}), bf16[4,6,24,128]{3,2,1,0:T(8,128)(2,1)S(1)}, u32[]{:S(2)}, u32[]{:S(2)}) async-start(bf16[4,6,24,128]{3,2,1,0:T(8,128)(2,1)} %bitcast.7), calls=%async_computation.1 | async-start | bytes 294912 | tf_op jit(solution)/shard_map/all_to_all | solution.py:133
  100.3 0.6 reshape.145
  101.6 4.5 %all-to-all-done.1 = bf16[4,6,24,128]{3,2,1,0:T(8,128)(2,1)S(1)} async-done(((bf16[4,6,24,128]{3,2,1,0:T(8,128)(2,1)}), bf16[4,6,24,128]{3,2,1,0:T(8,128)(2,1)S(1)}, u32[]{:S(2)}, u32[]{:S(2)}) %all-to-all-start.1) | async-done | bytes 147488 | tf_op jit(solution)/shard_map/all_to_all | solution.py:133
  106.9 0.4 fusion.3
  107.2 0.6 fusion.54
  108.1 0.4 fusion.19
  109.1 9.5 %all_to_all.48 = bf16[1,6,96,128]{3,1,0,2:T(8,128)(2,1)S(1)} all-to-all(bf16[1,6,96,128]{3,1,0,2:T(8,128)(2,1)S(1)} %copy.103), channel_id=1, replica_groups=mesh['crop'=2,'row'=4,'col'=4] {'col'}, dimensions={2} | all-to-all | bytes 294912 | tf_op jit(solution)/shard_map/all_to_all | solution.py:139
  118.6 0.9 fusion.16
  (64 shorter events, 4.1 us)
Async XLA Ops:
  0.0 3.1 %copy-start = (bf16[128,512]{1,0:T(8,128)(2,1)S(1)}, bf16[128,512]{1,0:T(8,128)(2,1)}, u32[]{:S(2)}) copy-start(bf16[128,512]{1,0:T(8,128)(2,1)} %param.17) | copy-start | bytes 393220
  17.3 33.2 %all-to-all-start = ((bf16[96,24,128]{2,1,0:T(8,128)(2,1)}), bf16[96,24,128]{2,1,0:T(8,128)(2,1)S(1)}, u32[]{:S(2)}, u32[]{:S(2)}) async-start(bf16[96,24,128]{2,1,0:T(8,128)(2,1)} %all_gather.10), calls=%async_computation | async-start | bytes 1179648 | tf_op jit(solution)/shard_map/all_to_all | solution.py:103
  22.1 26.8 %copy-start.6 = (s32[4,4]{1,0:T(4,128)S(1)}, s32[4,4]{1,0:T(4,128)}, u32[]{:S(2)}) copy-start(s32[4,4]{1,0:T(4,128)} %param.15) | copy-start | bytes 196
  22.1 27.1 %copy-start.13 = (s32[96]{0:T(128)S(1)}, s32[96]{0:T(128)}, u32[]{:S(2)}) copy-start(s32[96]{0:T(128)} %param.14) | copy-start | bytes 1156
  22.1 27.2 %copy-start.1 = (bf16[24,24,128]{2,1,0:T(8,128)(2,1)S(1)}, bf16[24,24,128]{2,1,0:T(8,128)(2,1)}, u32[]{:S(2)}) copy-start(bf16[24,24,128]{2,1,0:T(8,128)(2,1)} %param.13) | copy-start | bytes 442372
  22.1 27.2 %copy-start.8 = (f32[128]{0:T(128)S(1)}, f32[128]{0:T(128)}, u32[]{:S(2)}) copy-start(f32[128]{0:T(128)} %param.16) | copy-start | bytes 1540
  22.2 27.2 %copy-start.11 = (bf16[128,128]{1,0:T(8,128)(2,1)S(1)}, bf16[128,128]{1,0:T(8,128)(2,1)}, u32[]{:S(2)}) copy-start(bf16[128,128]{1,0:T(8,128)(2,1)} %param.18) | copy-start | bytes 98308
  51.5 1.0 copy-start.2
  51.6 1.0 copy-start.4
  51.6 1.0 copy-start.9
  52.0 1.3 %copy-start.10 = (f32[128]{0:T(128)S(1)}, f32[128]{0:T(128)}, u32[]{:S(2)}) copy-start(f32[128]{0:T(128)} %param.21) | copy-start | bytes 1540
  52.2 2.0 %copy-start.7 = (bf16[128,4]{0,1:T(4,128)(2,1)S(1)}, bf16[128,4]{0,1:T(4,128)(2,1)}, u32[]{:S(2)}) copy-start(bf16[128,4]{0,1:T(4,128)(2,1)} %param.24) | copy-start | bytes 3076
  96.8 9.3 %all-to-all-start.1 = ((bf16[4,6,24,128]{3,2,1,0:T(8,128)(2,1)}), bf16[4,6,24,128]{3,2,1,0:T(8,128)(2,1)S(1)}, u32[]{:S(2)}, u32[]{:S(2)}) async-start(bf16[4,6,24,128]{3,2,1,0:T(8,128)(2,1)} %bitcast.7), calls=%async_computation.1 | async-start | bytes 294912 | tf_op jit(solution)/shard_map/all_to_all | solution.py:133
  100.9 5.2 %copy-start.3 = (bf16[128,384]{1,0:T(8,128)(2,1)S(1)}, bf16[128,384]{1,0:T(8,128)(2,1)}, u32[]{:S(2)}) copy-start(bf16[128,384]{1,0:T(8,128)(2,1)} %param.22) | copy-start | bytes 294916
  108.1 0.8 copy-start.12
  108.8 9.8 %copy-start.5 = (bf16[128,128]{1,0:T(8,128)(2,1)S(1)}, bf16[128,128]{1,0:T(8,128)(2,1)}, u32[]{:S(2)}) copy-start(bf16[128,128]{1,0:T(8,128)(2,1)} %param.25) | copy-start | bytes 98308
where the time goes:
time: 120 us
  blocking collectives  89.7 us (75%)
  starting transfers between devices  8.21 us (7%)
  matrix products  7.37 us (6%)
  other arithmetic  4.92 us (4%)
  waiting for transfers between devices  4.48 us (4%)
  local copies, waits for them, and re-layouts  4.43 us (4%)
    all_gather x1, blocking collectives, shards(): gathered = lax.all_gather(flat_bias, ('row', 'col'), axis=1, tiled=True)  41.3 us
    all_gather x1, blocking collectives, shards(): left_panel = lax.all_gather(left_factor, 'col', axis=1, tiled=True)  26.3 us
    all_gather x1, blocking collectives, shards(): right_stacked = lax.all_gather(right_factor, 'row', axis=0, tiled=True)  12.6 us
    all_to_all x1, blocking collectives, shards(): lax.all_to_all(attended_rows, 'col', split_axis=2, concat_axis=0, tiled=T...  9.46 us
    all_to_all x1, starting transfers between devices, shards(): lax.all_to_all(right_stacked, 'col', split_axis=0, concat_axis=1, tiled=T...  4.87 us
    all_to_all x1, waiting for transfers between devices, shards(): lax.all_to_all(grouped, 'col', split_axis=0, concat_axis=2, tiled=True)  4.48 us
    all_to_all x1, starting transfers between devices, shards(): lax.all_to_all(grouped, 'col', split_axis=0, concat_axis=2, tiled=True)  3.34 us
  transfers between devices with their start and end apart: 2, of which 1 were waited for; matrix products, arithmetic and copies ran while one was open for 3% of the time, Pallas kernels for 0%

commit v1 on v0

v1 whole, which is shorter than its diff:
```python
import functools
import math

import jax
import jax.numpy as jnp
from jax import lax
from jax.experimental import pallas as pl
from jax.experimental.pallas import tpu as pltpu
from jax.sharding import PartitionSpec as P

norm_epsilon = 1e-05
VMEM = pl.BlockSpec(memory_space=pltpu.VMEM)
PARAMS = pltpu.CompilerParams(vmem_limit_bytes=48 * 1024 * 1024)


def layer_norm(inputs, gain):
    average = jnp.mean(inputs, axis=-1, keepdims=True)
    centered = inputs - average
    variance = jnp.mean(centered * centered, axis=-1, keepdims=True)
    return centered * lax.rsqrt(variance + norm_epsilon) * gain


def dot(left, right):
    return jnp.dot(left, right, preferred_element_type=jnp.float32)


def pair_mask(row_mask, column_mask, rows, columns, row_start, column_start):
    along_rows = row_mask[pl.ds(row_start, rows)]
    along_columns = column_mask[pl.ds(pl.multiple_of(column_start, 8), columns), :]
    return (along_rows * along_columns[None]).reshape(rows * columns, -1)


def own_kernel(rows, columns, state, row_mask, column_mask, gain, w_in, w_gate, left, right, gate):
    channels = state.shape[1]
    row_start = lax.axis_index("row") * rows
    column_start = lax.axis_index("col") * columns
    normed = layer_norm(state[...].astype(jnp.float32), gain[...]).astype(jnp.bfloat16)
    mask = pair_mask(row_mask, column_mask, rows, columns, row_start, column_start)
    part = dot(normed, w_in[:, : 2 * channels])
    value = mask * jax.nn.sigmoid(part[:, :channels]) * part[:, channels:]
    left[...] = value.astype(jnp.bfloat16).astype(jnp.float32)
    part = dot(normed, w_in[:, 2 * channels :])
    value = mask * jax.nn.sigmoid(part[:, :channels]) * part[:, channels:]
    right[...] = value.astype(jnp.bfloat16).astype(jnp.float32)
    gate[...] = jax.nn.sigmoid(dot(normed, w_gate[...]))


def product_kernel(rows, columns, row_devices, column_devices, row_mask, column_mask, gain, w_in, left, right_own, *refs):
    states, refs = refs[: row_devices - 1], refs[row_devices - 1 :]
    outs, right = refs[:column_devices], refs[column_devices]
    channels = left.shape[1]
    size = rows * columns
    split = rows // columns
    row_index, column_index = lax.axis_index("row"), lax.axis_index("col")
    right[pl.ds(0, size), :] = right_own[...]
    for step, state in enumerate(states, 1):
        normed = layer_norm(state[...].astype(jnp.float32), gain[...]).astype(jnp.bfloat16)
        row_start = lax.bitwise_xor(row_index, step) * rows
        mask = pair_mask(row_mask, column_mask, rows, columns, row_start, column_index * columns)
        part = dot(normed, w_in[:, 2 * channels :])
        value = mask * jax.nn.sigmoid(part[:, :channels]) * part[:, channels:]
        right[pl.ds(step * size, size), :] = value.astype(jnp.bfloat16).astype(jnp.float32)
    group = 4 if rows % 4 == 0 else 2
    for step, out in enumerate(outs):
        target = lax.bitwise_xor(column_index, step)
        held = lax.bitwise_xor(row_index, target // split)
        base = held * size + (target % split) * columns * columns

        def block(at, carry, out=out, base=base):
            sums = [jnp.zeros((columns, channels), jnp.float32) for _ in range(group)]
            for k in range(columns):
                factor = right[pl.ds(base + k, columns, stride=columns), :]
                for g in range(group):
                    row = left[pl.ds((at * group + g) * columns + k, 1), :]
                    sums[g] = sums[g] + row * factor
            width = group * columns
            start = pl.multiple_of(at * width, 16)
            out[pl.ds(start, width), :] = jnp.concatenate(sums, 0).astype(jnp.bfloat16)
            return carry

        lax.fori_loop(0, rows // group, block, 0)


def middle_kernel(rows, columns, split, state, gate, product_gain, w_out, attend_gain, w_bias, *refs):
    parts, (middle, attend, bias) = refs[:-3], refs[-3:]
    product = parts[0][...].astype(jnp.float32)
    for part in parts[1:]:
        product = product + part[...].astype(jnp.float32)
    normed = layer_norm(product, product_gain[...]).astype(jnp.bfloat16)
    value = state[...].astype(jnp.float32) + gate[...] * dot(normed, w_out[...])
    rounded = value.astype(jnp.bfloat16)
    middle[...] = rounded
    normed = layer_norm(rounded.astype(jnp.float32), attend_gain[...]).astype(jnp.bfloat16)
    attend[...] = normed
    spread = dot(normed, w_bias[...]).reshape(rows, columns, -1)
    lane = lax.broadcasted_iota(jnp.int32, spread.shape[1:], 1) % columns
    for part in range(split):
        total = jnp.zeros(spread.shape[1:], jnp.float32)
        for j in range(columns):
            total = jnp.where(lane == j, spread[part * columns + j], total)
        bias[part] = total.astype(jnp.bfloat16)


def attend_kernel(rows, columns, heads, split, column_devices, middle, allowed, w_query, w_key_value, w_gate, w_out, *refs):
    tiles, refs = refs[:column_devices], refs[column_devices:]
    biases, refs = refs[:column_devices], refs[column_devices:]
    out, keys, values, queries, gates, bias, gated = refs
    channels = middle.shape[1]
    width = channels // heads
    tokens = columns * column_devices
    row_index, column_index = lax.axis_index("row"), lax.axis_index("col")
    for step, tile in enumerate(tiles):
        part = dot(tile[...], w_key_value[...]).reshape(rows, columns, 2 * channels)
        keys[:, pl.ds(step * columns, columns), :] = part[..., :channels]
        values[:, pl.ds(step * columns, columns), :] = part[..., channels:]
    own = tiles[0][...]
    queries[...] = dot(own, w_query[...])
    gates[...] = jax.nn.sigmoid(dot(own, w_gate[...]))
    for step, piece in enumerate(biases):
        place = lax.bitwise_xor(row_index * split + column_index % split, step)
        place = lax.bitwise_xor(place, column_index)
        bias[pl.ds(pl.multiple_of(place * columns, 8), columns), :] = piece[...].astype(jnp.float32)
    for step in range(column_devices):
        start = pl.multiple_of(lax.bitwise_xor(column_index, step) * columns, 8)
        here = pl.ds(step * columns, columns)
        bias[here, :] = jnp.where(allowed[pl.ds(start, columns), :] > 0, bias[here, :], -1e30)
    added = bias[...].T
    head_of_lane = lax.broadcasted_iota(jnp.int32, (1, channels), 1) // width
    picks = [head_of_lane == h for h in range(heads)]
    scale = 1.0 / math.sqrt(width)
    ones = jnp.ones((tokens, channels), jnp.bfloat16)

    def row(at, carry):
        start = pl.multiple_of(at * columns, 8)
        query = queries[pl.ds(start, columns), :]
        stacked = jnp.concatenate([jnp.where(pick, query, 0.0) for pick in picks], 0).astype(jnp.bfloat16)
        key = keys[at].astype(jnp.bfloat16)
        scores = lax.dot_general(stacked, key, (((1,), (1,)), ((), ())), preferred_element_type=jnp.float32)
        scores = scores * scale + added
        weights = jnp.exp(scores - jnp.max(scores, axis=-1, keepdims=True)).astype(jnp.bfloat16)
        value = jnp.concatenate([values[at].astype(jnp.bfloat16), ones], 1)
        mixed = dot(weights, value)
        mixed = mixed[:, :channels] / mixed[:, channels:]
        total = jnp.zeros((columns, channels), jnp.float32)
        for h, pick in enumerate(picks):
            total = jnp.where(pick, mixed[h * columns : (h + 1) * columns], total)
        gated[pl.ds(start, columns), :] = total * gates[pl.ds(start, columns), :]
        return carry

    lax.fori_loop(0, rows, row, 0, unroll=4)
    update = dot(gated[...].astype(jnp.bfloat16), w_out[...])
    out[...] = (middle[...].astype(jnp.float32) + update).astype(jnp.bfloat16)


def call(kernel, outs, args, scratch=()):
    return pl.pallas_call(
        kernel,
        out_shape=outs,
        in_specs=[VMEM] * len(args),
        out_specs=jax.tree.map(lambda _: VMEM, outs),
        scratch_shapes=scratch,
        compiler_params=PARAMS,
    )(*args)


def exchange(value, axis, step):
    size = lax.axis_size(axis)
    return lax.ppermute(value, axis, [(at, at ^ step) for at in range(size)])


def shards(
    pair_state,
    token_mask,
    block_pattern,
    triangle_norm,
    triangle_input,
    triangle_gate,
    product_norm,
    triangle_output,
    attend_norm,
    attend_inputs,
    attend_gate,
    attend_bias,
    attend_output,
):
    rows, columns, channels = pair_state.shape
    row_devices, column_devices = lax.axis_size("row"), lax.axis_size("col")
    heads = attend_bias.shape[1]
    split = rows // columns
    tokens = columns * column_devices
    size = rows * columns
    row_index, column_index = lax.axis_index("row"), lax.axis_index("col")
    tile = jax.ShapeDtypeStruct((size, channels), jnp.bfloat16)
    wide = jax.ShapeDtypeStruct((size, channels), jnp.float32)
    state = pair_state.reshape(size, channels)
    others = [exchange(state, "row", step) for step in range(1, row_devices)]

    valid = token_mask.astype(jnp.float32)
    row_mask = jnp.broadcast_to(valid[:, None, None], (tokens, 1, channels))
    column_mask = jnp.broadcast_to(valid[:, None], (tokens, channels))
    blocks = block_pattern.shape[0]
    block_width = tokens // blocks
    pattern = jnp.repeat(jnp.repeat(block_pattern, block_width, axis=0), block_width, axis=1)
    pattern = lax.dynamic_slice_in_dim(pattern, column_index * columns, columns, axis=0)
    allowed = ((pattern > 0) & (token_mask[None, :] > 0)).astype(jnp.float32).T
    allowed = jnp.tile(allowed, (1, heads))
    w_bias = jnp.repeat(attend_bias, columns, axis=1)

    left, right, gate = call(
        functools.partial(own_kernel, rows, columns),
        [wide, wide, wide],
        [state, row_mask, column_mask, triangle_norm[None], triangle_input, triangle_gate],
    )
    parts = call(
        functools.partial(product_kernel, rows, columns, row_devices, column_devices),
        [tile] * column_devices,
        [row_mask, column_mask, triangle_norm[None], triangle_input, left, right] + others,
        [pltpu.VMEM((row_devices * size, channels), jnp.float32)],
    )
    parts = [parts[0]] + [exchange(parts[step], "col", step) for step in range(1, column_devices)]
    middle, attend, bias = call(
        functools.partial(middle_kernel, rows, columns, split),
        [tile, tile, jax.ShapeDtypeStruct((split, columns, heads * columns), jnp.bfloat16)],
        [state, gate, product_norm[None], triangle_output, attend_norm[None], w_bias] + parts,
    )
    tiles = [attend] + [exchange(attend, "col", step) for step in range(1, column_devices)]
    biases = []
    for step in range(column_devices):
        piece = bias[0]
        if split > 1:
            piece = lax.dynamic_index_in_dim(bias, lax.bitwise_xor(column_index, step) % split, 0, False)
        pairs = []
        for a in range(row_devices):
            for b in range(column_devices):
                turn = b ^ step
                pairs.append((a * column_devices + b, (turn // split) * column_devices + split * a + turn % split))
        biases.append(lax.ppermute(piece, ("row", "col"), pairs))
    stack = pltpu.VMEM((rows, tokens, channels), jnp.float32)
    flat = pltpu.VMEM((size, channels), jnp.float32)
    result = call(
        functools.partial(attend_kernel, rows, columns, heads, split, column_devices),
        tile,
        [middle, allowed, attend_inputs[:, :channels], attend_inputs[:, channels:], attend_gate, attend_output]
        + tiles
        + biases,
        [stack, stack, flat, flat, pltpu.VMEM((tokens, heads * columns), jnp.float32), flat],
    )
    return result.reshape(rows, columns, channels)


def solution(mesh):
    return jax.shard_map(
        shards,
        mesh=mesh,
        in_specs=(
            P(("crop", "row"), "col", None),
            P("crop"),
            P("crop", None),
            P(),
            P(),
            P(),
            P(),
            P(),
            P(),
            P(),
            P(),
            P(),
            P(),
        ),
        out_specs=P(("crop", "row"), "col", None),
        check_vma=False,
    )
```

time: 120 us -> 58.2 us (0.49)
  blocking collectives: 89.7 us -> 0 us
  waiting for transfers between devices: 4.48 us -> 20.6 us
  Pallas kernels: 0 us -> 12.8 us
  starting transfers between devices: 8.21 us -> 20 us
  matrix products: 7.37 us -> 0 us
  other arithmetic: 4.92 us -> 0.1 us
    all_gather x3 -> x0, blocking collectives: 80.2 us -> none  [the longest x1 41.3 us: shards(): gathered = lax.all_gather(flat_bias, ('row', 'col'), axis=1, tiled=True)]
    ppermute x0 -> x13, waiting for transfers between devices: none -> 20.6 us  [the longest x9 16.3 us: exchange(): return lax.ppermute(value, axis, [(at, at ^ step) for at in range(size)])]
    ppermute x0 -> x13, starting transfers between devices: none -> 20 us  [the longest x9 13.3 us: exchange(): return lax.ppermute(value, axis, [(at, at ^ step) for at in range(size)])]
    pallas_call x0 -> x4, Pallas kernels: none -> 12.8 us  [call(): pl.pallas_call(kernel, out_shape=outs, in_specs=[VMEM] * len(args), out_s...]
    all_to_all x1 -> x0, blocking collectives: 9.46 us -> none  [shards(): lax.all_to_all(attended_rows, 'col', split_axis=2, concat_axis=0, tiled=T...]
    all_to_all x2 -> x0, starting transfers between devices: 8.21 us -> none  [the longest x1 4.87 us: shards(): lax.all_to_all(right_stacked, 'col', split_axis=0, concat_axis=1, tiled=T...]
    dot_general x10 -> x0, matrix products: 6.74 us -> none  [the longest x1 1.3 us: shards(): jnp.dot(normed, triangle_input, preferred_element_type=jnp.float32)]
    all_to_all x2 -> x0, waiting for transfers between devices: 4.48 us -> none  [the longest x1 4.48 us: shards(): lax.all_to_all(grouped, 'col', split_axis=0, concat_axis=2, tiled=True)]
  transfers between devices with their start and end apart: 2 -> 13, of which waited for: 1 -> 5; matrix products, arithmetic and copies ran while one was open for 3% -> 1% of each run, Pallas kernels for 0% -> 1%
where the time goes in v1:
time: 58.2 us; the launch traced here: 57.6 us
  waiting for transfers between devices  20.6 us (35%)
  starting transfers between devices  20 us (34%)
  Pallas kernels  12.8 us (22%)
  local copies, waits for them, and re-layouts  3.96 us (7%)
    ppermute x9, waiting for transfers between devices, exchange(): return lax.ppermute(value, axis, [(at, at ^ step) for at in range(size)])  16.3 us
    ppermute x9, starting transfers between devices, exchange(): return lax.ppermute(value, axis, [(at, at ^ step) for at in range(size)])  13.3 us
    pallas_call x4, Pallas kernels, call(): pl.pallas_call(kernel, out_shape=outs, in_specs=[VMEM] * len(args), out_s...  12.8 us
    ppermute x4, starting transfers between devices, shards(): biases.append(lax.ppermute(piece, ('row', 'col'), pairs))  6.7 us
    ppermute x4, waiting for transfers between devices, shards(): biases.append(lax.ppermute(piece, ('row', 'col'), pairs))  4.37 us
    unnamed x31, local copies, waits for them, and re-layouts  3.29 us
  transfers between devices with their start and end apart: 13, of which 5 were waited for; matrix products, arithmetic and copies ran while one was open for 1% of the time, Pallas kernels for 1%

profile of v1, /device:TPU:0, one launch (start us, length us, event | category | flops | bytes accessed | tf_op | source)
XLA Modules:
  0.0 57.6 jit_solution(4473752247756800981)
XLA Ops:
  0.0 2.9 %collective-permute-start = (bf16[576,128]{1,0:T(8,128)(2,1)}, bf16[576,128]{1,0:T(8,128)(2,1)S(1)}, u32[]{:S(2)}, u32[]{:S(2)}) collective-permute-start(bf16[576,128]{1,0:T(8,128)(2,1)} %bitcast.13), channel_id=1, source_target_pairs={{0,4},{4,0},{8,12},{12,8},{1,5},{5,1},{9,13},{13,9},{2,6},{6,2},{1... | collective-permute-start | bytes 442376 | tf_op jit(solution)/shard_map/ppermute | solution.py:168
  2.9 1.5 %collective-permute-start.1 = (bf16[576,128]{1,0:T(8,128)(2,1)}, bf16[576,128]{1,0:T(8,128)(2,1)S(1)}, u32[]{:S(2)}, u32[]{:S(2)}) collective-permute-start(bf16[576,128]{1,0:T(8,128)(2,1)} %bitcast.14), channel_id=1, source_target_pairs={{0,8},{4,12},{8,0},{12,4},{1,9},{5,13},{9,1},{13,5},{2,10},{6,14},... | collective-permute-start | bytes 442376 | tf_op jit(solution)/shard_map/ppermute | solution.py:168
  4.7 0.7 %copy-done.4 = bf16[128,128]{1,0:T(8,128)(2,1)S(1)} copy-done((bf16[128,128]{1,0:T(8,128)(2,1)S(1)}, bf16[128,128]{1,0:T(8,128)(2,1)}, u32[]{:S(2)}) %copy-start.4) | copy-done | bytes 32792
  5.4 0.9 %copy-done = bf16[24,24,128]{2,1,0:T(8,128)(2,1)S(1)} copy-done((bf16[24,24,128]{2,1,0:T(8,128)(2,1)S(1)}, bf16[24,24,128]{2,1,0:T(8,128)(2,1)}, u32[]{:S(2)}) %copy-start) | copy-done | bytes 147480
  6.3 0.9 %copy-done.2 = bf16[128,512]{1,0:T(8,128)(2,1)S(1)} copy-done((bf16[128,512]{1,0:T(8,128)(2,1)S(1)}, bf16[128,512]{1,0:T(8,128)(2,1)}, u32[]{:S(2)}) %copy-start.2) | copy-done | bytes 131096
  7.2 0.6 %shard_map.127 = (f32[576,128]{1,0:T(8,128)S(1)}, f32[576,128]{1,0:T(8,128)S(1)}, f32[576,128]{1,0:T(8,128)S(1)}) custom-call(bf16[576,128]{1,0:T(8,128)(2,1)S(1)} %bitcast.16, f32[96,1,128]{2,1,0:T(1,128)S(1)} %broadcast_in_dim.32.row_mask, f32[96,128]{1,0:T(8,128)S(1)} %broadcast_in_dim.33.column_mask, f32[1,128]{1,0:T(1,128)S(1)} %bitcast.18, ...), custom_call_target="tpu_custom_call" | custom-call | tf_op jit(solution)/shard_map/pallas_call | solution.py:156
  7.9 3.8 %collective-permute-done.1.refs_1_ = bf16[576,128]{1,0:T(8,128)(2,1)S(1)} collective-permute-done((bf16[576,128]{1,0:T(8,128)(2,1)}, bf16[576,128]{1,0:T(8,128)(2,1)S(1)}, u32[]{:S(2)}, u32[]{:S(2)}) %collective-permute-start.1) | collective-permute-done | bytes 147488 | tf_op jit(solution)/shard_map/ppermute | solution.py:168
  11.6 3.7 %shard_map.128 = (bf16[576,128]{1,0:T(8,128)(2,1)S(1)}, bf16[576,128]{1,0:T(8,128)(2,1)S(1)}, bf16[576,128]{1,0:T(8,128)(2,1)S(1)}, bf16[576,128]{1,0:T(8,128)(2,1)S(1)}) custom-call(f32[96,1,128]{2,1,0:T(1,128)S(1)} %broadcast_in_dim.32.row_mask, f32[96,128]{1,0:T(8,128)S(1)} %broadcast_in_dim.33.column_mask, f32[1,128]{1,0:T(1,128)S(1)} %bitcast.19, ...), custom_call_target="tpu_custom_call" | custom-call | tf_op jit(solution)/shard_map/pallas_call | solution.py:156
  15.3 1.6 %collective-permute-start.3 = (bf16[576,128]{1,0:T(8,128)(2,1)S(1)}, bf16[576,128]{1,0:T(8,128)(2,1)S(1)}, u32[]{:S(2)}, u32[]{:S(2)}) collective-permute-start(bf16[576,128]{1,0:T(8,128)(2,1)S(1)} %get-tuple-element.19), channel_id=1, source_target_pairs={{0,1},{1,0},{2,3},{3,2},{4,5},{5,4},{6,7},{7,6},{8,9},{9,8},{10,11... | collective-permute-start | bytes 442376 | tf_op jit(solution)/shard_map/ppermute | solution.py:168
  17.0 2.6 %collective-permute-start.4 = (bf16[576,128]{1,0:T(8,128)(2,1)S(1)}, bf16[576,128]{1,0:T(8,128)(2,1)S(1)}, u32[]{:S(2)}, u32[]{:S(2)}) collective-permute-start(bf16[576,128]{1,0:T(8,128)(2,1)S(1)} %get-tuple-element.20), channel_id=1, source_target_pairs={{0,2},{1,3},{2,0},{3,1},{4,6},{5,7},{6,4},{7,5},{8,10},{9,11},{10,... | collective-permute-start | bytes 442376 | tf_op jit(solution)/shard_map/ppermute | solution.py:168
  19.9 2.4 %collective-permute-done.3.refs_1_ = bf16[576,128]{1,0:T(8,128)(2,1)S(1)} collective-permute-done((bf16[576,128]{1,0:T(8,128)(2,1)S(1)}, bf16[576,128]{1,0:T(8,128)(2,1)S(1)}, u32[]{:S(2)}, u32[]{:S(2)}) %collective-permute-start.3) | collective-permute-done | bytes 147488 | tf_op jit(solution)/shard_map/ppermute | solution.py:168
  22.3 7.9 %collective-permute-done.4.refs_2_ = bf16[576,128]{1,0:T(8,128)(2,1)S(1)} collective-permute-done((bf16[576,128]{1,0:T(8,128)(2,1)S(1)}, bf16[576,128]{1,0:T(8,128)(2,1)S(1)}, u32[]{:S(2)}, u32[]{:S(2)}) %collective-permute-start.4) | collective-permute-done | bytes 147488 | tf_op jit(solution)/shard_map/ppermute | solution.py:168
  30.2 0.6 %copy-done.9 = f32[128]{0:T(128)S(1)} copy-done((f32[128]{0:T(128)S(1)}, f32[128]{0:T(128)}, u32[]{:S(2)}) %copy-start.9) | copy-done | bytes 536
  30.9 0.7 %shard_map.129 = (bf16[576,128]{1,0:T(8,128)(2,1)S(1)}, bf16[576,128]{1,0:T(8,128)(2,1)S(1)}, bf16[1,24,96]{2,1,0:T(8,128)(2,1)S(1)}) custom-call(bf16[576,128]{1,0:T(8,128)(2,1)S(1)} %bitcast.17, f32[576,128]{1,0:T(8,128)S(1)} %get-tuple-element.15.gate, f32[1,128]{1,0:T(1,128)S(1)} %bitcast.20, bf16[128,128]{1,0:T(8,128)(2,1)S(1)} %copy-done.5, ...), custom_call_target="tpu_custom_call" | custom-call | tf_op jit(solution)/shard_map/pallas_call | solution.py:156
  31.6 1.3 %collective-permute-start.10 = (bf16[24,96]{1,0:T(8,128)(2,1)S(1)}, bf16[24,96]{1,0:T(8,128)(2,1)S(1)}, u32[]{:S(2)}, u32[]{:S(2)}) collective-permute-start(bf16[24,96]{1,0:T(8,128)(2,1)S(1)} %bitcast.22), channel_id=1, source_target_pairs={{0,4},{1,0},{2,12},{3,8},{4,5},{5,1},{6,13},{7,9},{8,6},{9,2},{10,... | collective-permute-start | bytes 13832 | tf_op jit(solution)/shard_map/ppermute | solution.py:237
  32.9 4.0 %collective-permute-start.11 = (bf16[24,96]{1,0:T(8,128)(2,1)S(1)}, bf16[24,96]{1,0:T(8,128)(2,1)S(1)}, u32[]{:S(2)}, u32[]{:S(2)}) collective-permute-start(bf16[24,96]{1,0:T(8,128)(2,1)S(1)} %bitcast.23), channel_id=1, source_target_pairs={{0,8},{1,12},{2,0},{3,4},{4,9},{5,13},{6,1},{7,5},{8,10},{9,14},{1... | collective-permute-start | bytes 13832 | tf_op jit(solution)/shard_map/ppermute | solution.py:237
  37.3 0.8 %collective-permute-start.6 = (bf16[576,128]{1,0:T(8,128)(2,1)S(1)}, bf16[576,128]{1,0:T(8,128)(2,1)S(1)}, u32[]{:S(2)}, u32[]{:S(2)}) collective-permute-start(bf16[576,128]{1,0:T(8,128)(2,1)S(1)} %get-tuple-element.23.refs_0_), channel_id=1, source_target_pairs={{0,1},{1,0},{2,3},{3,2},{4,5},{5,4},{6,7},{7,6},{8,9},{9,8},{10,11... | collective-permute-start | bytes 442376 | tf_op jit(solution)/shard_map/ppermute | solution.py:168
  38.0 1.1 %collective-permute-start.7 = (bf16[576,128]{1,0:T(8,128)(2,1)S(1)}, bf16[576,128]{1,0:T(8,128)(2,1)S(1)}, u32[]{:S(2)}, u32[]{:S(2)}) collective-permute-start(bf16[576,128]{1,0:T(8,128)(2,1)S(1)} %get-tuple-element.23.refs_0_), channel_id=1, source_target_pairs={{0,2},{1,3},{2,0},{3,1},{4,6},{5,7},{6,4},{7,5},{8,10},{9,11},{10,... | collective-permute-start | bytes 442376 | tf_op jit(solution)/shard_map/ppermute | solution.py:168
  39.2 2.5 %collective-permute-start.8 = (bf16[576,128]{1,0:T(8,128)(2,1)S(1)}, bf16[576,128]{1,0:T(8,128)(2,1)S(1)}, u32[]{:S(2)}, u32[]{:S(2)}) collective-permute-start(bf16[576,128]{1,0:T(8,128)(2,1)S(1)} %get-tuple-element.23.refs_0_), channel_id=1, source_target_pairs={{0,3},{1,2},{2,1},{3,0},{4,7},{5,6},{6,5},{7,4},{8,11},{9,10},{10,... | collective-permute-start | bytes 442376 | tf_op jit(solution)/shard_map/ppermute | solution.py:168
  41.6 0.7 %collective-permute-start.12 = (bf16[24,96]{1,0:T(8,128)(2,1)S(1)}, bf16[24,96]{1,0:T(8,128)(2,1)S(1)}, u32[]{:S(2)}, u32[]{:S(2)}) collective-permute-start(bf16[24,96]{1,0:T(8,128)(2,1)S(1)} %bitcast.24), channel_id=1, source_target_pairs={{0,12},{1,8},{2,4},{3,0},{4,13},{5,9},{6,5},{7,1},{8,14},{9,10},{1... | collective-permute-start | bytes 13832 | tf_op jit(solution)/shard_map/ppermute | solution.py:237
  42.3 0.7 %collective-permute-start.9 = (bf16[24,96]{1,0:T(8,128)(2,1)S(1)}, bf16[24,96]{1,0:T(8,128)(2,1)S(1)}, u32[]{:S(2)}, u32[]{:S(2)}) collective-permute-start(bf16[24,96]{1,0:T(8,128)(2,1)S(1)} %bitcast.25), channel_id=1, source_target_pairs={{0,0},{1,4},{2,8},{3,12},{4,1},{5,5},{6,9},{7,13},{8,2},{9,6},{10,... | collective-permute-start | bytes 13832 | tf_op jit(solution)/shard_map/ppermute | solution.py:237
  43.3 4.4 %collective-permute-done.12.refs_7_ = bf16[24,96]{1,0:T(8,128)(2,1)S(1)} collective-permute-done((bf16[24,96]{1,0:T(8,128)(2,1)S(1)}, bf16[24,96]{1,0:T(8,128)(2,1)S(1)}, u32[]{:S(2)}, u32[]{:S(2)}) %collective-permute-start.12) | collective-permute-done | bytes 4640 | tf_op jit(solution)/shard_map/ppermute | solution.py:237
  47.7 2.2 %collective-permute-done.7.refs_2_ = bf16[576,128]{1,0:T(8,128)(2,1)S(1)} collective-permute-done((bf16[576,128]{1,0:T(8,128)(2,1)S(1)}, bf16[576,128]{1,0:T(8,128)(2,1)S(1)}, u32[]{:S(2)}, u32[]{:S(2)}) %collective-permute-start.7) | collective-permute-done | bytes 147488 | tf_op jit(solution)/shard_map/ppermute | solution.py:168
  49.9 7.7 %shard_map.130 = bf16[576,128]{1,0:T(8,128)(2,1)} custom-call(bf16[576,128]{1,0:T(8,128)(2,1)S(1)} %get-tuple-element.22.middle, f32[96,96]{1,0:T(8,128)S(1)} %copy.21.allowed, bf16[128,128]{1,0:T(8,128)(2,1)S(1)} %slice.6.w_query, bf16[128,256]{1,0:T(8,128)(2,1)S(1)} %slice.7.w_key_value, bf16[128,128]{1,0:T(8,128)(2,1)S(1)} %copy-done.6, ...), custom_call_target="tpu_custom_call" | custom-call | tf_op jit(solution)/shard_map/pallas_call | solution.py:156
  (52 shorter events, 1.2 us)
Async XLA Ops:
  0.0 4.5 %copy-start.14 = (s32[96]{0:T(128)S(1)}, s32[96]{0:T(128)}, u32[]{:S(2)}) copy-start(s32[96]{0:T(128)} %param.14) | copy-start | bytes 1156
  0.0 7.8 %collective-permute-start = (bf16[576,128]{1,0:T(8,128)(2,1)}, bf16[576,128]{1,0:T(8,128)(2,1)S(1)}, u32[]{:S(2)}, u32[]{:S(2)}) collective-permute-start(bf16[576,128]{1,0:T(8,128)(2,1)} %bitcast.13), channel_id=1, source_target_pairs={{0,4},{4,0},{8,12},{12,8},{1,5},{5,1},{9,13},{13,9},{2,6},{6,2},{1... | collective-permute-start | bytes 442376 | tf_op jit(solution)/shard_map/ppermute | solution.py:168
  2.9 8.7 %collective-permute-start.1 = (bf16[576,128]{1,0:T(8,128)(2,1)}, bf16[576,128]{1,0:T(8,128)(2,1)S(1)}, u32[]{:S(2)}, u32[]{:S(2)}) collective-permute-start(bf16[576,128]{1,0:T(8,128)(2,1)} %bitcast.14), channel_id=1, source_target_pairs={{0,8},{4,12},{8,0},{12,4},{1,9},{5,13},{9,1},{13,5},{2,10},{6,14},... | collective-permute-start | bytes 442376 | tf_op jit(solution)/shard_map/ppermute | solution.py:168
  4.5 7.2 %collective-permute-start.2 = (bf16[576,128]{1,0:T(8,128)(2,1)}, bf16[576,128]{1,0:T(8,128)(2,1)S(1)}, u32[]{:S(2)}, u32[]{:S(2)}) collective-permute-start(bf16[576,128]{1,0:T(8,128)(2,1)} %bitcast.15), channel_id=1, source_target_pairs={{0,12},{4,8},{8,4},{12,0},{1,13},{5,9},{9,5},{13,1},{2,14},{6,10},... | collective-permute-start | bytes 442376 | tf_op jit(solution)/shard_map/ppermute | solution.py:168
  5.4 0.9 %copy-start = (bf16[24,24,128]{2,1,0:T(8,128)(2,1)S(1)}, bf16[24,24,128]{2,1,0:T(8,128)(2,1)}, u32[]{:S(2)}) copy-start(bf16[24,24,128]{2,1,0:T(8,128)(2,1)} %param.13) | copy-start | bytes 442372
  6.3 0.9 %copy-start.2 = (bf16[128,512]{1,0:T(8,128)(2,1)S(1)}, bf16[128,512]{1,0:T(8,128)(2,1)}, u32[]{:S(2)}) copy-start(bf16[128,512]{1,0:T(8,128)(2,1)} %w_in.3) | copy-start | bytes 393220
  7.2 4.4 %copy-start.3 = (bf16[128,512]{1,0:T(8,128)(2,1)S(1)}, bf16[128,512]{1,0:T(8,128)(2,1)}, u32[]{:S(2)}) copy-start(bf16[128,512]{1,0:T(8,128)(2,1)} %w_in.3) | copy-start | bytes 393220
  11.6 18.6 %copy-start.1 = (bf16[24,24,128]{2,1,0:T(8,128)(2,1)S(1)}, bf16[24,24,128]{2,1,0:T(8,128)(2,1)}, u32[]{:S(2)}) copy-start(bf16[24,24,128]{2,1,0:T(8,128)(2,1)} %param.13) | copy-start | bytes 442372
  15.3 7.0 %collective-permute-start.3 = (bf16[576,128]{1,0:T(8,128)(2,1)S(1)}, bf16[576,128]{1,0:T(8,128)(2,1)S(1)}, u32[]{:S(2)}, u32[]{:S(2)}) collective-permute-start(bf16[576,128]{1,0:T(8,128)(2,1)S(1)} %get-tuple-element.19), channel_id=1, source_target_pairs={{0,1},{1,0},{2,3},{3,2},{4,5},{5,4},{6,7},{7,6},{8,9},{9,8},{10,11... | collective-permute-start | bytes 442376 | tf_op jit(solution)/shard_map/ppermute | solution.py:168
  17.0 2.8 %copy-start.13 = (bf16[128,4]{0,1:T(4,128)(2,1)S(1)}, bf16[128,4]{0,1:T(4,128)(2,1)}, u32[]{:S(2)}) copy-start(bf16[128,4]{0,1:T(4,128)(2,1)} %param.24) | copy-start | bytes 3076
  17.0 13.2 %collective-permute-start.4 = (bf16[576,128]{1,0:T(8,128)(2,1)S(1)}, bf16[576,128]{1,0:T(8,128)(2,1)S(1)}, u32[]{:S(2)}, u32[]{:S(2)}) collective-permute-start(bf16[576,128]{1,0:T(8,128)(2,1)S(1)} %get-tuple-element.20), channel_id=1, source_target_pairs={{0,2},{1,3},{2,0},{3,1},{4,6},{5,7},{6,4},{7,5},{8,10},{9,11},{10,... | collective-permute-start | bytes 442376 | tf_op jit(solution)/shard_map/ppermute | solution.py:168
  19.6 10.6 %collective-permute-start.5 = (bf16[576,128]{1,0:T(8,128)(2,1)S(1)}, bf16[576,128]{1,0:T(8,128)(2,1)S(1)}, u32[]{:S(2)}, u32[]{:S(2)}) collective-permute-start(bf16[576,128]{1,0:T(8,128)(2,1)S(1)} %get-tuple-element.21), channel_id=1, source_target_pairs={{0,3},{1,2},{2,1},{3,0},{4,7},{5,6},{6,5},{7,4},{8,11},{9,10},{10,... | collective-permute-start | bytes 442376 | tf_op jit(solution)/shard_map/ppermute | solution.py:168
  19.8 10.4 %copy-start.5 = (bf16[128,128]{1,0:T(8,128)(2,1)S(1)}, bf16[128,128]{1,0:T(8,128)(2,1)}, u32[]{:S(2)}) copy-start(bf16[128,128]{1,0:T(8,128)(2,1)} %w_out.2) | copy-start | bytes 98308
  30.9 6.1 %copy-start.12 = (s32[4,4]{1,0:T(4,128)S(1)}, s32[4,4]{1,0:T(4,128)}, u32[]{:S(2)}) copy-start(s32[4,4]{1,0:T(4,128)} %param.15) | copy-start | bytes 196
  31.6 11.5 %copy-start.11 = (bf16[128,384]{1,0:T(8,128)(2,1)S(1)}, bf16[128,384]{1,0:T(8,128)(2,1)}, u32[]{:S(2)}) copy-start(bf16[128,384]{1,0:T(8,128)(2,1)} %param.22) | copy-start | bytes 294916
  31.6 10.0 %collective-permute-start.10 = (bf16[24,96]{1,0:T(8,128)(2,1)S(1)}, bf16[24,96]{1,0:T(8,128)(2,1)S(1)}, u32[]{:S(2)}, u32[]{:S(2)}) collective-permute-start(bf16[24,96]{1,0:T(8,128)(2,1)S(1)} %bitcast.22), channel_id=1, source_target_pairs={{0,4},{1,0},{2,12},{3,8},{4,5},{5,1},{6,13},{7,9},{8,6},{9,2},{10,... | collective-permute-start | bytes 13832 | tf_op jit(solution)/shard_map/ppermute | solution.py:237
  32.9 9.4 %collective-permute-start.11 = (bf16[24,96]{1,0:T(8,128)(2,1)S(1)}, bf16[24,96]{1,0:T(8,128)(2,1)S(1)}, u32[]{:S(2)}, u32[]{:S(2)}) collective-permute-start(bf16[24,96]{1,0:T(8,128)(2,1)S(1)} %bitcast.23), channel_id=1, source_target_pairs={{0,8},{1,12},{2,0},{3,4},{4,9},{5,13},{6,1},{7,5},{8,10},{9,14},{1... | collective-permute-start | bytes 13832 | tf_op jit(solution)/shard_map/ppermute | solution.py:237
  37.3 10.4 %collective-permute-start.6 = (bf16[576,128]{1,0:T(8,128)(2,1)S(1)}, bf16[576,128]{1,0:T(8,128)(2,1)S(1)}, u32[]{:S(2)}, u32[]{:S(2)}) collective-permute-start(bf16[576,128]{1,0:T(8,128)(2,1)S(1)} %get-tuple-element.23.refs_0_), channel_id=1, source_target_pairs={{0,1},{1,0},{2,3},{3,2},{4,5},{5,4},{6,7},{7,6},{8,9},{9,8},{10,11... | collective-permute-start | bytes 442376 | tf_op jit(solution)/shard_map/ppermute | solution.py:168
  38.0 11.9 %collective-permute-start.7 = (bf16[576,128]{1,0:T(8,128)(2,1)S(1)}, bf16[576,128]{1,0:T(8,128)(2,1)S(1)}, u32[]{:S(2)}, u32[]{:S(2)}) collective-permute-start(bf16[576,128]{1,0:T(8,128)(2,1)S(1)} %get-tuple-element.23.refs_0_), channel_id=1, source_target_pairs={{0,2},{1,3},{2,0},{3,1},{4,6},{5,7},{6,4},{7,5},{8,10},{9,11},{10,... | collective-permute-start | bytes 442376 | tf_op jit(solution)/shard_map/ppermute | solution.py:168
  39.2 10.7 %collective-permute-start.8 = (bf16[576,128]{1,0:T(8,128)(2,1)S(1)}, bf16[576,128]{1,0:T(8,128)(2,1)S(1)}, u32[]{:S(2)}, u32[]{:S(2)}) collective-permute-start(bf16[576,128]{1,0:T(8,128)(2,1)S(1)} %get-tuple-element.23.refs_0_), channel_id=1, source_target_pairs={{0,3},{1,2},{2,1},{3,0},{4,7},{5,6},{6,5},{7,4},{8,11},{9,10},{10,... | collective-permute-start | bytes 442376 | tf_op jit(solution)/shard_map/ppermute | solution.py:168
  41.6 6.0 %collective-permute-start.12 = (bf16[24,96]{1,0:T(8,128)(2,1)S(1)}, bf16[24,96]{1,0:T(8,128)(2,1)S(1)}, u32[]{:S(2)}, u32[]{:S(2)}) collective-permute-start(bf16[24,96]{1,0:T(8,128)(2,1)S(1)} %bitcast.24), channel_id=1, source_target_pairs={{0,12},{1,8},{2,4},{3,0},{4,13},{5,9},{6,5},{7,1},{8,14},{9,10},{1... | collective-permute-start | bytes 13832 | tf_op jit(solution)/shard_map/ppermute | solution.py:237
  42.3 5.4 %collective-permute-start.9 = (bf16[24,96]{1,0:T(8,128)(2,1)S(1)}, bf16[24,96]{1,0:T(8,128)(2,1)S(1)}, u32[]{:S(2)}, u32[]{:S(2)}) collective-permute-start(bf16[24,96]{1,0:T(8,128)(2,1)S(1)} %bitcast.25), channel_id=1, source_target_pairs={{0,0},{1,4},{2,8},{3,12},{4,1},{5,5},{6,9},{7,13},{8,2},{9,6},{10,... | collective-permute-start | bytes 13832 | tf_op jit(solution)/shard_map/ppermute | solution.py:237
  43.2 6.7 %copy-start.6 = (bf16[128,128]{1,0:T(8,128)(2,1)S(1)}, bf16[128,128]{1,0:T(8,128)(2,1)}, u32[]{:S(2)}) copy-start(bf16[128,128]{1,0:T(8,128)(2,1)} %w_gate.3) | copy-start | bytes 98308
  43.2 6.7 %copy-start.7 = (bf16[128,128]{1,0:T(8,128)(2,1)S(1)}, bf16[128,128]{1,0:T(8,128)(2,1)}, u32[]{:S(2)}) copy-start(bf16[128,128]{1,0:T(8,128)(2,1)} %w_out.3) | copy-start | bytes 98308
  (4 other events, 2.8 us)

commit v2 on v1

--- a/solution.py
+++ b/solution.py
@@ -30,8 +30,34 @@
     return (along_rows * along_columns[None]).reshape(rows * columns, -1)
 
 
-def own_kernel(rows, columns, state, row_mask, column_mask, gain, w_in, w_gate, left, right, gate):
+def right_factor(rows, columns, step, normed, row_mask, column_mask, w_in):
+    channels = normed.shape[1]
+    row_start = lax.bitwise_xor(lax.axis_index("row"), step) * rows
+    mask = pair_mask(row_mask, column_mask, rows, columns, row_start, lax.axis_index("col") * columns)
+    part = dot(normed, w_in[:, 2 * channels :])
+    value = mask * jax.nn.sigmoid(part[:, :channels]) * part[:, channels:]
+    return value.astype(jnp.bfloat16).astype(jnp.float32)
+
+
+def multiply(rows, columns, left, right, base, out, out_base):
+    channels = left.shape[1]
+    group = 4 if rows % 4 == 0 else 2
+    for at in range(rows // group):
+        sums = [jnp.zeros((columns, channels), jnp.float32) for _ in range(group)]
+        for k in range(columns):
+            factor = right[pl.ds(base + k, columns, stride=columns), :]
+            for g in range(group):
+                row = left[pl.ds((at * group + g) * columns + k, 1), :]
+                sums[g] = sums[g] + row * factor
+        width = group * columns
+        out[pl.ds(out_base + at * width, width), :] = jnp.concatenate(sums, 0).astype(jnp.bfloat16)
+
+
+def own_kernel(rows, columns, state, row_mask, column_mask, gain, w_in, w_gate, *refs):
+    count = (len(refs) - 4) // 2
+    weights, (left, gate, part_out), copies, right = refs[:count], refs[count : count + 3], refs[count + 3 : -1], refs[-1]
     channels = state.shape[1]
+    size = rows * columns
     row_start = lax.axis_index("row") * rows
     column_start = lax.axis_index("col") * columns
     normed = layer_norm(state[...].astype(jnp.float32), gain[...]).astype(jnp.bfloat16)
@@ -39,46 +65,44 @@
     part = dot(normed, w_in[:, : 2 * channels])
     value = mask * jax.nn.sigmoid(part[:, :channels]) * part[:, channels:]
     left[...] = value.astype(jnp.bfloat16).astype(jnp.float32)
-    part = dot(normed, w_in[:, 2 * channels :])
-    value = mask * jax.nn.sigmoid(part[:, :channels]) * part[:, channels:]
-    right[...] = value.astype(jnp.bfloat16).astype(jnp.float32)
+    right[...] = right_factor(rows, columns, 0, normed, row_mask, column_mask, w_in)
     gate[...] = jax.nn.sigmoid(dot(normed, w_gate[...]))
-
-
-def product_kernel(rows, columns, row_devices, column_devices, row_mask, column_mask, gain, w_in, left, right_own, *refs):
-    states, refs = refs[: row_devices - 1], refs[row_devices - 1 :]
-    outs, right = refs[:column_devices], refs[column_devices]
-    channels = left.shape[1]
+    for part in range(rows // columns):
+        multiply(rows, columns, left, right, part * columns * columns, part_out, part * size)
+    for weight, copy in zip(weights, copies):
+        copy[...] = weight[...]
+
+
+def early_kernel(rows, columns, steps, row_mask, column_mask, gain, w_in, left, *refs):
+    states, part_out, right = refs[: len(steps)], refs[-2], refs[-1]
     size = rows * columns
     split = rows // columns
+    for at, (step, state) in enumerate(zip(steps, states)):
+        normed = layer_norm(state[...].astype(jnp.float32), gain[...]).astype(jnp.bfloat16)
+        right[...] = right_factor(rows, columns, step, normed, row_mask, column_mask, w_in)
+        for part in range(split):
+            multiply(rows, columns, left, right, part * columns * columns, part_out, (at * split + part) * size)
+
+
+def late_kernel(rows, columns, steps, column_devices, row_mask, column_mask, gain, w_in, left, own, early, *refs):
+    states, refs = refs[: len(steps)], refs[len(steps) :]
+    outs, late, right = refs[:column_devices], refs[column_devices], refs[column_devices + 1]
+    size = rows * columns
+    split = rows // columns
+    early_kernel(rows, columns, steps, row_mask, column_mask, gain, w_in, left, *states, late, right)
     row_index, column_index = lax.axis_index("row"), lax.axis_index("col")
-    right[pl.ds(0, size), :] = right_own[...]
-    for step, state in enumerate(states, 1):
-        normed = layer_norm(state[...].astype(jnp.float32), gain[...]).astype(jnp.bfloat16)
-        row_start = lax.bitwise_xor(row_index, step) * rows
-        mask = pair_mask(row_mask, column_mask, rows, columns, row_start, column_index * columns)
-        part = dot(normed, w_in[:, 2 * channels :])
-        value = mask * jax.nn.sigmoid(part[:, :channels]) * part[:, channels:]
-        right[pl.ds(step * size, size), :] = value.astype(jnp.bfloat16).astype(jnp.float32)
-    group = 4 if rows % 4 == 0 else 2
     for step, out in enumerate(outs):
         target = lax.bitwise_xor(column_index, step)
-        held = lax.bitwise_xor(row_index, target // split)
-        base = held * size + (target % split) * columns * columns
-
-        def block(at, carry, out=out, base=base):
-            sums = [jnp.zeros((columns, channels), jnp.float32) for _ in range(group)]
-            for k in range(columns):
-                factor = right[pl.ds(base + k, columns, stride=columns), :]
-                for g in range(group):
-                    row = left[pl.ds((at * group + g) * columns + k, 1), :]
-                    sums[g] = sums[g] + row * factor
-            width = group * columns
-            start = pl.multiple_of(at * width, 16)
-            out[pl.ds(start, width), :] = jnp.concatenate(sums, 0).astype(jnp.bfloat16)
-            return carry
-
-        lax.fori_loop(0, rows // group, block, 0)
+        place = lax.bitwise_xor(row_index, target // split) * split + target % split
+
+        def fill(source, first, last, out=out, place=place):
+            @pl.when((place >= first) & (place < last))
+            def _():
+                out[...] = source[pl.ds(pl.multiple_of((place - first) * size, 16), size), :]
+
+        fill(own, 0, split)
+        fill(early, split, steps[0] * split)
+        fill(late, steps[0] * split, (steps[-1] + 1) * split)
 
 
 def middle_kernel(rows, columns, split, state, gate, product_gain, w_out, attend_gain, w_bias, *refs):
@@ -101,7 +125,7 @@
         bias[part] = total.astype(jnp.bfloat16)
 
 
-def attend_kernel(rows, columns, heads, split, column_devices, middle, allowed, w_query, w_key_value, w_gate, w_out, *refs):
+def attend_kernel(rows, columns, heads, split, column_devices, middle, allowed, w_inputs, w_gate, w_out, *refs):
     tiles, refs = refs[:column_devices], refs[column_devices:]
     biases, refs = refs[:column_devices], refs[column_devices:]
     out, keys, values, queries, gates, bias, gated = refs
@@ -110,11 +134,11 @@
     tokens = columns * column_devices
     row_index, column_index = lax.axis_index("row"), lax.axis_index("col")
     for step, tile in enumerate(tiles):
-        part = dot(tile[...], w_key_value[...]).reshape(rows, columns, 2 * channels)
+        part = dot(tile[...], w_inputs[:, channels:]).reshape(rows, columns, 2 * channels)
         keys[:, pl.ds(step * columns, columns), :] = part[..., :channels]
         values[:, pl.ds(step * columns, columns), :] = part[..., channels:]
     own = tiles[0][...]
-    queries[...] = dot(own, w_query[...])
+    queries[...] = dot(own, w_inputs[:, :channels])
     gates[...] = jax.nn.sigmoid(dot(own, w_gate[...]))
     for step, piece in enumerate(biases):
         place = lax.bitwise_xor(row_index * split + column_index % split, step)
@@ -125,29 +149,43 @@
         here = pl.ds(step * columns, columns)
         bias[here, :] = jnp.where(allowed[pl.ds(start, columns), :] > 0, bias[here, :], -1e30)
     added = bias[...].T
-    head_of_lane = lax.broadcasted_iota(jnp.int32, (1, channels), 1) // width
+    head_of_lane = (lax.broadcasted_iota(jnp.int32, (1, 2 * channels), 1) % channels) // width
     picks = [head_of_lane == h for h in range(heads)]
     scale = 1.0 / math.sqrt(width)
     ones = jnp.ones((tokens, channels), jnp.bfloat16)
 
-    def row(at, carry):
-        start = pl.multiple_of(at * columns, 8)
-        query = queries[pl.ds(start, columns), :]
-        stacked = jnp.concatenate([jnp.where(pick, query, 0.0) for pick in picks], 0).astype(jnp.bfloat16)
-        key = keys[at].astype(jnp.bfloat16)
-        scores = lax.dot_general(stacked, key, (((1,), (1,)), ((), ())), preferred_element_type=jnp.float32)
-        scores = scores * scale + added
-        weights = jnp.exp(scores - jnp.max(scores, axis=-1, keepdims=True)).astype(jnp.bfloat16)
-        value = jnp.concatenate([values[at].astype(jnp.bfloat16), ones], 1)
-        mixed = dot(weights, value)
-        mixed = mixed[:, :channels] / mixed[:, channels:]
-        total = jnp.zeros((columns, channels), jnp.float32)
-        for h, pick in enumerate(picks):
-            total = jnp.where(pick, mixed[h * columns : (h + 1) * columns], total)
-        gated[pl.ds(start, columns), :] = total * gates[pl.ds(start, columns), :]
+    group = max(1, min(rows, 2304 // tokens))
+    while rows % group:
+        group -= 1
+
+    def several(first, carry):
+        places = [first * group + g for g in range(group)]
+        starts = [pl.multiple_of(at * columns, 8) for at in places]
+        scores = []
+        for at, start in zip(places, starts):
+            query = queries[pl.ds(start, columns), :]
+            stacked = jnp.concatenate([jnp.where(pick[:, :channels], query, 0.0) for pick in picks], 0).astype(jnp.bfloat16)
+            key = keys[at].astype(jnp.bfloat16)
+            scores.append(lax.dot_general(stacked, key, (((1,), (1,)), ((), ())), preferred_element_type=jnp.float32))
+        scores = [score * scale + added for score in scores]
+        tops = [jnp.max(score, axis=-1, keepdims=True) for score in scores]
+        weights = [jnp.exp(score - top).astype(jnp.bfloat16) for score, top in zip(scores, tops)]
+        mixed = [
+            dot(weight, jnp.concatenate([values[at].astype(jnp.bfloat16), ones], 1))
+            for weight, at in zip(weights, places)
+        ]
+        for mix, start in zip(mixed, starts):
+            total = mix[:columns]
+            for h in range(1, heads):
+                total = jnp.where(picks[h], mix[h * columns : (h + 1) * columns], total)
+            here = pl.ds(start, columns)
+            gated[here, :] = total[:, :channels] / total[:, channels:] * gates[here, :]
         return carry
 
-    lax.fori_loop(0, rows, row, 0, unroll=4)
+    if group == rows:
+        several(0, 0)
+    else:
+        lax.fori_loop(0, rows // group, several, 0)
     update = dot(gated[...].astype(jnp.bfloat16), w_out[...])
     out[...] = (middle[...].astype(jnp.float32) + update).astype(jnp.bfloat16)
 
@@ -206,24 +244,50 @@
     allowed = jnp.tile(allowed, (1, heads))
     w_bias = jnp.repeat(attend_bias, columns, axis=1)
 
-    left, right, gate = call(
+    norm_in = triangle_norm[None]
+    weights = [
+        product_norm[None],
+        triangle_output,
+        attend_norm[None],
+        w_bias,
+        allowed,
+        attend_inputs,
+        attend_gate,
+        attend_output,
+    ]
+    flat = pltpu.VMEM((size, channels), jnp.float32)
+    left, gate, own, *weights = call(
         functools.partial(own_kernel, rows, columns),
-        [wide, wide, wide],
-        [state, row_mask, column_mask, triangle_norm[None], triangle_input, triangle_gate],
+        [wide, wide, jax.ShapeDtypeStruct((split * size, channels), jnp.bfloat16)]
+        + [jax.ShapeDtypeStruct(weight.shape, weight.dtype) for weight in weights],
+        [state, row_mask, column_mask, norm_in, triangle_input, triangle_gate] + weights,
+        [flat],
+    )
+    w_product, w_middle, w_attend, w_bias, allowed, w_inputs, w_gate, w_out = weights
+    half = row_devices // 2
+    early_steps, late_steps = list(range(1, half)), list(range(half, row_devices))
+    common = [row_mask, column_mask, norm_in, triangle_input, left]
+    early = call(
+        functools.partial(early_kernel, rows, columns, early_steps),
+        jax.ShapeDtypeStruct((len(early_steps) * split * size, channels), jnp.bfloat16),
+        common + [others[step - 1] for step in early_steps],
+        [flat],
     )
     parts = call(
-        functools.partial(product_kernel, rows, columns, row_devices, column_devices),
+        functools.partial(late_kernel, rows, columns, late_steps, column_devices),
         [tile] * column_devices,
-        [row_mask, column_mask, triangle_norm[None], triangle_input, left, right] + others,
-        [pltpu.VMEM((row_devices * size, channels), jnp.float32)],
-    )
-    parts = [parts[0]] + [exchange(parts[step], "col", step) for step in range(1, column_devices)]
+        common + [own, early] + [others[step - 1] for step in late_steps],
+        [pltpu.VMEM((len(late_steps) * split * size, channels), jnp.bfloat16), flat],
+    )
+    order = sorted(range(1, column_devices), key=lambda step: (step != 2, step))
+    parts = [parts[0]] + [exchange(parts[step], "col", step) for step in order]
     middle, attend, bias = call(
         functools.partial(middle_kernel, rows, columns, split),
         [tile, tile, jax.ShapeDtypeStruct((split, columns, heads * columns), jnp.bfloat16)],
-        [state, gate, product_norm[None], triangle_output, attend_norm[None], w_bias] + parts,
-    )
-    tiles = [attend] + [exchange(attend, "col", step) for step in range(1, column_devices)]
+        [state, gate, w_product, w_middle, w_attend, w_bias] + parts,
+    )
+    moved = {step: exchange(attend, "col", step) for step in order}
+    tiles = [attend] + [moved[step] for step in range(1, column_devices)]
     biases = []
     for step in range(column_devices):
         piece = bias[0]
@@ -236,11 +300,10 @@
                 pairs.append((a * column_devices + b, (turn // split) * column_devices + split * a + turn % split))
         biases.append(lax.ppermute(piece, ("row", "col"), pairs))
     stack = pltpu.VMEM((rows, tokens, channels), jnp.float32)
-    flat = pltpu.VMEM((size, channels), jnp.float32)
     result = call(
         functools.partial(attend_kernel, rows, columns, heads, split, column_devices),
         tile,
-        [middle, allowed, attend_inputs[:, :channels], attend_inputs[:, channels:], attend_gate, attend_output]
+        [middle, allowed, w_inputs, w_gate, w_out]
         + tiles
         + biases,
         [stack, stack, flat, flat, pltpu.VMEM((tokens, heads * columns), jnp.float32), flat],

time: 58.2 us -> 53.2 us (0.914)
  the two profiles are of different devices: /device:TPU:0 before, /device:TPU:4 now
where the time goes in v2:
time: 53.2 us; the launch traced here: 53 us
  starting transfers between devices  24.8 us (47%)
  waiting for transfers between devices  18.6 us (35%)
  Pallas kernels  6.59 us (12%)
  local copies, waits for them, and re-layouts  2.69 us (5%)
    ppermute x9, starting transfers between devices, exchange(): return lax.ppermute(value, axis, [(at, at ^ step) for at in range(size)])  13.1 us
    ppermute x4, starting transfers between devices, shards(): biases.append(lax.ppermute(piece, ('row', 'col'), pairs))  11.7 us
    ppermute x9, waiting for transfers between devices, exchange(): return lax.ppermute(value, axis, [(at, at ^ step) for at in range(size)])  11.1 us
    ppermute x4, waiting for transfers between devices, shards(): biases.append(lax.ppermute(piece, ('row', 'col'), pairs))  7.49 us
    pallas_call x5, Pallas kernels, call(): pl.pallas_call(kernel, out_shape=outs, in_specs=[VMEM] * len(args), out_s...  6.59 us
    unnamed x27, local copies, waits for them, and re-layouts  2.03 us
  transfers between devices with their start and end apart: 13, of which 6 were waited for; matrix products, arithmetic and copies ran while one was open for 2% of the time, Pallas kernels for 4%

profile of v2, /device:TPU:4, one launch (start us, length us, event | category | flops | bytes accessed | tf_op | source)
XLA Modules:
  0.0 53.0 jit_solution(13616907917547801803)
XLA Ops:
  0.0 1.4 %collective-permute-start.2 = (bf16[576,128]{1,0:T(8,128)(2,1)}, bf16[576,128]{1,0:T(8,128)(2,1)S(1)}, u32[]{:S(2)}, u32[]{:S(2)}) collective-permute-start(bf16[576,128]{1,0:T(8,128)(2,1)} %bitcast.13), channel_id=1, source_target_pairs={{0,12},{4,8},{8,4},{12,0},{1,13},{5,9},{9,5},{13,1},{2,14},{6,10},... | collective-permute-start | bytes 442376 | tf_op jit(solution)/shard_map/ppermute | solution.py:206
  1.4 1.5 %collective-permute-start.1 = (bf16[576,128]{1,0:T(8,128)(2,1)}, bf16[576,128]{1,0:T(8,128)(2,1)S(1)}, u32[]{:S(2)}, u32[]{:S(2)}) collective-permute-start(bf16[576,128]{1,0:T(8,128)(2,1)} %bitcast.14), channel_id=1, source_target_pairs={{0,8},{4,12},{8,0},{12,4},{1,9},{5,13},{9,1},{13,5},{2,10},{6,14},... | collective-permute-start | bytes 442376 | tf_op jit(solution)/shard_map/ppermute | solution.py:206
  3.0 0.5 %collective-permute-start = (bf16[576,128]{1,0:T(8,128)(2,1)}, bf16[576,128]{1,0:T(8,128)(2,1)S(1)}, u32[]{:S(2)}, u32[]{:S(2)}) collective-permute-start(bf16[576,128]{1,0:T(8,128)(2,1)} %bitcast.15), channel_id=1, source_target_pairs={{0,4},{4,0},{8,12},{12,8},{1,5},{5,1},{9,13},{13,9},{2,6},{6,2},{1... | collective-permute-start | bytes 442376 | tf_op jit(solution)/shard_map/ppermute | solution.py:206
  3.5 0.7 %copy-done.10 = s32[4,4]{1,0:T(4,128)S(1)} copy-done((s32[4,4]{1,0:T(4,128)S(1)}, s32[4,4]{1,0:T(4,128)}, u32[]{:S(2)}) %copy-start.10) | copy-done | bytes 88
  4.4 0.6 %copy-done.11 = bf16[128,4]{0,1:T(4,128)(2,1)S(1)} copy-done((bf16[128,4]{0,1:T(4,128)(2,1)S(1)}, bf16[128,4]{0,1:T(4,128)(2,1)}, u32[]{:S(2)}) %copy-start.11) | copy-done | bytes 1048
  6.4 1.1 %shard_map.127 = (f32[576,128]{1,0:T(8,128)S(1)}, f32[576,128]{1,0:T(8,128)S(1)}, bf16[576,128]{1,0:T(8,128)(2,1)S(1)}, f32[1,128]{1,0:T(1,128)S(1)}, bf16[128,1...) custom-call(bf16[576,128]{1,0:T(8,128)(2,1)S(1)} %bitcast.16, ...), custom_call_target="tpu_custom_call" | custom-call | tf_op jit(solution)/shard_map/pallas_call | solution.py:194
  7.5 1.2 %collective-permute-done.refs_0_ = bf16[576,128]{1,0:T(8,128)(2,1)S(1)} collective-permute-done((bf16[576,128]{1,0:T(8,128)(2,1)}, bf16[576,128]{1,0:T(8,128)(2,1)S(1)}, u32[]{:S(2)}, u32[]{:S(2)}) %collective-permute-start) | collective-permute-done | bytes 147488 | tf_op jit(solution)/shard_map/ppermute | solution.py:206
  8.7 0.9 %shard_map.128.early = bf16[576,128]{1,0:T(8,128)(2,1)S(1)} custom-call(f32[96,1,128]{2,1,0:T(1,128)S(1)} %broadcast_in_dim.31.row_mask, f32[96,128]{1,0:T(8,128)S(1)} %broadcast_in_dim.32.column_mask, f32[1,128]{1,0:T(1,128)S(1)} %bitcast.19, bf16[128,512]{1,0:T(8,128)(2,1)S(1)} %copy-done, f32[576,128]{1,0:T(8,128)S(1)} %get-tuple-element.28.left, ...), custom_call_target="tpu_custom_call" | custom-call | tf_op jit(solution)/shard_map/pallas_call | solution.py:194
  9.9 1.8 %shard_map.129 = (bf16[576,128]{1,0:T(8,128)(2,1)S(1)}, bf16[576,128]{1,0:T(8,128)(2,1)S(1)}, bf16[576,128]{1,0:T(8,128)(2,1)S(1)}, bf16[576,128]{1,0:T(8,128)(2,1)S(1)}) custom-call(f32[96,1,128]{2,1,0:T(1,128)S(1)} %broadcast_in_dim.31.row_mask, f32[96,128]{1,0:T(8,128)S(1)} %broadcast_in_dim.32.column_mask, f32[1,128]{1,0:T(1,128)S(1)} %bitcast.20, ...), custom_call_target="tpu_custom_call" | custom-call | tf_op jit(solution)/shard_map/pallas_call | solution.py:194
  11.6 2.7 %collective-permute-start.3 = (bf16[576,128]{1,0:T(8,128)(2,1)S(1)}, bf16[576,128]{1,0:T(8,128)(2,1)S(1)}, u32[]{:S(2)}, u32[]{:S(2)}) collective-permute-start(bf16[576,128]{1,0:T(8,128)(2,1)S(1)} %get-tuple-element.31), channel_id=1, source_target_pairs={{0,2},{1,3},{2,0},{3,1},{4,6},{5,7},{6,4},{7,5},{8,10},{9,11},{10,... | collective-permute-start | bytes 442376 | tf_op jit(solution)/shard_map/ppermute | solution.py:206
  14.3 1.6 %collective-permute-start.4 = (bf16[576,128]{1,0:T(8,128)(2,1)S(1)}, bf16[576,128]{1,0:T(8,128)(2,1)S(1)}, u32[]{:S(2)}, u32[]{:S(2)}) collective-permute-start(bf16[576,128]{1,0:T(8,128)(2,1)S(1)} %get-tuple-element.32), channel_id=1, source_target_pairs={{0,1},{1,0},{2,3},{3,2},{4,5},{5,4},{6,7},{7,6},{8,9},{9,8},{10,11... | collective-permute-start | bytes 442376 | tf_op jit(solution)/shard_map/ppermute | solution.py:206
  15.9 0.2 collective-permute-start.5
  16.1 7.2 %collective-permute-done.3.refs_1_ = bf16[576,128]{1,0:T(8,128)(2,1)S(1)} collective-permute-done((bf16[576,128]{1,0:T(8,128)(2,1)S(1)}, bf16[576,128]{1,0:T(8,128)(2,1)S(1)}, u32[]{:S(2)}, u32[]{:S(2)}) %collective-permute-start.3) | collective-permute-done | bytes 147488 | tf_op jit(solution)/shard_map/ppermute | solution.py:206
  23.3 2.5 %collective-permute-done.5.refs_3_ = bf16[576,128]{1,0:T(8,128)(2,1)S(1)} collective-permute-done((bf16[576,128]{1,0:T(8,128)(2,1)S(1)}, bf16[576,128]{1,0:T(8,128)(2,1)S(1)}, u32[]{:S(2)}, u32[]{:S(2)}) %collective-permute-start.5) | collective-permute-done | bytes 147488 | tf_op jit(solution)/shard_map/ppermute | solution.py:206
  25.8 0.7 %shard_map.130 = (bf16[576,128]{1,0:T(8,128)(2,1)S(1)}, bf16[576,128]{1,0:T(8,128)(2,1)S(1)}, bf16[1,24,96]{2,1,0:T(8,128)(2,1)S(1)}) custom-call(bf16[576,128]{1,0:T(8,128)(2,1)S(1)} %bitcast.17, f32[576,128]{1,0:T(8,128)S(1)} %get-tuple-element.23.gate, f32[1,128]{1,0:T(1,128)S(1)} %get-tuple-element.24.product_gain, ...), custom_call_target="tpu_custom_call" | custom-call | tf_op jit(solution)/shard_map/pallas_call | solution.py:194
  26.6 2.5 %collective-permute-start.8 = (bf16[576,128]{1,0:T(8,128)(2,1)S(1)}, bf16[576,128]{1,0:T(8,128)(2,1)S(1)}, u32[]{:S(2)}, u32[]{:S(2)}) collective-permute-start(bf16[576,128]{1,0:T(8,128)(2,1)S(1)} %get-tuple-element.39.refs_0_), channel_id=1, source_target_pairs={{0,3},{1,2},{2,1},{3,0},{4,7},{5,6},{6,5},{7,4},{8,11},{9,10},{10,... | collective-permute-start | bytes 442376 | tf_op jit(solution)/shard_map/ppermute | solution.py:206
  29.1 2.2 %collective-permute-start.7 = (bf16[576,128]{1,0:T(8,128)(2,1)S(1)}, bf16[576,128]{1,0:T(8,128)(2,1)S(1)}, u32[]{:S(2)}, u32[]{:S(2)}) collective-permute-start(bf16[576,128]{1,0:T(8,128)(2,1)S(1)} %get-tuple-element.39.refs_0_), channel_id=1, source_target_pairs={{0,2},{1,3},{2,0},{3,1},{4,6},{5,7},{6,4},{7,5},{8,10},{9,11},{10,... | collective-permute-start | bytes 442376 | tf_op jit(solution)/shard_map/ppermute | solution.py:206
  31.3 0.5 collective-permute-start.6
  31.8 4.4 %collective-permute-start.12 = (bf16[24,96]{1,0:T(8,128)(2,1)S(1)}, bf16[24,96]{1,0:T(8,128)(2,1)S(1)}, u32[]{:S(2)}, u32[]{:S(2)}) collective-permute-start(bf16[24,96]{1,0:T(8,128)(2,1)S(1)} %bitcast.23), channel_id=1, source_target_pairs={{0,12},{1,8},{2,4},{3,0},{4,13},{5,9},{6,5},{7,1},{8,14},{9,10},{1... | collective-permute-start | bytes 13832 | tf_op jit(solution)/shard_map/ppermute | solution.py:301
  36.2 2.1 %collective-permute-done.12.refs_7_ = bf16[24,96]{1,0:T(8,128)(2,1)S(1)} collective-permute-done((bf16[24,96]{1,0:T(8,128)(2,1)S(1)}, bf16[24,96]{1,0:T(8,128)(2,1)S(1)}, u32[]{:S(2)}, u32[]{:S(2)}) %collective-permute-start.12) | collective-permute-done | bytes 4640 | tf_op jit(solution)/shard_map/ppermute | solution.py:301
  38.3 5.3 %collective-permute-start.10 = (bf16[24,96]{1,0:T(8,128)(2,1)S(1)}, bf16[24,96]{1,0:T(8,128)(2,1)S(1)}, u32[]{:S(2)}, u32[]{:S(2)}) collective-permute-start(bf16[24,96]{1,0:T(8,128)(2,1)S(1)} %bitcast.25), channel_id=1, source_target_pairs={{0,4},{1,0},{2,12},{3,8},{4,5},{5,1},{6,13},{7,9},{8,6},{9,2},{10,... | collective-permute-start | bytes 13832 | tf_op jit(solution)/shard_map/ppermute | solution.py:301
  43.7 1.9 %collective-permute-start.9 = (bf16[24,96]{1,0:T(8,128)(2,1)S(1)}, bf16[24,96]{1,0:T(8,128)(2,1)S(1)}, u32[]{:S(2)}, u32[]{:S(2)}) collective-permute-start(bf16[24,96]{1,0:T(8,128)(2,1)S(1)} %bitcast.26), channel_id=1, source_target_pairs={{0,0},{1,4},{2,8},{3,12},{4,1},{5,5},{6,9},{7,13},{8,2},{9,6},{10,... | collective-permute-start | bytes 13832 | tf_op jit(solution)/shard_map/ppermute | solution.py:301
  45.6 5.4 %collective-permute-done.9.refs_4_ = bf16[24,96]{1,0:T(8,128)(2,1)S(1)} collective-permute-done((bf16[24,96]{1,0:T(8,128)(2,1)S(1)}, bf16[24,96]{1,0:T(8,128)(2,1)S(1)}, u32[]{:S(2)}, u32[]{:S(2)}) %collective-permute-start.9) | collective-permute-done | bytes 4640 | tf_op jit(solution)/shard_map/ppermute | solution.py:301
  51.0 2.0 %shard_map.131 = bf16[576,128]{1,0:T(8,128)(2,1)} custom-call(bf16[576,128]{1,0:T(8,128)(2,1)S(1)} %get-tuple-element.34.middle, f32[96,96]{1,0:T(8,128)S(1)} %get-tuple-element.35.allowed, bf16[128,384]{1,0:T(8,128)(2,1)S(1)} %get-tuple-element.36.w_inputs, bf16[128,128]{1,0:T(8,128)(2,1)S(1)} %get-tuple-element.37.w_gate, ...), custom_call_target="tpu_custom_call" | custom-call | tf_op jit(solution)/shard_map/pallas_call | solution.py:194
  (47 shorter events, 1.7 us)
Async XLA Ops:
  0.0 3.5 %copy-start.12 = (s32[96]{0:T(128)S(1)}, s32[96]{0:T(128)}, u32[]{:S(2)}) copy-start(s32[96]{0:T(128)} %param.14) | copy-start | bytes 1156
  0.0 9.7 %collective-permute-start.2 = (bf16[576,128]{1,0:T(8,128)(2,1)}, bf16[576,128]{1,0:T(8,128)(2,1)S(1)}, u32[]{:S(2)}, u32[]{:S(2)}) collective-permute-start(bf16[576,128]{1,0:T(8,128)(2,1)} %bitcast.13), channel_id=1, source_target_pairs={{0,12},{4,8},{8,4},{12,0},{1,13},{5,9},{9,5},{13,1},{2,14},{6,10},... | collective-permute-start | bytes 442376 | tf_op jit(solution)/shard_map/ppermute | solution.py:206
  1.4 8.4 %collective-permute-start.1 = (bf16[576,128]{1,0:T(8,128)(2,1)}, bf16[576,128]{1,0:T(8,128)(2,1)S(1)}, u32[]{:S(2)}, u32[]{:S(2)}) collective-permute-start(bf16[576,128]{1,0:T(8,128)(2,1)} %bitcast.14), channel_id=1, source_target_pairs={{0,8},{4,12},{8,0},{12,4},{1,9},{5,13},{9,1},{13,5},{2,10},{6,14},... | collective-permute-start | bytes 442376 | tf_op jit(solution)/shard_map/ppermute | solution.py:206
  3.0 5.8 %collective-permute-start = (bf16[576,128]{1,0:T(8,128)(2,1)}, bf16[576,128]{1,0:T(8,128)(2,1)S(1)}, u32[]{:S(2)}, u32[]{:S(2)}) collective-permute-start(bf16[576,128]{1,0:T(8,128)(2,1)} %bitcast.15), channel_id=1, source_target_pairs={{0,4},{4,0},{8,12},{12,8},{1,5},{5,1},{9,13},{13,9},{2,6},{6,2},{1... | collective-permute-start | bytes 442376 | tf_op jit(solution)/shard_map/ppermute | solution.py:206
  5.0 0.8 %copy-start.6 = (bf16[128,128]{1,0:T(8,128)(2,1)S(1)}, bf16[128,128]{1,0:T(8,128)(2,1)}, u32[]{:S(2)}) copy-start(bf16[128,128]{1,0:T(8,128)(2,1)} %refs_7_.1) | copy-start | bytes 98308
  5.2 0.8 %copy-start.4 = (bf16[128,128]{1,0:T(8,128)(2,1)S(1)}, bf16[128,128]{1,0:T(8,128)(2,1)}, u32[]{:S(2)}) copy-start(bf16[128,128]{1,0:T(8,128)(2,1)} %refs_1_.1) | copy-start | bytes 98308
  5.2 0.8 %copy-start.5 = (bf16[128,128]{1,0:T(8,128)(2,1)S(1)}, bf16[128,128]{1,0:T(8,128)(2,1)}, u32[]{:S(2)}) copy-start(bf16[128,128]{1,0:T(8,128)(2,1)} %refs_6_.1) | copy-start | bytes 98308
  5.2 0.9 %copy-start.2 = (bf16[128,384]{1,0:T(8,128)(2,1)S(1)}, bf16[128,384]{1,0:T(8,128)(2,1)}, u32[]{:S(2)}) copy-start(bf16[128,384]{1,0:T(8,128)(2,1)} %refs_5_.1) | copy-start | bytes 294916
  5.3 0.9 %copy-start.1 = (bf16[24,24,128]{2,1,0:T(8,128)(2,1)S(1)}, bf16[24,24,128]{2,1,0:T(8,128)(2,1)}, u32[]{:S(2)}) copy-start(bf16[24,24,128]{2,1,0:T(8,128)(2,1)} %param.13) | copy-start | bytes 442372
  5.4 1.0 %copy-start = (bf16[128,512]{1,0:T(8,128)(2,1)S(1)}, bf16[128,512]{1,0:T(8,128)(2,1)}, u32[]{:S(2)}) copy-start(bf16[128,512]{1,0:T(8,128)(2,1)} %w_in.5) | copy-start | bytes 393220
  5.6 0.8 %copy-start.3 = (bf16[128,128]{1,0:T(8,128)(2,1)S(1)}, bf16[128,128]{1,0:T(8,128)(2,1)}, u32[]{:S(2)}) copy-start(bf16[128,128]{1,0:T(8,128)(2,1)} %w_gate.1) | copy-start | bytes 98308
  5.6 0.8 %copy-start.7 = (f32[128]{0:T(128)S(1)}, f32[128]{0:T(128)}, u32[]{:S(2)}) copy-start(f32[128]{0:T(128)} %param.16) | copy-start | bytes 1540
  5.6 0.8 %copy-start.8 = (f32[128]{0:T(128)S(1)}, f32[128]{0:T(128)}, u32[]{:S(2)}) copy-start(f32[128]{0:T(128)} %param.19) | copy-start | bytes 1540
  5.6 0.8 %copy-start.9 = (f32[128]{0:T(128)S(1)}, f32[128]{0:T(128)}, u32[]{:S(2)}) copy-start(f32[128]{0:T(128)} %param.21) | copy-start | bytes 1540
  11.6 11.7 %collective-permute-start.3 = (bf16[576,128]{1,0:T(8,128)(2,1)S(1)}, bf16[576,128]{1,0:T(8,128)(2,1)S(1)}, u32[]{:S(2)}, u32[]{:S(2)}) collective-permute-start(bf16[576,128]{1,0:T(8,128)(2,1)S(1)} %get-tuple-element.31), channel_id=1, source_target_pairs={{0,2},{1,3},{2,0},{3,1},{4,6},{5,7},{6,4},{7,5},{8,10},{9,11},{10,... | collective-permute-start | bytes 442376 | tf_op jit(solution)/shard_map/ppermute | solution.py:206
  14.3 9.0 %collective-permute-start.4 = (bf16[576,128]{1,0:T(8,128)(2,1)S(1)}, bf16[576,128]{1,0:T(8,128)(2,1)S(1)}, u32[]{:S(2)}, u32[]{:S(2)}) collective-permute-start(bf16[576,128]{1,0:T(8,128)(2,1)S(1)} %get-tuple-element.32), channel_id=1, source_target_pairs={{0,1},{1,0},{2,3},{3,2},{4,5},{5,4},{6,7},{7,6},{8,9},{9,8},{10,11... | collective-permute-start | bytes 442376 | tf_op jit(solution)/shard_map/ppermute | solution.py:206
  15.9 10.0 %collective-permute-start.5 = (bf16[576,128]{1,0:T(8,128)(2,1)S(1)}, bf16[576,128]{1,0:T(8,128)(2,1)S(1)}, u32[]{:S(2)}, u32[]{:S(2)}) collective-permute-start(bf16[576,128]{1,0:T(8,128)(2,1)S(1)} %get-tuple-element.33), channel_id=1, source_target_pairs={{0,3},{1,2},{2,1},{3,0},{4,7},{5,6},{6,5},{7,4},{8,11},{9,10},{10,... | collective-permute-start | bytes 442376 | tf_op jit(solution)/shard_map/ppermute | solution.py:206
  26.6 24.4 %collective-permute-start.8 = (bf16[576,128]{1,0:T(8,128)(2,1)S(1)}, bf16[576,128]{1,0:T(8,128)(2,1)S(1)}, u32[]{:S(2)}, u32[]{:S(2)}) collective-permute-start(bf16[576,128]{1,0:T(8,128)(2,1)S(1)} %get-tuple-element.39.refs_0_), channel_id=1, source_target_pairs={{0,3},{1,2},{2,1},{3,0},{4,7},{5,6},{6,5},{7,4},{8,11},{9,10},{10,... | collective-permute-start | bytes 442376 | tf_op jit(solution)/shard_map/ppermute | solution.py:206
  29.1 21.9 %collective-permute-start.7 = (bf16[576,128]{1,0:T(8,128)(2,1)S(1)}, bf16[576,128]{1,0:T(8,128)(2,1)S(1)}, u32[]{:S(2)}, u32[]{:S(2)}) collective-permute-start(bf16[576,128]{1,0:T(8,128)(2,1)S(1)} %get-tuple-element.39.refs_0_), channel_id=1, source_target_pairs={{0,2},{1,3},{2,0},{3,1},{4,6},{5,7},{6,4},{7,5},{8,10},{9,11},{10,... | collective-permute-start | bytes 442376 | tf_op jit(solution)/shard_map/ppermute | solution.py:206
  31.3 19.7 %collective-permute-start.6 = (bf16[576,128]{1,0:T(8,128)(2,1)S(1)}, bf16[576,128]{1,0:T(8,128)(2,1)S(1)}, u32[]{:S(2)}, u32[]{:S(2)}) collective-permute-start(bf16[576,128]{1,0:T(8,128)(2,1)S(1)} %get-tuple-element.39.refs_0_), channel_id=1, source_target_pairs={{0,1},{1,0},{2,3},{3,2},{4,5},{5,4},{6,7},{7,6},{8,9},{9,8},{10,11... | collective-permute-start | bytes 442376 | tf_op jit(solution)/shard_map/ppermute | solution.py:206
  31.8 6.5 %collective-permute-start.12 = (bf16[24,96]{1,0:T(8,128)(2,1)S(1)}, bf16[24,96]{1,0:T(8,128)(2,1)S(1)}, u32[]{:S(2)}, u32[]{:S(2)}) collective-permute-start(bf16[24,96]{1,0:T(8,128)(2,1)S(1)} %bitcast.23), channel_id=1, source_target_pairs={{0,12},{1,8},{2,4},{3,0},{4,13},{5,9},{6,5},{7,1},{8,14},{9,10},{1... | collective-permute-start | bytes 13832 | tf_op jit(solution)/shard_map/ppermute | solution.py:301
  36.2 7.5 %collective-permute-start.11 = (bf16[24,96]{1,0:T(8,128)(2,1)S(1)}, bf16[24,96]{1,0:T(8,128)(2,1)S(1)}, u32[]{:S(2)}, u32[]{:S(2)}) collective-permute-start(bf16[24,96]{1,0:T(8,128)(2,1)S(1)} %bitcast.24), channel_id=1, source_target_pairs={{0,8},{1,12},{2,0},{3,4},{4,9},{5,13},{6,1},{7,5},{8,10},{9,14},{1... | collective-permute-start | bytes 13832 | tf_op jit(solution)/shard_map/ppermute | solution.py:301
  38.3 7.3 %collective-permute-start.10 = (bf16[24,96]{1,0:T(8,128)(2,1)S(1)}, bf16[24,96]{1,0:T(8,128)(2,1)S(1)}, u32[]{:S(2)}, u32[]{:S(2)}) collective-permute-start(bf16[24,96]{1,0:T(8,128)(2,1)S(1)} %bitcast.25), channel_id=1, source_target_pairs={{0,4},{1,0},{2,12},{3,8},{4,5},{5,1},{6,13},{7,9},{8,6},{9,2},{10,... | collective-permute-start | bytes 13832 | tf_op jit(solution)/shard_map/ppermute | solution.py:301
  43.7 7.3 %collective-permute-start.9 = (bf16[24,96]{1,0:T(8,128)(2,1)S(1)}, bf16[24,96]{1,0:T(8,128)(2,1)S(1)}, u32[]{:S(2)}, u32[]{:S(2)}) collective-permute-start(bf16[24,96]{1,0:T(8,128)(2,1)S(1)} %bitcast.26), channel_id=1, source_target_pairs={{0,0},{1,4},{2,8},{3,12},{4,1},{5,5},{6,9},{7,13},{8,2},{9,6},{10,... | collective-permute-start | bytes 13832 | tf_op jit(solution)/shard_map/ppermute | solution.py:301
  (2 other events, 1.4 us)

commit v3 on v2

--- a/solution.py
+++ b/solution.py
@@ -101,8 +101,8 @@
                 out[...] = source[pl.ds(pl.multiple_of((place - first) * size, 16), size), :]
 
         fill(own, 0, split)
-        fill(early, split, steps[0] * split)
-        fill(late, steps[0] * split, (steps[-1] + 1) * split)
+        fill(late, split, (steps[-1] + 1) * split)
+        fill(early, (steps[-1] + 1) * split, (steps[-1] + 1) * split + early.shape[0] // size)
 
 
 def middle_kernel(rows, columns, split, state, gate, product_gain, w_out, attend_gain, w_bias, *refs):
@@ -116,24 +116,36 @@
     middle[...] = rounded
     normed = layer_norm(rounded.astype(jnp.float32), attend_gain[...]).astype(jnp.bfloat16)
     attend[...] = normed
+    for part, total in enumerate(bias_parts(rows, columns, split, normed, w_bias)):
+        bias[part] = total.astype(jnp.bfloat16)
+
+
+def bias_parts(rows, columns, split, normed, w_bias):
     spread = dot(normed, w_bias[...]).reshape(rows, columns, -1)
     lane = lax.broadcasted_iota(jnp.int32, spread.shape[1:], 1) % columns
+    parts = []
     for part in range(split):
         total = jnp.zeros(spread.shape[1:], jnp.float32)
         for j in range(columns):
             total = jnp.where(lane == j, spread[part * columns + j], total)
-        bias[part] = total.astype(jnp.bfloat16)
-
-
-def attend_kernel(rows, columns, heads, split, column_devices, middle, allowed, w_inputs, w_gate, w_out, *refs):
+        parts.append(total)
+    return parts
+
+
+def neighbor_kernel(rows, columns, split, own, attend, w_bias, bias):
+    for part, total in enumerate(bias_parts(rows, columns, split, attend[...], w_bias)):
+        bias[part] = jnp.concatenate([own[part].astype(jnp.float32), total], 0).astype(jnp.bfloat16)
+
+
+def attend_kernel(rows, columns, heads, split, column_devices, arrival, middle, allowed, w_inputs, w_gate, w_out, *refs):
     tiles, refs = refs[:column_devices], refs[column_devices:]
-    biases, refs = refs[:column_devices], refs[column_devices:]
+    biases, refs = refs[: column_devices // 2], refs[column_devices // 2 :]
     out, keys, values, queries, gates, bias, gated = refs
     channels = middle.shape[1]
     width = channels // heads
     tokens = columns * column_devices
     row_index, column_index = lax.axis_index("row"), lax.axis_index("col")
-    for step, tile in enumerate(tiles):
+    for step, tile in zip(arrival, tiles):
         part = dot(tile[...], w_inputs[:, channels:]).reshape(rows, columns, 2 * channels)
         keys[:, pl.ds(step * columns, columns), :] = part[..., :channels]
         values[:, pl.ds(step * columns, columns), :] = part[..., channels:]
@@ -141,9 +153,12 @@
     queries[...] = dot(own, w_inputs[:, :channels])
     gates[...] = jax.nn.sigmoid(dot(own, w_gate[...]))
     for step, piece in enumerate(biases):
-        place = lax.bitwise_xor(row_index * split + column_index % split, step)
-        place = lax.bitwise_xor(place, column_index)
-        bias[pl.ds(pl.multiple_of(place * columns, 8), columns), :] = piece[...].astype(jnp.float32)
+        piece = piece[...].astype(jnp.float32)
+        for side in range(2):
+            place = lax.bitwise_xor(row_index * split + column_index % split, 2 * step + 1 - side)
+            place = lax.bitwise_xor(place, column_index)
+            here = pl.ds(pl.multiple_of(place * columns, 8), columns)
+            bias[here, :] = piece[side * columns : (side + 1) * columns]
     for step in range(column_devices):
         start = pl.multiple_of(lax.bitwise_xor(column_index, step) * columns, 8)
         here = pl.ds(step * columns, columns)
@@ -264,8 +279,8 @@
         [flat],
     )
     w_product, w_middle, w_attend, w_bias, allowed, w_inputs, w_gate, w_out = weights
-    half = row_devices // 2
-    early_steps, late_steps = list(range(1, half)), list(range(half, row_devices))
+    early_steps = list(range(row_devices - row_devices // 4, row_devices))
+    late_steps = list(range(1, early_steps[0]))
     common = [row_mask, column_mask, norm_in, triangle_input, left]
     early = call(
         functools.partial(early_kernel, rows, columns, early_steps),
@@ -279,7 +294,7 @@
         common + [own, early] + [others[step - 1] for step in late_steps],
         [pltpu.VMEM((len(late_steps) * split * size, channels), jnp.bfloat16), flat],
     )
-    order = sorted(range(1, column_devices), key=lambda step: (step != 2, step))
+    order = list(range(column_devices - 1, 2, -1)) + [1, 2]
     parts = [parts[0]] + [exchange(parts[step], "col", step) for step in order]
     middle, attend, bias = call(
         functools.partial(middle_kernel, rows, columns, split),
@@ -287,12 +302,18 @@
         [state, gate, w_product, w_middle, w_attend, w_bias] + parts,
     )
     moved = {step: exchange(attend, "col", step) for step in order}
-    tiles = [attend] + [moved[step] for step in range(1, column_devices)]
+    arrival = [0, 1] + list(range(column_devices - 1, 1, -1))
+    tiles = [attend] + [moved[step] for step in arrival[1:]]
+    both = call(
+        functools.partial(neighbor_kernel, rows, columns, split),
+        jax.ShapeDtypeStruct((split, 2 * columns, heads * columns), jnp.bfloat16),
+        [bias, moved[1], w_bias],
+    )
     biases = []
-    for step in range(column_devices):
-        piece = bias[0]
+    for step in range(1, column_devices, 2):
+        piece = both[0]
         if split > 1:
-            piece = lax.dynamic_index_in_dim(bias, lax.bitwise_xor(column_index, step) % split, 0, False)
+            piece = lax.dynamic_index_in_dim(both, lax.bitwise_xor(column_index, step) % split, 0, False)
         pairs = []
         for a in range(row_devices):
             for b in range(column_devices):
@@ -301,7 +322,7 @@
         biases.append(lax.ppermute(piece, ("row", "col"), pairs))
     stack = pltpu.VMEM((rows, tokens, channels), jnp.float32)
     result = call(
-        functools.partial(attend_kernel, rows, columns, heads, split, column_devices),
+        functools.partial(attend_kernel, rows, columns, heads, split, column_devices, arrival),
         tile,
         [middle, allowed, w_inputs, w_gate, w_out]
         + tiles

time: 53.2 us -> 47.6 us (0.89)
  the two profiles are of different devices: /device:TPU:4 before, /device:TPU:6 now
where the time goes in v3:
time: 47.6 us; the launch traced here: 47.4 us
  waiting for transfers between devices  23.5 us (49%)
  starting transfers between devices  14.2 us (30%)
  Pallas kernels  6.77 us (14%)
  local copies, waits for them, and re-layouts  2.69 us (6%)
    ppermute x9, waiting for transfers between devices, exchange(): return lax.ppermute(value, axis, [(at, at ^ step) for at in range(size)])  20.4 us
    ppermute x9, starting transfers between devices, exchange(): return lax.ppermute(value, axis, [(at, at ^ step) for at in range(size)])  12.4 us
    pallas_call x6, Pallas kernels, call(): pl.pallas_call(kernel, out_shape=outs, in_specs=[VMEM] * len(args), out_s...  6.77 us
    ppermute x2, waiting for transfers between devices, shards(): biases.append(lax.ppermute(piece, ('row', 'col'), pairs))  3.14 us
    unnamed x27, local copies, waits for them, and re-layouts  2.03 us
    ppermute x2, starting transfers between devices, shards(): biases.append(lax.ppermute(piece, ('row', 'col'), pairs))  1.81 us
  transfers between devices with their start and end apart: 11, of which 7 were waited for; matrix products, arithmetic and copies ran while one was open for 2% of the time, Pallas kernels for 5%

profile of v3, /device:TPU:6, one launch (start us, length us, event | category | flops | bytes accessed | tf_op | source)
XLA Modules:
  0.0 47.4 jit_solution(11660294250185802803)
XLA Ops:
  0.0 0.5 %collective-permute-start.2 = (bf16[576,128]{1,0:T(8,128)(2,1)}, bf16[576,128]{1,0:T(8,128)(2,1)S(1)}, u32[]{:S(2)}, u32[]{:S(2)}) collective-permute-start(bf16[576,128]{1,0:T(8,128)(2,1)} %bitcast.13), channel_id=1, source_target_pairs={{0,8},{4,12},{8,0},{12,4},{1,9},{5,13},{9,1},{13,5},{2,10},{6,14},... | collective-permute-start | bytes 442376 | tf_op jit(solution)/shard_map/ppermute | solution.py:221
  0.6 2.9 %collective-permute-start = (bf16[576,128]{1,0:T(8,128)(2,1)}, bf16[576,128]{1,0:T(8,128)(2,1)S(1)}, u32[]{:S(2)}, u32[]{:S(2)}) collective-permute-start(bf16[576,128]{1,0:T(8,128)(2,1)} %bitcast.15), channel_id=1, source_target_pairs={{0,12},{4,8},{8,4},{12,0},{1,13},{5,9},{9,5},{13,1},{2,14},{6,10},... | collective-permute-start | bytes 442376 | tf_op jit(solution)/shard_map/ppermute | solution.py:221
  3.5 0.7 %copy-done.10 = s32[4,4]{1,0:T(4,128)S(1)} copy-done((s32[4,4]{1,0:T(4,128)S(1)}, s32[4,4]{1,0:T(4,128)}, u32[]{:S(2)}) %copy-start.10) | copy-done | bytes 88
  4.4 0.6 %copy-done.11 = bf16[128,4]{0,1:T(4,128)(2,1)S(1)} copy-done((bf16[128,4]{0,1:T(4,128)(2,1)S(1)}, bf16[128,4]{0,1:T(4,128)(2,1)}, u32[]{:S(2)}) %copy-start.11) | copy-done | bytes 1048
  6.0 0.2 copy-done.2
  6.4 1.1 %shard_map.127 = (f32[576,128]{1,0:T(8,128)S(1)}, f32[576,128]{1,0:T(8,128)S(1)}, bf16[576,128]{1,0:T(8,128)(2,1)S(1)}, f32[1,128]{1,0:T(1,128)S(1)}, bf16[128,1...) custom-call(bf16[576,128]{1,0:T(8,128)(2,1)S(1)} %bitcast.16, ...), custom_call_target="tpu_custom_call" | custom-call | tf_op jit(solution)/shard_map/pallas_call | solution.py:209
  7.5 2.6 %collective-permute-done.refs_0_ = bf16[576,128]{1,0:T(8,128)(2,1)S(1)} collective-permute-done((bf16[576,128]{1,0:T(8,128)(2,1)}, bf16[576,128]{1,0:T(8,128)(2,1)S(1)}, u32[]{:S(2)}, u32[]{:S(2)}) %collective-permute-start) | collective-permute-done | bytes 147488 | tf_op jit(solution)/shard_map/ppermute | solution.py:221
  10.1 0.9 %shard_map.128.early = bf16[576,128]{1,0:T(8,128)(2,1)S(1)} custom-call(f32[96,1,128]{2,1,0:T(1,128)S(1)} %broadcast_in_dim.31.row_mask, f32[96,128]{1,0:T(8,128)S(1)} %broadcast_in_dim.32.column_mask, f32[1,128]{1,0:T(1,128)S(1)} %bitcast.21, bf16[128,512]{1,0:T(8,128)(2,1)S(1)} %copy-done, f32[576,128]{1,0:T(8,128)S(1)} %get-tuple-element.28.left, ...), custom_call_target="tpu_custom_call" | custom-call | tf_op jit(solution)/shard_map/pallas_call | solution.py:209
  11.1 1.8 %shard_map.129 = (bf16[576,128]{1,0:T(8,128)(2,1)S(1)}, bf16[576,128]{1,0:T(8,128)(2,1)S(1)}, bf16[576,128]{1,0:T(8,128)(2,1)S(1)}, bf16[576,128]{1,0:T(8,128)(2,1)S(1)}) custom-call(f32[96,1,128]{2,1,0:T(1,128)S(1)} %broadcast_in_dim.31.row_mask, f32[96,128]{1,0:T(8,128)S(1)} %broadcast_in_dim.32.column_mask, f32[1,128]{1,0:T(1,128)S(1)} %bitcast.22, ...), custom_call_target="tpu_custom_call" | custom-call | tf_op jit(solution)/shard_map/pallas_call | solution.py:209
  12.9 3.7 %collective-permute-start.3 = (bf16[576,128]{1,0:T(8,128)(2,1)S(1)}, bf16[576,128]{1,0:T(8,128)(2,1)S(1)}, u32[]{:S(2)}, u32[]{:S(2)}) collective-permute-start(bf16[576,128]{1,0:T(8,128)(2,1)S(1)} %get-tuple-element.31), channel_id=1, source_target_pairs={{0,3},{1,2},{2,1},{3,0},{4,7},{5,6},{6,5},{7,4},{8,11},{9,10},{10,... | collective-permute-start | bytes 442376 | tf_op jit(solution)/shard_map/ppermute | solution.py:221
  16.6 0.8 %collective-permute-start.5 = (bf16[576,128]{1,0:T(8,128)(2,1)S(1)}, bf16[576,128]{1,0:T(8,128)(2,1)S(1)}, u32[]{:S(2)}, u32[]{:S(2)}) collective-permute-start(bf16[576,128]{1,0:T(8,128)(2,1)S(1)} %get-tuple-element.33), channel_id=1, source_target_pairs={{0,2},{1,3},{2,0},{3,1},{4,6},{5,7},{6,4},{7,5},{8,10},{9,11},{10,... | collective-permute-start | bytes 442376 | tf_op jit(solution)/shard_map/ppermute | solution.py:221
  17.4 4.3 %collective-permute-done.3.refs_1_ = bf16[576,128]{1,0:T(8,128)(2,1)S(1)} collective-permute-done((bf16[576,128]{1,0:T(8,128)(2,1)S(1)}, bf16[576,128]{1,0:T(8,128)(2,1)S(1)}, u32[]{:S(2)}, u32[]{:S(2)}) %collective-permute-start.3) | collective-permute-done | bytes 147488 | tf_op jit(solution)/shard_map/ppermute | solution.py:221
  21.6 1.6 %collective-permute-done.4.refs_2_ = bf16[576,128]{1,0:T(8,128)(2,1)S(1)} collective-permute-done((bf16[576,128]{1,0:T(8,128)(2,1)S(1)}, bf16[576,128]{1,0:T(8,128)(2,1)S(1)}, u32[]{:S(2)}, u32[]{:S(2)}) %collective-permute-start.4) | collective-permute-done | bytes 147488 | tf_op jit(solution)/shard_map/ppermute | solution.py:221
  23.3 4.6 %collective-permute-done.5.refs_3_ = bf16[576,128]{1,0:T(8,128)(2,1)S(1)} collective-permute-done((bf16[576,128]{1,0:T(8,128)(2,1)S(1)}, bf16[576,128]{1,0:T(8,128)(2,1)S(1)}, u32[]{:S(2)}, u32[]{:S(2)}) %collective-permute-start.5) | collective-permute-done | bytes 147488 | tf_op jit(solution)/shard_map/ppermute | solution.py:221
  27.9 0.7 %shard_map.130 = (bf16[576,128]{1,0:T(8,128)(2,1)S(1)}, bf16[576,128]{1,0:T(8,128)(2,1)S(1)}, bf16[1,24,96]{2,1,0:T(8,128)(2,1)S(1)}) custom-call(bf16[576,128]{1,0:T(8,128)(2,1)S(1)} %bitcast.17, f32[576,128]{1,0:T(8,128)S(1)} %get-tuple-element.23.gate, f32[1,128]{1,0:T(1,128)S(1)} %get-tuple-element.24.product_gain, ...), custom_call_target="tpu_custom_call" | custom-call | tf_op jit(solution)/shard_map/pallas_call | solution.py:209
  28.6 3.4 %collective-permute-start.8 = (bf16[576,128]{1,0:T(8,128)(2,1)S(1)}, bf16[576,128]{1,0:T(8,128)(2,1)S(1)}, u32[]{:S(2)}, u32[]{:S(2)}) collective-permute-start(bf16[576,128]{1,0:T(8,128)(2,1)S(1)} %get-tuple-element.39.refs_0_), channel_id=1, source_target_pairs={{0,2},{1,3},{2,0},{3,1},{4,6},{5,7},{6,4},{7,5},{8,10},{9,11},{10,... | collective-permute-start | bytes 442376 | tf_op jit(solution)/shard_map/ppermute | solution.py:221
  32.0 1.0 %collective-permute-start.7 = (bf16[576,128]{1,0:T(8,128)(2,1)S(1)}, bf16[576,128]{1,0:T(8,128)(2,1)S(1)}, u32[]{:S(2)}, u32[]{:S(2)}) collective-permute-start(bf16[576,128]{1,0:T(8,128)(2,1)S(1)} %get-tuple-element.39.refs_0_), channel_id=1, source_target_pairs={{0,3},{1,2},{2,1},{3,0},{4,7},{5,6},{6,5},{7,4},{8,11},{9,10},{10,... | collective-permute-start | bytes 442376 | tf_op jit(solution)/shard_map/ppermute | solution.py:221
  33.0 3.3 %collective-permute-done.6.attend.refs_1_ = bf16[576,128]{1,0:T(8,128)(2,1)S(1)} collective-permute-done((bf16[576,128]{1,0:T(8,128)(2,1)S(1)}, bf16[576,128]{1,0:T(8,128)(2,1)S(1)}, u32[]{:S(2)}, u32[]{:S(2)}) %collective-permute-start.6) | collective-permute-done | bytes 147488 | tf_op jit(solution)/shard_map/ppermute | solution.py:221
  36.3 0.2 shard_map.131
  36.5 0.5 %collective-permute-start.10 = (bf16[48,96]{1,0:T(8,128)(2,1)S(1)}, bf16[48,96]{1,0:T(8,128)(2,1)S(1)}, u32[]{:S(2)}, u32[]{:S(2)}) collective-permute-start(bf16[48,96]{1,0:T(8,128)(2,1)S(1)} %bitcast.18), channel_id=1, source_target_pairs={{0,12},{1,8},{2,4},{3,0},{4,13},{5,9},{6,5},{7,1},{8,14},{9,10},{1... | collective-permute-start | bytes 27656 | tf_op jit(solution)/shard_map/ppermute | solution.py:322
  37.0 1.3 %collective-permute-start.9 = (bf16[48,96]{1,0:T(8,128)(2,1)S(1)}, bf16[48,96]{1,0:T(8,128)(2,1)S(1)}, u32[]{:S(2)}, u32[]{:S(2)}) collective-permute-start(bf16[48,96]{1,0:T(8,128)(2,1)S(1)} %bitcast.19), channel_id=1, source_target_pairs={{0,4},{1,0},{2,12},{3,8},{4,5},{5,1},{6,13},{7,9},{8,6},{9,2},{10,... | collective-permute-start | bytes 27656 | tf_op jit(solution)/shard_map/ppermute | solution.py:322
  38.3 4.0 %collective-permute-done.8.refs_3_ = bf16[576,128]{1,0:T(8,128)(2,1)S(1)} collective-permute-done((bf16[576,128]{1,0:T(8,128)(2,1)S(1)}, bf16[576,128]{1,0:T(8,128)(2,1)S(1)}, u32[]{:S(2)}, u32[]{:S(2)}) %collective-permute-start.8) | collective-permute-done | bytes 147488 | tf_op jit(solution)/shard_map/ppermute | solution.py:221
  42.3 3.1 %collective-permute-done.9.refs_4_ = bf16[48,96]{1,0:T(8,128)(2,1)S(1)} collective-permute-done((bf16[48,96]{1,0:T(8,128)(2,1)S(1)}, bf16[48,96]{1,0:T(8,128)(2,1)S(1)}, u32[]{:S(2)}, u32[]{:S(2)}) %collective-permute-start.9) | collective-permute-done | bytes 9248 | tf_op jit(solution)/shard_map/ppermute | solution.py:322
  45.4 2.0 %shard_map.132 = bf16[576,128]{1,0:T(8,128)(2,1)} custom-call(bf16[576,128]{1,0:T(8,128)(2,1)S(1)} %get-tuple-element.34.middle, f32[96,96]{1,0:T(8,128)S(1)} %get-tuple-element.35.allowed, bf16[128,384]{1,0:T(8,128)(2,1)S(1)} %get-tuple-element.36.w_inputs, bf16[128,128]{1,0:T(8,128)(2,1)S(1)} %get-tuple-element.37.w_gate, ...), custom_call_target="tpu_custom_call" | custom-call | tf_op jit(solution)/shard_map/pallas_call | solution.py:209
  (44 shorter events, 1.5 us)
Async XLA Ops:
  0.0 3.5 %copy-start.12 = (s32[96]{0:T(128)S(1)}, s32[96]{0:T(128)}, u32[]{:S(2)}) copy-start(s32[96]{0:T(128)} %param.14) | copy-start | bytes 1156
  0.0 11.1 %collective-permute-start.2 = (bf16[576,128]{1,0:T(8,128)(2,1)}, bf16[576,128]{1,0:T(8,128)(2,1)S(1)}, u32[]{:S(2)}, u32[]{:S(2)}) collective-permute-start(bf16[576,128]{1,0:T(8,128)(2,1)} %bitcast.13), channel_id=1, source_target_pairs={{0,8},{4,12},{8,0},{12,4},{1,9},{5,13},{9,1},{13,5},{2,10},{6,14},... | collective-permute-start | bytes 442376 | tf_op jit(solution)/shard_map/ppermute | solution.py:221
  0.5 10.6 %collective-permute-start.1 = (bf16[576,128]{1,0:T(8,128)(2,1)}, bf16[576,128]{1,0:T(8,128)(2,1)S(1)}, u32[]{:S(2)}, u32[]{:S(2)}) collective-permute-start(bf16[576,128]{1,0:T(8,128)(2,1)} %bitcast.14), channel_id=1, source_target_pairs={{0,4},{4,0},{8,12},{12,8},{1,5},{5,1},{9,13},{13,9},{2,6},{6,2},{1... | collective-permute-start | bytes 442376 | tf_op jit(solution)/shard_map/ppermute | solution.py:221
  0.6 9.5 %collective-permute-start = (bf16[576,128]{1,0:T(8,128)(2,1)}, bf16[576,128]{1,0:T(8,128)(2,1)S(1)}, u32[]{:S(2)}, u32[]{:S(2)}) collective-permute-start(bf16[576,128]{1,0:T(8,128)(2,1)} %bitcast.15), channel_id=1, source_target_pairs={{0,12},{4,8},{8,4},{12,0},{1,13},{5,9},{9,5},{13,1},{2,14},{6,10},... | collective-permute-start | bytes 442376 | tf_op jit(solution)/shard_map/ppermute | solution.py:221
  3.5 0.7 %copy-start.10 = (s32[4,4]{1,0:T(4,128)S(1)}, s32[4,4]{1,0:T(4,128)}, u32[]{:S(2)}) copy-start(s32[4,4]{1,0:T(4,128)} %param.15) | copy-start | bytes 196
  4.4 0.7 %copy-start.11 = (bf16[128,4]{0,1:T(4,128)(2,1)S(1)}, bf16[128,4]{0,1:T(4,128)(2,1)}, u32[]{:S(2)}) copy-start(bf16[128,4]{0,1:T(4,128)(2,1)} %param.24) | copy-start | bytes 3076
  5.0 0.8 %copy-start.6 = (bf16[128,128]{1,0:T(8,128)(2,1)S(1)}, bf16[128,128]{1,0:T(8,128)(2,1)}, u32[]{:S(2)}) copy-start(bf16[128,128]{1,0:T(8,128)(2,1)} %refs_7_.1) | copy-start | bytes 98308
  5.2 0.8 %copy-start.4 = (bf16[128,128]{1,0:T(8,128)(2,1)S(1)}, bf16[128,128]{1,0:T(8,128)(2,1)}, u32[]{:S(2)}) copy-start(bf16[128,128]{1,0:T(8,128)(2,1)} %refs_1_.1) | copy-start | bytes 98308
  5.2 0.8 %copy-start.5 = (bf16[128,128]{1,0:T(8,128)(2,1)S(1)}, bf16[128,128]{1,0:T(8,128)(2,1)}, u32[]{:S(2)}) copy-start(bf16[128,128]{1,0:T(8,128)(2,1)} %refs_6_.1) | copy-start | bytes 98308
  5.2 0.9 %copy-start.2 = (bf16[128,384]{1,0:T(8,128)(2,1)S(1)}, bf16[128,384]{1,0:T(8,128)(2,1)}, u32[]{:S(2)}) copy-start(bf16[128,384]{1,0:T(8,128)(2,1)} %refs_5_.1) | copy-start | bytes 294916
  5.3 0.9 %copy-start.1 = (bf16[24,24,128]{2,1,0:T(8,128)(2,1)S(1)}, bf16[24,24,128]{2,1,0:T(8,128)(2,1)}, u32[]{:S(2)}) copy-start(bf16[24,24,128]{2,1,0:T(8,128)(2,1)} %param.13) | copy-start | bytes 442372
  5.4 1.0 %copy-start = (bf16[128,512]{1,0:T(8,128)(2,1)S(1)}, bf16[128,512]{1,0:T(8,128)(2,1)}, u32[]{:S(2)}) copy-start(bf16[128,512]{1,0:T(8,128)(2,1)} %w_in.5) | copy-start | bytes 393220
  5.6 0.8 %copy-start.3 = (bf16[128,128]{1,0:T(8,128)(2,1)S(1)}, bf16[128,128]{1,0:T(8,128)(2,1)}, u32[]{:S(2)}) copy-start(bf16[128,128]{1,0:T(8,128)(2,1)} %w_gate.1) | copy-start | bytes 98308
  5.6 0.8 %copy-start.7 = (f32[128]{0:T(128)S(1)}, f32[128]{0:T(128)}, u32[]{:S(2)}) copy-start(f32[128]{0:T(128)} %param.16) | copy-start | bytes 1540
  5.6 0.8 %copy-start.8 = (f32[128]{0:T(128)S(1)}, f32[128]{0:T(128)}, u32[]{:S(2)}) copy-start(f32[128]{0:T(128)} %param.19) | copy-start | bytes 1540
  5.6 0.8 %copy-start.9 = (f32[128]{0:T(128)S(1)}, f32[128]{0:T(128)}, u32[]{:S(2)}) copy-start(f32[128]{0:T(128)} %param.21) | copy-start | bytes 1540
  12.9 8.7 %collective-permute-start.3 = (bf16[576,128]{1,0:T(8,128)(2,1)S(1)}, bf16[576,128]{1,0:T(8,128)(2,1)S(1)}, u32[]{:S(2)}, u32[]{:S(2)}) collective-permute-start(bf16[576,128]{1,0:T(8,128)(2,1)S(1)} %get-tuple-element.31), channel_id=1, source_target_pairs={{0,3},{1,2},{2,1},{3,0},{4,7},{5,6},{6,5},{7,4},{8,11},{9,10},{10,... | collective-permute-start | bytes 442376 | tf_op jit(solution)/shard_map/ppermute | solution.py:221
  16.6 6.7 %collective-permute-start.4 = (bf16[576,128]{1,0:T(8,128)(2,1)S(1)}, bf16[576,128]{1,0:T(8,128)(2,1)S(1)}, u32[]{:S(2)}, u32[]{:S(2)}) collective-permute-start(bf16[576,128]{1,0:T(8,128)(2,1)S(1)} %get-tuple-element.32), channel_id=1, source_target_pairs={{0,1},{1,0},{2,3},{3,2},{4,5},{5,4},{6,7},{7,6},{8,9},{9,8},{10,11... | collective-permute-start | bytes 442376 | tf_op jit(solution)/shard_map/ppermute | solution.py:221
  16.6 11.3 %collective-permute-start.5 = (bf16[576,128]{1,0:T(8,128)(2,1)S(1)}, bf16[576,128]{1,0:T(8,128)(2,1)S(1)}, u32[]{:S(2)}, u32[]{:S(2)}) collective-permute-start(bf16[576,128]{1,0:T(8,128)(2,1)S(1)} %get-tuple-element.33), channel_id=1, source_target_pairs={{0,2},{1,3},{2,0},{3,1},{4,6},{5,7},{6,4},{7,5},{8,10},{9,11},{10,... | collective-permute-start | bytes 442376 | tf_op jit(solution)/shard_map/ppermute | solution.py:221
  28.6 7.7 %collective-permute-start.6 = (bf16[576,128]{1,0:T(8,128)(2,1)S(1)}, bf16[576,128]{1,0:T(8,128)(2,1)S(1)}, u32[]{:S(2)}, u32[]{:S(2)}) collective-permute-start(bf16[576,128]{1,0:T(8,128)(2,1)S(1)} %get-tuple-element.39.refs_0_), channel_id=1, source_target_pairs={{0,1},{1,0},{2,3},{3,2},{4,5},{5,4},{6,7},{7,6},{8,9},{9,8},{10,11... | collective-permute-start | bytes 442376 | tf_op jit(solution)/shard_map/ppermute | solution.py:221
  28.6 13.6 %collective-permute-start.8 = (bf16[576,128]{1,0:T(8,128)(2,1)S(1)}, bf16[576,128]{1,0:T(8,128)(2,1)S(1)}, u32[]{:S(2)}, u32[]{:S(2)}) collective-permute-start(bf16[576,128]{1,0:T(8,128)(2,1)S(1)} %get-tuple-element.39.refs_0_), channel_id=1, source_target_pairs={{0,2},{1,3},{2,0},{3,1},{4,6},{5,7},{6,4},{7,5},{8,10},{9,11},{10,... | collective-permute-start | bytes 442376 | tf_op jit(solution)/shard_map/ppermute | solution.py:221
  32.0 10.3 %collective-permute-start.7 = (bf16[576,128]{1,0:T(8,128)(2,1)S(1)}, bf16[576,128]{1,0:T(8,128)(2,1)S(1)}, u32[]{:S(2)}, u32[]{:S(2)}) collective-permute-start(bf16[576,128]{1,0:T(8,128)(2,1)S(1)} %get-tuple-element.39.refs_0_), channel_id=1, source_target_pairs={{0,3},{1,2},{2,1},{3,0},{4,7},{5,6},{6,5},{7,4},{8,11},{9,10},{10,... | collective-permute-start | bytes 442376 | tf_op jit(solution)/shard_map/ppermute | solution.py:221
  36.5 5.8 %collective-permute-start.10 = (bf16[48,96]{1,0:T(8,128)(2,1)S(1)}, bf16[48,96]{1,0:T(8,128)(2,1)S(1)}, u32[]{:S(2)}, u32[]{:S(2)}) collective-permute-start(bf16[48,96]{1,0:T(8,128)(2,1)S(1)} %bitcast.18), channel_id=1, source_target_pairs={{0,12},{1,8},{2,4},{3,0},{4,13},{5,9},{6,5},{7,1},{8,14},{9,10},{1... | collective-permute-start | bytes 27656 | tf_op jit(solution)/shard_map/ppermute | solution.py:322
  37.0 8.4 %collective-permute-start.9 = (bf16[48,96]{1,0:T(8,128)(2,1)S(1)}, bf16[48,96]{1,0:T(8,128)(2,1)S(1)}, u32[]{:S(2)}, u32[]{:S(2)}) collective-permute-start(bf16[48,96]{1,0:T(8,128)(2,1)S(1)} %bitcast.19), channel_id=1, source_target_pairs={{0,4},{1,0},{2,12},{3,8},{4,5},{5,1},{6,13},{7,9},{8,6},{9,2},{10,... | collective-permute-start | bytes 27656 | tf_op jit(solution)/shard_map/ppermute | solution.py:322

commit v4 on v3

--- a/solution.py
+++ b/solution.py
@@ -10,7 +10,6 @@
 
 norm_epsilon = 1e-05
 VMEM = pl.BlockSpec(memory_space=pltpu.VMEM)
-PARAMS = pltpu.CompilerParams(vmem_limit_bytes=48 * 1024 * 1024)
 
 
 def layer_norm(inputs, gain):
@@ -84,8 +83,9 @@
             multiply(rows, columns, left, right, part * columns * columns, part_out, (at * split + part) * size)
 
 
-def late_kernel(rows, columns, steps, column_devices, row_mask, column_mask, gain, w_in, left, own, early, *refs):
+def late_kernel(rows, columns, steps, column_devices, *refs):
     states, refs = refs[: len(steps)], refs[len(steps) :]
+    row_mask, column_mask, gain, w_in, left, own, early, *refs = refs
     outs, late, right = refs[:column_devices], refs[column_devices], refs[column_devices + 1]
     size = rows * columns
     split = rows // columns
@@ -206,13 +206,15 @@
 
 
 def call(kernel, outs, args, scratch=()):
+    arrays = jax.tree.leaves(outs) + list(args) + list(scratch)
+    held = sum(math.prod(array.shape) * jnp.dtype(array.dtype).itemsize for array in arrays)
     return pl.pallas_call(
         kernel,
         out_shape=outs,
         in_specs=[VMEM] * len(args),
         out_specs=jax.tree.map(lambda _: VMEM, outs),
         scratch_shapes=scratch,
-        compiler_params=PARAMS,
+        compiler_params=pltpu.CompilerParams(vmem_limit_bytes=min(56, 12 + 2 * held // 2**20) * 2**20),
     )(*args)
 
 
@@ -291,7 +293,7 @@
     parts = call(
         functools.partial(late_kernel, rows, columns, late_steps, column_devices),
         [tile] * column_devices,
-        common + [own, early] + [others[step - 1] for step in late_steps],
+        [others[step - 1] for step in late_steps] + common + [own, early],
         [pltpu.VMEM((len(late_steps) * split * size, channels), jnp.bfloat16), flat],
     )
     order = list(range(column_devices - 1, 2, -1)) + [1, 2]

time: 47.6 us -> 47.4 us (level)
  the two profiles are of different devices: /device:TPU:6 before, /device:TPU:0 now
where the time goes in v4:
time: 47.4 us; the launch traced here: 46.5 us
  waiting for transfers between devices  21.7 us (46%)
  starting transfers between devices  15 us (32%)
  Pallas kernels  6.77 us (14%)
  local copies, waits for them, and re-layouts  2.69 us (6%)
    ppermute x9, waiting for transfers between devices, exchange(): return lax.ppermute(value, axis, [(at, at ^ step) for at in range(size)])  21.7 us
    ppermute x9, starting transfers between devices, exchange(): return lax.ppermute(value, axis, [(at, at ^ step) for at in range(size)])  13.4 us
    pallas_call x6, Pallas kernels, call(): pl.pallas_call(kernel, out_shape=outs, in_specs=[VMEM] * len(args), out_s...  6.77 us
    unnamed x27, local copies, waits for them, and re-layouts  2.03 us
    ppermute x2, starting transfers between devices, shards(): biases.append(lax.ppermute(piece, ('row', 'col'), pairs))  1.66 us
  transfers between devices with their start and end apart: 11, of which 7 were waited for; matrix products, arithmetic and copies ran while one was open for 2% of the time, Pallas kernels for 5%

profile of v4, /device:TPU:0, one launch (start us, length us, event | category | flops | bytes accessed | tf_op | source)
XLA Modules:
  0.0 46.5 jit_solution(816296444463732089)
XLA Ops:
  0.0 3.9 %collective-permute-start.2 = (bf16[576,128]{1,0:T(8,128)(2,1)}, bf16[576,128]{1,0:T(8,128)(2,1)S(1)}, u32[]{:S(2)}, u32[]{:S(2)}) collective-permute-start(bf16[576,128]{1,0:T(8,128)(2,1)} %bitcast.13), channel_id=1, source_target_pairs={{0,12},{4,8},{8,4},{12,0},{1,13},{5,9},{9,5},{13,1},{2,14},{6,10},... | collective-permute-start | bytes 442376 | tf_op jit(solution)/shard_map/ppermute | solution.py:223
  3.9 0.5 %collective-permute-start.1 = (bf16[576,128]{1,0:T(8,128)(2,1)}, bf16[576,128]{1,0:T(8,128)(2,1)S(1)}, u32[]{:S(2)}, u32[]{:S(2)}) collective-permute-start(bf16[576,128]{1,0:T(8,128)(2,1)} %bitcast.14), channel_id=1, source_target_pairs={{0,8},{4,12},{8,0},{12,4},{1,9},{5,13},{9,1},{13,5},{2,10},{6,14},... | collective-permute-start | bytes 442376 | tf_op jit(solution)/shard_map/ppermute | solution.py:223
  4.6 0.7 %copy-done.10 = s32[4,4]{1,0:T(4,128)S(1)} copy-done((s32[4,4]{1,0:T(4,128)S(1)}, s32[4,4]{1,0:T(4,128)}, u32[]{:S(2)}) %copy-start.10) | copy-done | bytes 88
  5.5 0.6 %copy-done.11 = bf16[128,4]{0,1:T(4,128)(2,1)S(1)} copy-done((bf16[128,4]{0,1:T(4,128)(2,1)S(1)}, bf16[128,4]{0,1:T(4,128)(2,1)}, u32[]{:S(2)}) %copy-start.11) | copy-done | bytes 1048
  7.0 0.2 copy-done.2
  7.4 1.1 %shard_map.127 = (f32[576,128]{1,0:T(8,128)S(1)}, f32[576,128]{1,0:T(8,128)S(1)}, bf16[576,128]{1,0:T(8,128)(2,1)S(1)}, f32[1,128]{1,0:T(1,128)S(1)}, bf16[128,1...) custom-call(bf16[576,128]{1,0:T(8,128)(2,1)S(1)} %bitcast.16, ...), custom_call_target="tpu_custom_call" | custom-call | tf_op jit(solution)/shard_map/pallas_call | solution.py:211
  8.6 1.0 %shard_map.128.refs_8_ = bf16[576,128]{1,0:T(8,128)(2,1)S(1)} custom-call(f32[96,1,128]{2,1,0:T(1,128)S(1)} %broadcast_in_dim.31.row_mask.refs_2_, f32[96,128]{1,0:T(8,128)S(1)} %broadcast_in_dim.32.column_mask.refs_3_, f32[1,128]{1,0:T(1,128)S(1)} %bitcast.21, bf16[128,512]{1,0:T(8,128)(2,1)S(1)} %copy-done, f32[576,128]{1,0:T(8,128)S(1)} %get-tuple-element.28.left.refs_6_, ...), custom_call_target="tpu_custom_call" | custom-call | tf_op jit(solution)/shard_map/pallas_call | solution.py:211
  9.5 1.6 %collective-permute-done.1.refs_1_ = bf16[576,128]{1,0:T(8,128)(2,1)S(1)} collective-permute-done((bf16[576,128]{1,0:T(8,128)(2,1)}, bf16[576,128]{1,0:T(8,128)(2,1)S(1)}, u32[]{:S(2)}, u32[]{:S(2)}) %collective-permute-start.1) | collective-permute-done | bytes 147488 | tf_op jit(solution)/shard_map/ppermute | solution.py:223
  11.1 0.3 collective-permute-done.refs_0_
  11.4 1.8 %shard_map.129 = (bf16[576,128]{1,0:T(8,128)(2,1)S(1)}, bf16[576,128]{1,0:T(8,128)(2,1)S(1)}, bf16[576,128]{1,0:T(8,128)(2,1)S(1)}, bf16[576,128]{1,0:T(8,128)(2,1)S(1)}) custom-call(bf16[576,128]{1,0:T(8,128)(2,1)S(1)} %collective-permute-done.refs_0_, bf16[576,128]{1,0:T(8,128)(2,1)S(1)} %collective-permute-done.1.refs_1_, ...), custom_call_target="tpu_custom_call" | custom-call | tf_op jit(solution)/shard_map/pallas_call | solution.py:211
  13.2 3.7 %collective-permute-start.3 = (bf16[576,128]{1,0:T(8,128)(2,1)S(1)}, bf16[576,128]{1,0:T(8,128)(2,1)S(1)}, u32[]{:S(2)}, u32[]{:S(2)}) collective-permute-start(bf16[576,128]{1,0:T(8,128)(2,1)S(1)} %get-tuple-element.31), channel_id=1, source_target_pairs={{0,3},{1,2},{2,1},{3,0},{4,7},{5,6},{6,5},{7,4},{8,11},{9,10},{10,... | collective-permute-start | bytes 442376 | tf_op jit(solution)/shard_map/ppermute | solution.py:223
  16.8 0.8 %collective-permute-start.5 = (bf16[576,128]{1,0:T(8,128)(2,1)S(1)}, bf16[576,128]{1,0:T(8,128)(2,1)S(1)}, u32[]{:S(2)}, u32[]{:S(2)}) collective-permute-start(bf16[576,128]{1,0:T(8,128)(2,1)S(1)} %get-tuple-element.33), channel_id=1, source_target_pairs={{0,2},{1,3},{2,0},{3,1},{4,6},{5,7},{6,4},{7,5},{8,10},{9,11},{10,... | collective-permute-start | bytes 442376 | tf_op jit(solution)/shard_map/ppermute | solution.py:223
  17.6 4.2 %collective-permute-done.3.refs_1_ = bf16[576,128]{1,0:T(8,128)(2,1)S(1)} collective-permute-done((bf16[576,128]{1,0:T(8,128)(2,1)S(1)}, bf16[576,128]{1,0:T(8,128)(2,1)S(1)}, u32[]{:S(2)}, u32[]{:S(2)}) %collective-permute-start.3) | collective-permute-done | bytes 147488 | tf_op jit(solution)/shard_map/ppermute | solution.py:223
  21.8 3.2 %collective-permute-done.4.refs_2_ = bf16[576,128]{1,0:T(8,128)(2,1)S(1)} collective-permute-done((bf16[576,128]{1,0:T(8,128)(2,1)S(1)}, bf16[576,128]{1,0:T(8,128)(2,1)S(1)}, u32[]{:S(2)}, u32[]{:S(2)}) %collective-permute-start.4) | collective-permute-done | bytes 147488 | tf_op jit(solution)/shard_map/ppermute | solution.py:223
  25.0 4.4 %collective-permute-done.5.refs_3_ = bf16[576,128]{1,0:T(8,128)(2,1)S(1)} collective-permute-done((bf16[576,128]{1,0:T(8,128)(2,1)S(1)}, bf16[576,128]{1,0:T(8,128)(2,1)S(1)}, u32[]{:S(2)}, u32[]{:S(2)}) %collective-permute-start.5) | collective-permute-done | bytes 147488 | tf_op jit(solution)/shard_map/ppermute | solution.py:223
  29.4 0.7 %shard_map.130 = (bf16[576,128]{1,0:T(8,128)(2,1)S(1)}, bf16[576,128]{1,0:T(8,128)(2,1)S(1)}, bf16[1,24,96]{2,1,0:T(8,128)(2,1)S(1)}) custom-call(bf16[576,128]{1,0:T(8,128)(2,1)S(1)} %bitcast.17, f32[576,128]{1,0:T(8,128)S(1)} %get-tuple-element.23.gate, f32[1,128]{1,0:T(1,128)S(1)} %get-tuple-element.24.product_gain, ...), custom_call_target="tpu_custom_call" | custom-call | tf_op jit(solution)/shard_map/pallas_call | solution.py:211
  30.2 3.0 %collective-permute-start.8 = (bf16[576,128]{1,0:T(8,128)(2,1)S(1)}, bf16[576,128]{1,0:T(8,128)(2,1)S(1)}, u32[]{:S(2)}, u32[]{:S(2)}) collective-permute-start(bf16[576,128]{1,0:T(8,128)(2,1)S(1)} %get-tuple-element.39.refs_0_), channel_id=1, source_target_pairs={{0,2},{1,3},{2,0},{3,1},{4,6},{5,7},{6,4},{7,5},{8,10},{9,11},{10,... | collective-permute-start | bytes 442376 | tf_op jit(solution)/shard_map/ppermute | solution.py:223
  33.2 1.3 %collective-permute-start.7 = (bf16[576,128]{1,0:T(8,128)(2,1)S(1)}, bf16[576,128]{1,0:T(8,128)(2,1)S(1)}, u32[]{:S(2)}, u32[]{:S(2)}) collective-permute-start(bf16[576,128]{1,0:T(8,128)(2,1)S(1)} %get-tuple-element.39.refs_0_), channel_id=1, source_target_pairs={{0,3},{1,2},{2,1},{3,0},{4,7},{5,6},{6,5},{7,4},{8,11},{9,10},{10,... | collective-permute-start | bytes 442376 | tf_op jit(solution)/shard_map/ppermute | solution.py:223
  34.6 2.8 %collective-permute-done.6.attend.refs_1_ = bf16[576,128]{1,0:T(8,128)(2,1)S(1)} collective-permute-done((bf16[576,128]{1,0:T(8,128)(2,1)S(1)}, bf16[576,128]{1,0:T(8,128)(2,1)S(1)}, u32[]{:S(2)}, u32[]{:S(2)}) %collective-permute-start.6) | collective-permute-done | bytes 147488 | tf_op jit(solution)/shard_map/ppermute | solution.py:223
  37.4 0.2 shard_map.131
  37.5 1.3 %collective-permute-start.10 = (bf16[48,96]{1,0:T(8,128)(2,1)S(1)}, bf16[48,96]{1,0:T(8,128)(2,1)S(1)}, u32[]{:S(2)}, u32[]{:S(2)}) collective-permute-start(bf16[48,96]{1,0:T(8,128)(2,1)S(1)} %bitcast.18), channel_id=1, source_target_pairs={{0,12},{1,8},{2,4},{3,0},{4,13},{5,9},{6,5},{7,1},{8,14},{9,10},{1... | collective-permute-start | bytes 27656 | tf_op jit(solution)/shard_map/ppermute | solution.py:324
  38.9 0.4 collective-permute-start.9
  39.2 5.3 %collective-permute-done.8.refs_3_ = bf16[576,128]{1,0:T(8,128)(2,1)S(1)} collective-permute-done((bf16[576,128]{1,0:T(8,128)(2,1)S(1)}, bf16[576,128]{1,0:T(8,128)(2,1)S(1)}, u32[]{:S(2)}, u32[]{:S(2)}) %collective-permute-start.8) | collective-permute-done | bytes 147488 | tf_op jit(solution)/shard_map/ppermute | solution.py:223
  44.5 2.0 %shard_map.132 = bf16[576,128]{1,0:T(8,128)(2,1)} custom-call(bf16[576,128]{1,0:T(8,128)(2,1)S(1)} %get-tuple-element.34.middle, f32[96,96]{1,0:T(8,128)S(1)} %get-tuple-element.35.allowed, bf16[128,384]{1,0:T(8,128)(2,1)S(1)} %get-tuple-element.36.w_inputs, bf16[128,128]{1,0:T(8,128)(2,1)S(1)} %get-tuple-element.37.w_gate, ...), custom_call_target="tpu_custom_call" | custom-call | tf_op jit(solution)/shard_map/pallas_call | solution.py:211
  (44 shorter events, 1.5 us)
Async XLA Ops:
  0.0 4.5 %copy-start.12 = (s32[96]{0:T(128)S(1)}, s32[96]{0:T(128)}, u32[]{:S(2)}) copy-start(s32[96]{0:T(128)} %param.14) | copy-start | bytes 1156
  0.0 8.6 %collective-permute-start.2 = (bf16[576,128]{1,0:T(8,128)(2,1)}, bf16[576,128]{1,0:T(8,128)(2,1)S(1)}, u32[]{:S(2)}, u32[]{:S(2)}) collective-permute-start(bf16[576,128]{1,0:T(8,128)(2,1)} %bitcast.13), channel_id=1, source_target_pairs={{0,12},{4,8},{8,4},{12,0},{1,13},{5,9},{9,5},{13,1},{2,14},{6,10},... | collective-permute-start | bytes 442376 | tf_op jit(solution)/shard_map/ppermute | solution.py:223
  3.9 7.2 %collective-permute-start.1 = (bf16[576,128]{1,0:T(8,128)(2,1)}, bf16[576,128]{1,0:T(8,128)(2,1)S(1)}, u32[]{:S(2)}, u32[]{:S(2)}) collective-permute-start(bf16[576,128]{1,0:T(8,128)(2,1)} %bitcast.14), channel_id=1, source_target_pairs={{0,8},{4,12},{8,0},{12,4},{1,9},{5,13},{9,1},{13,5},{2,10},{6,14},... | collective-permute-start | bytes 442376 | tf_op jit(solution)/shard_map/ppermute | solution.py:223
  4.4 7.0 %collective-permute-start = (bf16[576,128]{1,0:T(8,128)(2,1)}, bf16[576,128]{1,0:T(8,128)(2,1)S(1)}, u32[]{:S(2)}, u32[]{:S(2)}) collective-permute-start(bf16[576,128]{1,0:T(8,128)(2,1)} %bitcast.15), channel_id=1, source_target_pairs={{0,4},{4,0},{8,12},{12,8},{1,5},{5,1},{9,13},{13,9},{2,6},{6,2},{1... | collective-permute-start | bytes 442376 | tf_op jit(solution)/shard_map/ppermute | solution.py:223
  4.5 0.7 %copy-start.10 = (s32[4,4]{1,0:T(4,128)S(1)}, s32[4,4]{1,0:T(4,128)}, u32[]{:S(2)}) copy-start(s32[4,4]{1,0:T(4,128)} %param.15) | copy-start | bytes 196
  5.4 0.7 %copy-start.11 = (bf16[128,4]{0,1:T(4,128)(2,1)S(1)}, bf16[128,4]{0,1:T(4,128)(2,1)}, u32[]{:S(2)}) copy-start(bf16[128,4]{0,1:T(4,128)(2,1)} %param.24) | copy-start | bytes 3076
  6.1 0.8 %copy-start.6 = (bf16[128,128]{1,0:T(8,128)(2,1)S(1)}, bf16[128,128]{1,0:T(8,128)(2,1)}, u32[]{:S(2)}) copy-start(bf16[128,128]{1,0:T(8,128)(2,1)} %refs_7_.1) | copy-start | bytes 98308
  6.2 0.8 %copy-start.4 = (bf16[128,128]{1,0:T(8,128)(2,1)S(1)}, bf16[128,128]{1,0:T(8,128)(2,1)}, u32[]{:S(2)}) copy-start(bf16[128,128]{1,0:T(8,128)(2,1)} %refs_1_.1) | copy-start | bytes 98308
  6.2 0.8 %copy-start.5 = (bf16[128,128]{1,0:T(8,128)(2,1)S(1)}, bf16[128,128]{1,0:T(8,128)(2,1)}, u32[]{:S(2)}) copy-start(bf16[128,128]{1,0:T(8,128)(2,1)} %refs_6_.1) | copy-start | bytes 98308
  6.2 0.9 %copy-start.2 = (bf16[128,384]{1,0:T(8,128)(2,1)S(1)}, bf16[128,384]{1,0:T(8,128)(2,1)}, u32[]{:S(2)}) copy-start(bf16[128,384]{1,0:T(8,128)(2,1)} %refs_5_.2) | copy-start | bytes 294916
  6.4 0.9 %copy-start.1 = (bf16[24,24,128]{2,1,0:T(8,128)(2,1)S(1)}, bf16[24,24,128]{2,1,0:T(8,128)(2,1)}, u32[]{:S(2)}) copy-start(bf16[24,24,128]{2,1,0:T(8,128)(2,1)} %param.13) | copy-start | bytes 442372
  6.4 1.0 %copy-start = (bf16[128,512]{1,0:T(8,128)(2,1)S(1)}, bf16[128,512]{1,0:T(8,128)(2,1)}, u32[]{:S(2)}) copy-start(bf16[128,512]{1,0:T(8,128)(2,1)} %refs_5_.3) | copy-start | bytes 393220
  6.6 0.8 %copy-start.3 = (bf16[128,128]{1,0:T(8,128)(2,1)S(1)}, bf16[128,128]{1,0:T(8,128)(2,1)}, u32[]{:S(2)}) copy-start(bf16[128,128]{1,0:T(8,128)(2,1)} %w_gate.1) | copy-start | bytes 98308
  6.6 0.8 %copy-start.7 = (f32[128]{0:T(128)S(1)}, f32[128]{0:T(128)}, u32[]{:S(2)}) copy-start(f32[128]{0:T(128)} %param.16) | copy-start | bytes 1540
  6.6 0.8 %copy-start.8 = (f32[128]{0:T(128)S(1)}, f32[128]{0:T(128)}, u32[]{:S(2)}) copy-start(f32[128]{0:T(128)} %param.19) | copy-start | bytes 1540
  6.6 0.8 %copy-start.9 = (f32[128]{0:T(128)S(1)}, f32[128]{0:T(128)}, u32[]{:S(2)}) copy-start(f32[128]{0:T(128)} %param.21) | copy-start | bytes 1540
  13.2 8.6 %collective-permute-start.3 = (bf16[576,128]{1,0:T(8,128)(2,1)S(1)}, bf16[576,128]{1,0:T(8,128)(2,1)S(1)}, u32[]{:S(2)}, u32[]{:S(2)}) collective-permute-start(bf16[576,128]{1,0:T(8,128)(2,1)S(1)} %get-tuple-element.31), channel_id=1, source_target_pairs={{0,3},{1,2},{2,1},{3,0},{4,7},{5,6},{6,5},{7,4},{8,11},{9,10},{10,... | collective-permute-start | bytes 442376 | tf_op jit(solution)/shard_map/ppermute | solution.py:223
  16.8 8.1 %collective-permute-start.4 = (bf16[576,128]{1,0:T(8,128)(2,1)S(1)}, bf16[576,128]{1,0:T(8,128)(2,1)S(1)}, u32[]{:S(2)}, u32[]{:S(2)}) collective-permute-start(bf16[576,128]{1,0:T(8,128)(2,1)S(1)} %get-tuple-element.32), channel_id=1, source_target_pairs={{0,1},{1,0},{2,3},{3,2},{4,5},{5,4},{6,7},{7,6},{8,9},{9,8},{10,11... | collective-permute-start | bytes 442376 | tf_op jit(solution)/shard_map/ppermute | solution.py:223
  16.8 12.6 %collective-permute-start.5 = (bf16[576,128]{1,0:T(8,128)(2,1)S(1)}, bf16[576,128]{1,0:T(8,128)(2,1)S(1)}, u32[]{:S(2)}, u32[]{:S(2)}) collective-permute-start(bf16[576,128]{1,0:T(8,128)(2,1)S(1)} %get-tuple-element.33), channel_id=1, source_target_pairs={{0,2},{1,3},{2,0},{3,1},{4,6},{5,7},{6,4},{7,5},{8,10},{9,11},{10,... | collective-permute-start | bytes 442376 | tf_op jit(solution)/shard_map/ppermute | solution.py:223
  30.1 7.2 %collective-permute-start.6 = (bf16[576,128]{1,0:T(8,128)(2,1)S(1)}, bf16[576,128]{1,0:T(8,128)(2,1)S(1)}, u32[]{:S(2)}, u32[]{:S(2)}) collective-permute-start(bf16[576,128]{1,0:T(8,128)(2,1)S(1)} %get-tuple-element.39.refs_0_), channel_id=1, source_target_pairs={{0,1},{1,0},{2,3},{3,2},{4,5},{5,4},{6,7},{7,6},{8,9},{9,8},{10,11... | collective-permute-start | bytes 442376 | tf_op jit(solution)/shard_map/ppermute | solution.py:223
  30.2 14.3 %collective-permute-start.8 = (bf16[576,128]{1,0:T(8,128)(2,1)S(1)}, bf16[576,128]{1,0:T(8,128)(2,1)S(1)}, u32[]{:S(2)}, u32[]{:S(2)}) collective-permute-start(bf16[576,128]{1,0:T(8,128)(2,1)S(1)} %get-tuple-element.39.refs_0_), channel_id=1, source_target_pairs={{0,2},{1,3},{2,0},{3,1},{4,6},{5,7},{6,4},{7,5},{8,10},{9,11},{10,... | collective-permute-start | bytes 442376 | tf_op jit(solution)/shard_map/ppermute | solution.py:223
  33.2 11.3 %collective-permute-start.7 = (bf16[576,128]{1,0:T(8,128)(2,1)S(1)}, bf16[576,128]{1,0:T(8,128)(2,1)S(1)}, u32[]{:S(2)}, u32[]{:S(2)}) collective-permute-start(bf16[576,128]{1,0:T(8,128)(2,1)S(1)} %get-tuple-element.39.refs_0_), channel_id=1, source_target_pairs={{0,3},{1,2},{2,1},{3,0},{4,7},{5,6},{6,5},{7,4},{8,11},{9,10},{10,... | collective-permute-start | bytes 442376 | tf_op jit(solution)/shard_map/ppermute | solution.py:223
  37.5 6.9 %collective-permute-start.10 = (bf16[48,96]{1,0:T(8,128)(2,1)S(1)}, bf16[48,96]{1,0:T(8,128)(2,1)S(1)}, u32[]{:S(2)}, u32[]{:S(2)}) collective-permute-start(bf16[48,96]{1,0:T(8,128)(2,1)S(1)} %bitcast.18), channel_id=1, source_target_pairs={{0,12},{1,8},{2,4},{3,0},{4,13},{5,9},{6,5},{7,1},{8,14},{9,10},{1... | collective-permute-start | bytes 27656 | tf_op jit(solution)/shard_map/ppermute | solution.py:324
  38.9 5.6 %collective-permute-start.9 = (bf16[48,96]{1,0:T(8,128)(2,1)S(1)}, bf16[48,96]{1,0:T(8,128)(2,1)S(1)}, u32[]{:S(2)}, u32[]{:S(2)}) collective-permute-start(bf16[48,96]{1,0:T(8,128)(2,1)S(1)} %bitcast.19), channel_id=1, source_target_pairs={{0,4},{1,0},{2,12},{3,8},{4,5},{5,1},{6,13},{7,9},{8,6},{9,2},{10,... | collective-permute-start | bytes 27656 | tf_op jit(solution)/shard_map/ppermute | solution.py:324

commit v5 on v4

--- a/solution.py
+++ b/solution.py
@@ -83,9 +83,10 @@
             multiply(rows, columns, left, right, part * columns * columns, part_out, (at * split + part) * size)
 
 
-def late_kernel(rows, columns, steps, column_devices, *refs):
+def late_kernel(rows, columns, steps, column_devices, early_groups, *refs):
     states, refs = refs[: len(steps)], refs[len(steps) :]
-    row_mask, column_mask, gain, w_in, left, own, early, *refs = refs
+    row_mask, column_mask, gain, w_in, left, own, *refs = refs
+    early, refs = refs[: len(early_groups)], refs[len(early_groups) :]
     outs, late, right = refs[:column_devices], refs[column_devices], refs[column_devices + 1]
     size = rows * columns
     split = rows // columns
@@ -101,8 +102,9 @@
                 out[...] = source[pl.ds(pl.multiple_of((place - first) * size, 16), size), :]
 
         fill(own, 0, split)
-        fill(late, split, (steps[-1] + 1) * split)
-        fill(early, (steps[-1] + 1) * split, (steps[-1] + 1) * split + early.shape[0] // size)
+        for group, source in zip(early_groups, early):
+            fill(source, group[0] * split, (group[-1] + 1) * split)
+        fill(late, steps[0] * split, (steps[-1] + 1) * split)
 
 
 def middle_kernel(rows, columns, split, state, gate, product_gain, w_out, attend_gain, w_bias, *refs):
@@ -281,19 +283,23 @@
         [flat],
     )
     w_product, w_middle, w_attend, w_bias, allowed, w_inputs, w_gate, w_out = weights
-    early_steps = list(range(row_devices - row_devices // 4, row_devices))
-    late_steps = list(range(1, early_steps[0]))
+    late_steps = list(range(row_devices - row_devices // 4, row_devices))
+    early_steps = list(range(1, late_steps[0]))
     common = [row_mask, column_mask, norm_in, triangle_input, left]
-    early = call(
-        functools.partial(early_kernel, rows, columns, early_steps),
-        jax.ShapeDtypeStruct((len(early_steps) * split * size, channels), jnp.bfloat16),
-        common + [others[step - 1] for step in early_steps],
-        [flat],
-    )
+    early_groups = [[step] for step in early_steps[::-1]]
+    early = [
+        call(
+            functools.partial(early_kernel, rows, columns, group),
+            jax.ShapeDtypeStruct((len(group) * split * size, channels), jnp.bfloat16),
+            common + [others[step - 1] for step in group],
+            [flat],
+        )
+        for group in early_groups
+    ]
     parts = call(
-        functools.partial(late_kernel, rows, columns, late_steps, column_devices),
+        functools.partial(late_kernel, rows, columns, late_steps, column_devices, early_groups),
         [tile] * column_devices,
-        [others[step - 1] for step in late_steps] + common + [own, early],
+        [others[step - 1] for step in late_steps] + common + [own] + early,
         [pltpu.VMEM((len(late_steps) * split * size, channels), jnp.bfloat16), flat],
     )
     order = list(range(column_devices - 1, 2, -1)) + [1, 2]

time: 47.4 us -> 45.3 us (0.956)
  waiting for transfers between devices: 21.7 us -> 19.4 us
    ppermute x9, waiting for transfers between devices: 21.7 us -> 19.1 us  [exchange(): return lax.ppermute(value, axis, [(at, at ^ step) for at in range(size)])]
    pallas_call x6 -> x7, Pallas kernels: 6.77 us -> 7.03 us  [call(): pl.pallas_call(kernel, out_shape=outs, in_specs=[VMEM] * len(args), out_s...]
  transfers between devices with their start and end apart: 11 -> 11, of which waited for: 7 -> 7; matrix products, arithmetic and copies ran while one was open for 2% -> 2% of each run, Pallas kernels for 5% -> 7%
where the time goes in v5:
time: 45.3 us; the launch traced here: 44.5 us
  waiting for transfers between devices  19.4 us (43%)
  starting transfers between devices  15 us (33%)
  Pallas kernels  7.03 us (16%)
  local copies, waits for them, and re-layouts  2.69 us (6%)
    ppermute x9, waiting for transfers between devices, exchange(): return lax.ppermute(value, axis, [(at, at ^ step) for at in range(size)])  19.1 us
    ppermute x9, starting transfers between devices, exchange(): return lax.ppermute(value, axis, [(at, at ^ step) for at in range(size)])  13.3 us
    pallas_call x7, Pallas kernels, call(): pl.pallas_call(kernel, out_shape=outs, in_specs=[VMEM] * len(args), out_s...  7.03 us
    unnamed x27, local copies, waits for them, and re-layouts  2.03 us
    ppermute x2, starting transfers between devices, shards(): biases.append(lax.ppermute(piece, ('row', 'col'), pairs))  1.67 us
  transfers between devices with their start and end apart: 11, of which 7 were waited for; matrix products, arithmetic and copies ran while one was open for 2% of the time, Pallas kernels for 7%

profile of v5, /device:TPU:0, one launch (start us, length us, event | category | flops | bytes accessed | tf_op | source)
XLA Modules:
  0.0 44.5 jit_solution(11605911875541237796)
XLA Ops:
  0.0 2.9 %collective-permute-start.2 = (bf16[576,128]{1,0:T(8,128)(2,1)}, bf16[576,128]{1,0:T(8,128)(2,1)S(1)}, u32[]{:S(2)}, u32[]{:S(2)}) collective-permute-start(bf16[576,128]{1,0:T(8,128)(2,1)} %bitcast.13), channel_id=1, source_target_pairs={{0,4},{4,0},{8,12},{12,8},{1,5},{5,1},{9,13},{13,9},{2,6},{6,2},{1... | collective-permute-start | bytes 442376 | tf_op jit(solution)/shard_map/ppermute | solution.py:225
  2.9 1.5 %collective-permute-start.1 = (bf16[576,128]{1,0:T(8,128)(2,1)}, bf16[576,128]{1,0:T(8,128)(2,1)S(1)}, u32[]{:S(2)}, u32[]{:S(2)}) collective-permute-start(bf16[576,128]{1,0:T(8,128)(2,1)} %bitcast.14), channel_id=1, source_target_pairs={{0,8},{4,12},{8,0},{12,4},{1,9},{5,13},{9,1},{13,5},{2,10},{6,14},... | collective-permute-start | bytes 442376 | tf_op jit(solution)/shard_map/ppermute | solution.py:225
  4.5 0.7 %copy-done.10 = s32[4,4]{1,0:T(4,128)S(1)} copy-done((s32[4,4]{1,0:T(4,128)S(1)}, s32[4,4]{1,0:T(4,128)}, u32[]{:S(2)}) %copy-start.10) | copy-done | bytes 88
  5.4 0.6 %copy-done.11 = bf16[128,4]{0,1:T(4,128)(2,1)S(1)} copy-done((bf16[128,4]{0,1:T(4,128)(2,1)S(1)}, bf16[128,4]{0,1:T(4,128)(2,1)}, u32[]{:S(2)}) %copy-start.11) | copy-done | bytes 1048
  6.9 0.2 copy-done.2
  7.4 1.1 %shard_map.127 = (f32[576,128]{1,0:T(8,128)S(1)}, f32[576,128]{1,0:T(8,128)S(1)}, bf16[576,128]{1,0:T(8,128)(2,1)S(1)}, f32[1,128]{1,0:T(1,128)S(1)}, bf16[128,1...) custom-call(bf16[576,128]{1,0:T(8,128)(2,1)S(1)} %bitcast.16, ...), custom_call_target="tpu_custom_call" | custom-call | tf_op jit(solution)/shard_map/pallas_call | solution.py:213
  8.5 1.0 %shard_map.129.refs_8_ = bf16[576,128]{1,0:T(8,128)(2,1)S(1)} custom-call(f32[96,1,128]{2,1,0:T(1,128)S(1)} %broadcast_in_dim.31.row_mask.refs_1_, f32[96,128]{1,0:T(8,128)S(1)} %broadcast_in_dim.32.column_mask.refs_2_, f32[1,128]{1,0:T(1,128)S(1)} %bitcast.21, bf16[128,512]{1,0:T(8,128)(2,1)S(1)} %copy-done, f32[576,128]{1,0:T(8,128)S(1)} %get-tuple-element.28.left.refs_5_, ...), custom_call_target="tpu_custom_call" | custom-call | tf_op jit(solution)/shard_map/pallas_call | solution.py:213
  9.5 2.1 %collective-permute-done.1.refs_0_ = bf16[576,128]{1,0:T(8,128)(2,1)S(1)} collective-permute-done((bf16[576,128]{1,0:T(8,128)(2,1)}, bf16[576,128]{1,0:T(8,128)(2,1)S(1)}, u32[]{:S(2)}, u32[]{:S(2)}) %collective-permute-start.1) | collective-permute-done | bytes 147488 | tf_op jit(solution)/shard_map/ppermute | solution.py:225
  11.6 0.9 %shard_map.128.refs_7_ = bf16[576,128]{1,0:T(8,128)(2,1)S(1)} custom-call(f32[96,1,128]{2,1,0:T(1,128)S(1)} %broadcast_in_dim.31.row_mask.refs_1_, f32[96,128]{1,0:T(8,128)S(1)} %broadcast_in_dim.32.column_mask.refs_2_, f32[1,128]{1,0:T(1,128)S(1)} %bitcast.22, bf16[128,512]{1,0:T(8,128)(2,1)S(1)} %copy-done, f32[576,128]{1,0:T(8,128)S(1)} %get-tuple-element.28.left.refs_5_, ...), custom_call_target="tpu_custom_call" | custom-call | tf_op jit(solution)/shard_map/pallas_call | solution.py:213
  12.6 1.1 %shard_map.130 = (bf16[576,128]{1,0:T(8,128)(2,1)S(1)}, bf16[576,128]{1,0:T(8,128)(2,1)S(1)}, bf16[576,128]{1,0:T(8,128)(2,1)S(1)}, bf16[576,128]{1,0:T(8,128)(2,1)S(1)}) custom-call(bf16[576,128]{1,0:T(8,128)(2,1)S(1)} %collective-permute-done.refs_0_, f32[96,1,128]{2,1,0:T(1,128)S(1)} %broadcast_in_dim.31.row_mask.refs_1_, ...), custom_call_target="tpu_custom_call" | custom-call | tf_op jit(solution)/shard_map/pallas_call | solution.py:213
  13.7 3.7 %collective-permute-start.3 = (bf16[576,128]{1,0:T(8,128)(2,1)S(1)}, bf16[576,128]{1,0:T(8,128)(2,1)S(1)}, u32[]{:S(2)}, u32[]{:S(2)}) collective-permute-start(bf16[576,128]{1,0:T(8,128)(2,1)S(1)} %get-tuple-element.31), channel_id=1, source_target_pairs={{0,3},{1,2},{2,1},{3,0},{4,7},{5,6},{6,5},{7,4},{8,11},{9,10},{10,... | collective-permute-start | bytes 442376 | tf_op jit(solution)/shard_map/ppermute | solution.py:225
  17.3 0.8 %collective-permute-start.5 = (bf16[576,128]{1,0:T(8,128)(2,1)S(1)}, bf16[576,128]{1,0:T(8,128)(2,1)S(1)}, u32[]{:S(2)}, u32[]{:S(2)}) collective-permute-start(bf16[576,128]{1,0:T(8,128)(2,1)S(1)} %get-tuple-element.33), channel_id=1, source_target_pairs={{0,2},{1,3},{2,0},{3,1},{4,6},{5,7},{6,4},{7,5},{8,10},{9,11},{10,... | collective-permute-start | bytes 442376 | tf_op jit(solution)/shard_map/ppermute | solution.py:225
  18.1 4.1 %collective-permute-done.3.refs_1_ = bf16[576,128]{1,0:T(8,128)(2,1)S(1)} collective-permute-done((bf16[576,128]{1,0:T(8,128)(2,1)S(1)}, bf16[576,128]{1,0:T(8,128)(2,1)S(1)}, u32[]{:S(2)}, u32[]{:S(2)}) %collective-permute-start.3) | collective-permute-done | bytes 147488 | tf_op jit(solution)/shard_map/ppermute | solution.py:225
  22.3 1.5 %collective-permute-done.4.refs_2_ = bf16[576,128]{1,0:T(8,128)(2,1)S(1)} collective-permute-done((bf16[576,128]{1,0:T(8,128)(2,1)S(1)}, bf16[576,128]{1,0:T(8,128)(2,1)S(1)}, u32[]{:S(2)}, u32[]{:S(2)}) %collective-permute-start.4) | collective-permute-done | bytes 147488 | tf_op jit(solution)/shard_map/ppermute | solution.py:225
  23.7 4.2 %collective-permute-done.5.refs_3_ = bf16[576,128]{1,0:T(8,128)(2,1)S(1)} collective-permute-done((bf16[576,128]{1,0:T(8,128)(2,1)S(1)}, bf16[576,128]{1,0:T(8,128)(2,1)S(1)}, u32[]{:S(2)}, u32[]{:S(2)}) %collective-permute-start.5) | collective-permute-done | bytes 147488 | tf_op jit(solution)/shard_map/ppermute | solution.py:225
  27.9 0.7 %shard_map.131 = (bf16[576,128]{1,0:T(8,128)(2,1)S(1)}, bf16[576,128]{1,0:T(8,128)(2,1)S(1)}, bf16[1,24,96]{2,1,0:T(8,128)(2,1)S(1)}) custom-call(bf16[576,128]{1,0:T(8,128)(2,1)S(1)} %bitcast.17, f32[576,128]{1,0:T(8,128)S(1)} %get-tuple-element.23.gate, f32[1,128]{1,0:T(1,128)S(1)} %get-tuple-element.24.product_gain, ...), custom_call_target="tpu_custom_call" | custom-call | tf_op jit(solution)/shard_map/pallas_call | solution.py:213
  28.7 3.4 %collective-permute-start.8 = (bf16[576,128]{1,0:T(8,128)(2,1)S(1)}, bf16[576,128]{1,0:T(8,128)(2,1)S(1)}, u32[]{:S(2)}, u32[]{:S(2)}) collective-permute-start(bf16[576,128]{1,0:T(8,128)(2,1)S(1)} %get-tuple-element.39.refs_0_), channel_id=1, source_target_pairs={{0,2},{1,3},{2,0},{3,1},{4,6},{5,7},{6,4},{7,5},{8,10},{9,11},{10,... | collective-permute-start | bytes 442376 | tf_op jit(solution)/shard_map/ppermute | solution.py:225
  32.1 1.0 %collective-permute-start.7 = (bf16[576,128]{1,0:T(8,128)(2,1)S(1)}, bf16[576,128]{1,0:T(8,128)(2,1)S(1)}, u32[]{:S(2)}, u32[]{:S(2)}) collective-permute-start(bf16[576,128]{1,0:T(8,128)(2,1)S(1)} %get-tuple-element.39.refs_0_), channel_id=1, source_target_pairs={{0,3},{1,2},{2,1},{3,0},{4,7},{5,6},{6,5},{7,4},{8,11},{9,10},{10,... | collective-permute-start | bytes 442376 | tf_op jit(solution)/shard_map/ppermute | solution.py:225
  33.1 3.5 %collective-permute-done.6.attend.refs_1_ = bf16[576,128]{1,0:T(8,128)(2,1)S(1)} collective-permute-done((bf16[576,128]{1,0:T(8,128)(2,1)S(1)}, bf16[576,128]{1,0:T(8,128)(2,1)S(1)}, u32[]{:S(2)}, u32[]{:S(2)}) %collective-permute-start.6) | collective-permute-done | bytes 147488 | tf_op jit(solution)/shard_map/ppermute | solution.py:225
  36.6 0.2 shard_map.132
  36.8 1.7 %collective-permute-start.10 = (bf16[48,96]{1,0:T(8,128)(2,1)S(1)}, bf16[48,96]{1,0:T(8,128)(2,1)S(1)}, u32[]{:S(2)}, u32[]{:S(2)}) collective-permute-start(bf16[48,96]{1,0:T(8,128)(2,1)S(1)} %bitcast.18), channel_id=1, source_target_pairs={{0,12},{1,8},{2,4},{3,0},{4,13},{5,9},{6,5},{7,1},{8,14},{9,10},{1... | collective-permute-start | bytes 27656 | tf_op jit(solution)/shard_map/ppermute | solution.py:330
  38.5 3.6 %collective-permute-done.8.refs_3_ = bf16[576,128]{1,0:T(8,128)(2,1)S(1)} collective-permute-done((bf16[576,128]{1,0:T(8,128)(2,1)S(1)}, bf16[576,128]{1,0:T(8,128)(2,1)S(1)}, u32[]{:S(2)}, u32[]{:S(2)}) %collective-permute-start.8) | collective-permute-done | bytes 147488 | tf_op jit(solution)/shard_map/ppermute | solution.py:225
  42.1 0.4 collective-permute-done.10.refs_5_
  42.5 2.0 %shard_map.133 = bf16[576,128]{1,0:T(8,128)(2,1)} custom-call(bf16[576,128]{1,0:T(8,128)(2,1)S(1)} %get-tuple-element.34.middle, f32[96,96]{1,0:T(8,128)S(1)} %get-tuple-element.35.allowed, bf16[128,384]{1,0:T(8,128)(2,1)S(1)} %get-tuple-element.36.w_inputs, bf16[128,128]{1,0:T(8,128)(2,1)S(1)} %get-tuple-element.37.w_gate, ...), custom_call_target="tpu_custom_call" | custom-call | tf_op jit(solution)/shard_map/pallas_call | solution.py:213
  (45 shorter events, 1.4 us)
Async XLA Ops:
  0.0 4.5 %copy-start.12 = (s32[96]{0:T(128)S(1)}, s32[96]{0:T(128)}, u32[]{:S(2)}) copy-start(s32[96]{0:T(128)} %param.14) | copy-start | bytes 1156
  0.0 8.5 %collective-permute-start.2 = (bf16[576,128]{1,0:T(8,128)(2,1)}, bf16[576,128]{1,0:T(8,128)(2,1)S(1)}, u32[]{:S(2)}, u32[]{:S(2)}) collective-permute-start(bf16[576,128]{1,0:T(8,128)(2,1)} %bitcast.13), channel_id=1, source_target_pairs={{0,4},{4,0},{8,12},{12,8},{1,5},{5,1},{9,13},{13,9},{2,6},{6,2},{1... | collective-permute-start | bytes 442376 | tf_op jit(solution)/shard_map/ppermute | solution.py:225
  2.9 8.7 %collective-permute-start.1 = (bf16[576,128]{1,0:T(8,128)(2,1)}, bf16[576,128]{1,0:T(8,128)(2,1)S(1)}, u32[]{:S(2)}, u32[]{:S(2)}) collective-permute-start(bf16[576,128]{1,0:T(8,128)(2,1)} %bitcast.14), channel_id=1, source_target_pairs={{0,8},{4,12},{8,0},{12,4},{1,9},{5,13},{9,1},{13,5},{2,10},{6,14},... | collective-permute-start | bytes 442376 | tf_op jit(solution)/shard_map/ppermute | solution.py:225
  4.5 8.1 %collective-permute-start = (bf16[576,128]{1,0:T(8,128)(2,1)}, bf16[576,128]{1,0:T(8,128)(2,1)S(1)}, u32[]{:S(2)}, u32[]{:S(2)}) collective-permute-start(bf16[576,128]{1,0:T(8,128)(2,1)} %bitcast.15), channel_id=1, source_target_pairs={{0,12},{4,8},{8,4},{12,0},{1,13},{5,9},{9,5},{13,1},{2,14},{6,10},... | collective-permute-start | bytes 442376 | tf_op jit(solution)/shard_map/ppermute | solution.py:225
  4.5 0.7 %copy-start.10 = (s32[4,4]{1,0:T(4,128)S(1)}, s32[4,4]{1,0:T(4,128)}, u32[]{:S(2)}) copy-start(s32[4,4]{1,0:T(4,128)} %param.15) | copy-start | bytes 196
  5.3 0.7 %copy-start.11 = (bf16[128,4]{0,1:T(4,128)(2,1)S(1)}, bf16[128,4]{0,1:T(4,128)(2,1)}, u32[]{:S(2)}) copy-start(bf16[128,4]{0,1:T(4,128)(2,1)} %param.24) | copy-start | bytes 3076
  6.0 0.8 %copy-start.6 = (bf16[128,128]{1,0:T(8,128)(2,1)S(1)}, bf16[128,128]{1,0:T(8,128)(2,1)}, u32[]{:S(2)}) copy-start(bf16[128,128]{1,0:T(8,128)(2,1)} %refs_7_.1) | copy-start | bytes 98308
  6.1 0.8 %copy-start.4 = (bf16[128,128]{1,0:T(8,128)(2,1)S(1)}, bf16[128,128]{1,0:T(8,128)(2,1)}, u32[]{:S(2)}) copy-start(bf16[128,128]{1,0:T(8,128)(2,1)} %refs_1_.1) | copy-start | bytes 98308
  6.2 0.8 %copy-start.5 = (bf16[128,128]{1,0:T(8,128)(2,1)S(1)}, bf16[128,128]{1,0:T(8,128)(2,1)}, u32[]{:S(2)}) copy-start(bf16[128,128]{1,0:T(8,128)(2,1)} %refs_6_.1) | copy-start | bytes 98308
  6.2 0.9 %copy-start.2 = (bf16[128,384]{1,0:T(8,128)(2,1)S(1)}, bf16[128,384]{1,0:T(8,128)(2,1)}, u32[]{:S(2)}) copy-start(bf16[128,384]{1,0:T(8,128)(2,1)} %refs_5_.1) | copy-start | bytes 294916
  6.3 0.9 %copy-start.1 = (bf16[24,24,128]{2,1,0:T(8,128)(2,1)S(1)}, bf16[24,24,128]{2,1,0:T(8,128)(2,1)}, u32[]{:S(2)}) copy-start(bf16[24,24,128]{2,1,0:T(8,128)(2,1)} %param.13) | copy-start | bytes 442372
  6.4 1.0 %copy-start = (bf16[128,512]{1,0:T(8,128)(2,1)S(1)}, bf16[128,512]{1,0:T(8,128)(2,1)}, u32[]{:S(2)}) copy-start(bf16[128,512]{1,0:T(8,128)(2,1)} %refs_4_.1) | copy-start | bytes 393220
  6.6 0.8 %copy-start.3 = (bf16[128,128]{1,0:T(8,128)(2,1)S(1)}, bf16[128,128]{1,0:T(8,128)(2,1)}, u32[]{:S(2)}) copy-start(bf16[128,128]{1,0:T(8,128)(2,1)} %w_gate.1) | copy-start | bytes 98308
  6.6 0.8 %copy-start.7 = (f32[128]{0:T(128)S(1)}, f32[128]{0:T(128)}, u32[]{:S(2)}) copy-start(f32[128]{0:T(128)} %param.16) | copy-start | bytes 1540
  6.6 0.8 %copy-start.8 = (f32[128]{0:T(128)S(1)}, f32[128]{0:T(128)}, u32[]{:S(2)}) copy-start(f32[128]{0:T(128)} %param.19) | copy-start | bytes 1540
  6.6 0.8 %copy-start.9 = (f32[128]{0:T(128)S(1)}, f32[128]{0:T(128)}, u32[]{:S(2)}) copy-start(f32[128]{0:T(128)} %param.21) | copy-start | bytes 1540
  13.7 8.6 %collective-permute-start.3 = (bf16[576,128]{1,0:T(8,128)(2,1)S(1)}, bf16[576,128]{1,0:T(8,128)(2,1)S(1)}, u32[]{:S(2)}, u32[]{:S(2)}) collective-permute-start(bf16[576,128]{1,0:T(8,128)(2,1)S(1)} %get-tuple-element.31), channel_id=1, source_target_pairs={{0,3},{1,2},{2,1},{3,0},{4,7},{5,6},{6,5},{7,4},{8,11},{9,10},{10,... | collective-permute-start | bytes 442376 | tf_op jit(solution)/shard_map/ppermute | solution.py:225
  17.3 6.4 %collective-permute-start.4 = (bf16[576,128]{1,0:T(8,128)(2,1)S(1)}, bf16[576,128]{1,0:T(8,128)(2,1)S(1)}, u32[]{:S(2)}, u32[]{:S(2)}) collective-permute-start(bf16[576,128]{1,0:T(8,128)(2,1)S(1)} %get-tuple-element.32), channel_id=1, source_target_pairs={{0,1},{1,0},{2,3},{3,2},{4,5},{5,4},{6,7},{7,6},{8,9},{9,8},{10,11... | collective-permute-start | bytes 442376 | tf_op jit(solution)/shard_map/ppermute | solution.py:225
  17.3 10.6 %collective-permute-start.5 = (bf16[576,128]{1,0:T(8,128)(2,1)S(1)}, bf16[576,128]{1,0:T(8,128)(2,1)S(1)}, u32[]{:S(2)}, u32[]{:S(2)}) collective-permute-start(bf16[576,128]{1,0:T(8,128)(2,1)S(1)} %get-tuple-element.33), channel_id=1, source_target_pairs={{0,2},{1,3},{2,0},{3,1},{4,6},{5,7},{6,4},{7,5},{8,10},{9,11},{10,... | collective-permute-start | bytes 442376 | tf_op jit(solution)/shard_map/ppermute | solution.py:225
  28.7 8.0 %collective-permute-start.6 = (bf16[576,128]{1,0:T(8,128)(2,1)S(1)}, bf16[576,128]{1,0:T(8,128)(2,1)S(1)}, u32[]{:S(2)}, u32[]{:S(2)}) collective-permute-start(bf16[576,128]{1,0:T(8,128)(2,1)S(1)} %get-tuple-element.39.refs_0_), channel_id=1, source_target_pairs={{0,1},{1,0},{2,3},{3,2},{4,5},{5,4},{6,7},{7,6},{8,9},{9,8},{10,11... | collective-permute-start | bytes 442376 | tf_op jit(solution)/shard_map/ppermute | solution.py:225
  28.7 13.4 %collective-permute-start.8 = (bf16[576,128]{1,0:T(8,128)(2,1)S(1)}, bf16[576,128]{1,0:T(8,128)(2,1)S(1)}, u32[]{:S(2)}, u32[]{:S(2)}) collective-permute-start(bf16[576,128]{1,0:T(8,128)(2,1)S(1)} %get-tuple-element.39.refs_0_), channel_id=1, source_target_pairs={{0,2},{1,3},{2,0},{3,1},{4,6},{5,7},{6,4},{7,5},{8,10},{9,11},{10,... | collective-permute-start | bytes 442376 | tf_op jit(solution)/shard_map/ppermute | solution.py:225
  32.1 10.0 %collective-permute-start.7 = (bf16[576,128]{1,0:T(8,128)(2,1)S(1)}, bf16[576,128]{1,0:T(8,128)(2,1)S(1)}, u32[]{:S(2)}, u32[]{:S(2)}) collective-permute-start(bf16[576,128]{1,0:T(8,128)(2,1)S(1)} %get-tuple-element.39.refs_0_), channel_id=1, source_target_pairs={{0,3},{1,2},{2,1},{3,0},{4,7},{5,6},{6,5},{7,4},{8,11},{9,10},{10,... | collective-permute-start | bytes 442376 | tf_op jit(solution)/shard_map/ppermute | solution.py:225
  36.8 5.7 %collective-permute-start.10 = (bf16[48,96]{1,0:T(8,128)(2,1)S(1)}, bf16[48,96]{1,0:T(8,128)(2,1)S(1)}, u32[]{:S(2)}, u32[]{:S(2)}) collective-permute-start(bf16[48,96]{1,0:T(8,128)(2,1)S(1)} %bitcast.18), channel_id=1, source_target_pairs={{0,12},{1,8},{2,4},{3,0},{4,13},{5,9},{6,5},{7,1},{8,14},{9,10},{1... | collective-permute-start | bytes 27656 | tf_op jit(solution)/shard_map/ppermute | solution.py:330
  38.5 4.0 %collective-permute-start.9 = (bf16[48,96]{1,0:T(8,128)(2,1)S(1)}, bf16[48,96]{1,0:T(8,128)(2,1)S(1)}, u32[]{:S(2)}, u32[]{:S(2)}) collective-permute-start(bf16[48,96]{1,0:T(8,128)(2,1)S(1)} %bitcast.19), channel_id=1, source_target_pairs={{0,4},{1,0},{2,12},{3,8},{4,5},{5,1},{6,13},{7,9},{8,6},{9,2},{10,... | collective-permute-start | bytes 27656 | tf_op jit(solution)/shard_map/ppermute | solution.py:330

commit v6 on v5

--- a/solution.py
+++ b/solution.py
@@ -64,7 +64,7 @@
     part = dot(normed, w_in[:, : 2 * channels])
     value = mask * jax.nn.sigmoid(part[:, :channels]) * part[:, channels:]
     left[...] = value.astype(jnp.bfloat16).astype(jnp.float32)
-    right[...] = right_factor(rows, columns, 0, normed, row_mask, column_mask, w_in)
+    right[pl.ds(0, size), :] = right_factor(rows, columns, 0, normed, row_mask, column_mask, w_in)
     gate[...] = jax.nn.sigmoid(dot(normed, w_gate[...]))
     for part in range(rows // columns):
         multiply(rows, columns, left, right, part * columns * columns, part_out, part * size)
@@ -78,7 +78,7 @@
     split = rows // columns
     for at, (step, state) in enumerate(zip(steps, states)):
         normed = layer_norm(state[...].astype(jnp.float32), gain[...]).astype(jnp.bfloat16)
-        right[...] = right_factor(rows, columns, step, normed, row_mask, column_mask, w_in)
+        right[pl.ds(0, size), :] = right_factor(rows, columns, step, normed, row_mask, column_mask, w_in)
         for part in range(split):
             multiply(rows, columns, left, right, part * columns * columns, part_out, (at * split + part) * size)
 
@@ -139,21 +139,33 @@
         bias[part] = jnp.concatenate([own[part].astype(jnp.float32), total], 0).astype(jnp.bfloat16)
 
 
-def attend_kernel(rows, columns, heads, split, column_devices, arrival, middle, allowed, w_inputs, w_gate, w_out, *refs):
-    tiles, refs = refs[:column_devices], refs[column_devices:]
+def project(rows, columns, w_inputs, tiles, keys, values):
+    channels = w_inputs.shape[0]
+    for at, tile in enumerate(tiles):
+        part = dot(tile[...], w_inputs[:, channels:]).reshape(rows, columns, 2 * channels)
+        here = pl.ds(at * columns, columns)
+        keys[:, here, :] = part[..., :channels]
+        values[:, here, :] = part[..., channels:]
+
+
+def near_kernel(rows, columns, count, w_inputs, w_gate, *refs):
+    tiles, (keys, values, queries, gates) = refs[:count], refs[count:]
+    own = tiles[0][...]
+    queries[...] = dot(own, w_inputs[:, : own.shape[1]])
+    gates[...] = jax.nn.sigmoid(dot(own, w_gate[...]))
+    project(rows, columns, w_inputs, tiles, keys, values)
+
+
+def attend_kernel(rows, columns, heads, split, column_devices, arrival, middle, allowed, w_inputs, w_out, near_keys, near_values, queries, gates, *refs):
+    far = len(arrival) - near_keys.shape[1] // columns
+    tiles, refs = refs[:far], refs[far:]
     biases, refs = refs[: column_devices // 2], refs[column_devices // 2 :]
-    out, keys, values, queries, gates, bias, gated = refs
+    out, far_keys, far_values, bias, gated = refs
     channels = middle.shape[1]
     width = channels // heads
     tokens = columns * column_devices
     row_index, column_index = lax.axis_index("row"), lax.axis_index("col")
-    for step, tile in zip(arrival, tiles):
-        part = dot(tile[...], w_inputs[:, channels:]).reshape(rows, columns, 2 * channels)
-        keys[:, pl.ds(step * columns, columns), :] = part[..., :channels]
-        values[:, pl.ds(step * columns, columns), :] = part[..., channels:]
-    own = tiles[0][...]
-    queries[...] = dot(own, w_inputs[:, :channels])
-    gates[...] = jax.nn.sigmoid(dot(own, w_gate[...]))
+    project(rows, columns, w_inputs, tiles, far_keys, far_values)
     for step, piece in enumerate(biases):
         piece = piece[...].astype(jnp.float32)
         for side in range(2):
@@ -161,11 +173,12 @@
             place = lax.bitwise_xor(place, column_index)
             here = pl.ds(pl.multiple_of(place * columns, 8), columns)
             bias[here, :] = piece[side * columns : (side + 1) * columns]
-    for step in range(column_devices):
+    pieces = []
+    for step in arrival:
         start = pl.multiple_of(lax.bitwise_xor(column_index, step) * columns, 8)
-        here = pl.ds(step * columns, columns)
-        bias[here, :] = jnp.where(allowed[pl.ds(start, columns), :] > 0, bias[here, :], -1e30)
-    added = bias[...].T
+        piece = bias[pl.ds(step * columns, columns), :]
+        pieces.append(jnp.where(allowed[pl.ds(start, columns), :] > 0, piece, -1e30))
+    added = jnp.concatenate(pieces, 0).T
     head_of_lane = (lax.broadcasted_iota(jnp.int32, (1, 2 * channels), 1) % channels) // width
     picks = [head_of_lane == h for h in range(heads)]
     scale = 1.0 / math.sqrt(width)
@@ -182,14 +195,15 @@
         for at, start in zip(places, starts):
             query = queries[pl.ds(start, columns), :]
             stacked = jnp.concatenate([jnp.where(pick[:, :channels], query, 0.0) for pick in picks], 0).astype(jnp.bfloat16)
-            key = keys[at].astype(jnp.bfloat16)
+            key = jnp.concatenate([near_keys[at], far_keys[at]], 0).astype(jnp.bfloat16)
             scores.append(lax.dot_general(stacked, key, (((1,), (1,)), ((), ())), preferred_element_type=jnp.float32))
         scores = [score * scale + added for score in scores]
         tops = [jnp.max(score, axis=-1, keepdims=True) for score in scores]
         weights = [jnp.exp(score - top).astype(jnp.bfloat16) for score, top in zip(scores, tops)]
+        held = [jnp.concatenate([near_values[at], far_values[at]], 0).astype(jnp.bfloat16) for at in places]
         mixed = [
-            dot(weight, jnp.concatenate([values[at].astype(jnp.bfloat16), ones], 1))
-            for weight, at in zip(weights, places)
+            dot(weight, jnp.concatenate([value, ones], 1))
+            for weight, value in zip(weights, held)
         ]
         for mix, start in zip(mixed, starts):
             total = mix[:columns]
@@ -275,24 +289,25 @@
         attend_output,
     ]
     flat = pltpu.VMEM((size, channels), jnp.float32)
+    padded = pltpu.VMEM((size + columns, channels), jnp.float32)
     left, gate, own, *weights = call(
         functools.partial(own_kernel, rows, columns),
         [wide, wide, jax.ShapeDtypeStruct((split * size, channels), jnp.bfloat16)]
         + [jax.ShapeDtypeStruct(weight.shape, weight.dtype) for weight in weights],
         [state, row_mask, column_mask, norm_in, triangle_input, triangle_gate] + weights,
-        [flat],
+        [padded],
     )
     w_product, w_middle, w_attend, w_bias, allowed, w_inputs, w_gate, w_out = weights
     late_steps = list(range(row_devices - row_devices // 4, row_devices))
     early_steps = list(range(1, late_steps[0]))
     common = [row_mask, column_mask, norm_in, triangle_input, left]
-    early_groups = [[step] for step in early_steps[::-1]]
+    early_groups = [[step] for step in early_steps]
     early = [
         call(
             functools.partial(early_kernel, rows, columns, group),
             jax.ShapeDtypeStruct((len(group) * split * size, channels), jnp.bfloat16),
             common + [others[step - 1] for step in group],
-            [flat],
+            [padded],
         )
         for group in early_groups
     ]
@@ -300,7 +315,7 @@
         functools.partial(late_kernel, rows, columns, late_steps, column_devices, early_groups),
         [tile] * column_devices,
         [others[step - 1] for step in late_steps] + common + [own] + early,
-        [pltpu.VMEM((len(late_steps) * split * size, channels), jnp.bfloat16), flat],
+        [pltpu.VMEM((len(late_steps) * split * size, channels), jnp.bfloat16), padded],
     )
     order = list(range(column_devices - 1, 2, -1)) + [1, 2]
     parts = [parts[0]] + [exchange(parts[step], "col", step) for step in order]
@@ -310,7 +325,7 @@
         [state, gate, w_product, w_middle, w_attend, w_bias] + parts,
     )
     moved = {step: exchange(attend, "col", step) for step in order}
-    arrival = [0, 1] + list(range(column_devices - 1, 1, -1))
+    arrival = list(range(column_devices))
     tiles = [attend] + [moved[step] for step in arrival[1:]]
     both = call(
         functools.partial(neighbor_kernel, rows, columns, split),
@@ -328,14 +343,19 @@
                 turn = b ^ step
                 pairs.append((a * column_devices + b, (turn // split) * column_devices + split * a + turn % split))
         biases.append(lax.ppermute(piece, ("row", "col"), pairs))
-    stack = pltpu.VMEM((rows, tokens, channels), jnp.float32)
+    near = 2
+    near_stack = jax.ShapeDtypeStruct((rows, near * columns, channels), jnp.float32)
+    held = call(
+        functools.partial(near_kernel, rows, columns, near),
+        [near_stack, near_stack, wide, wide],
+        [w_inputs, w_gate] + tiles[:near],
+    )
+    far_stack = pltpu.VMEM((rows, tokens - near * columns, channels), jnp.float32)
     result = call(
         functools.partial(attend_kernel, rows, columns, heads, split, column_devices, arrival),
         tile,
-        [middle, allowed, w_inputs, w_gate, w_out]
-        + tiles
-        + biases,
-        [stack, stack, flat, flat, pltpu.VMEM((tokens, heads * columns), jnp.float32), flat],
+        [middle, allowed, w_inputs, w_out, *held] + tiles[near:] + biases,
+        [far_stack, far_stack, pltpu.VMEM((tokens, heads * columns), jnp.float32), flat],
     )
     return result.reshape(rows, columns, channels)
 

time: 45.3 us -> 45 us (level)
    pallas_call x7 -> x8, Pallas kernels: 7.03 us -> 7.19 us  [call(): pl.pallas_call(kernel, out_shape=outs, in_specs=[VMEM] * len(args), out_s...]
  transfers between devices with their start and end apart: 11 -> 11, of which waited for: 7 -> 7; matrix products, arithmetic and copies ran while one was open for 2% -> 2% of each run, Pallas kernels for 7% -> 8%
where the time goes in v6:
time: 45 us; the launch traced here: 44.3 us
  waiting for transfers between devices  19.1 us (42%)
  starting transfers between devices  15 us (33%)
  Pallas kernels  7.19 us (16%)
  local copies, waits for them, and re-layouts  2.66 us (6%)
    ppermute x9, waiting for transfers between devices, exchange(): return lax.ppermute(value, axis, [(at, at ^ step) for at in range(size)])  18.7 us
    ppermute x9, starting transfers between devices, exchange(): return lax.ppermute(value, axis, [(at, at ^ step) for at in range(size)])  13.3 us
    pallas_call x8, Pallas kernels, call(): pl.pallas_call(kernel, out_shape=outs, in_specs=[VMEM] * len(args), out_s...  7.19 us
    unnamed x27, local copies, waits for them, and re-layouts  1.98 us
    ppermute x2, starting transfers between devices, shards(): biases.append(lax.ppermute(piece, ('row', 'col'), pairs))  1.66 us
  transfers between devices with their start and end apart: 11, of which 7 were waited for; matrix products, arithmetic and copies ran while one was open for 2% of the time, Pallas kernels for 8%

profile of v6, /device:TPU:0, one launch (start us, length us, event | category | flops | bytes accessed | tf_op | source)
XLA Modules:
  0.0 44.3 jit_solution(17779834827624542562)
XLA Ops:
  0.0 2.9 %collective-permute-start.1 = (bf16[576,128]{1,0:T(8,128)(2,1)}, bf16[576,128]{1,0:T(8,128)(2,1)S(1)}, u32[]{:S(2)}, u32[]{:S(2)}) collective-permute-start(bf16[576,128]{1,0:T(8,128)(2,1)} %bitcast.13), channel_id=1, source_target_pairs={{0,4},{4,0},{8,12},{12,8},{1,5},{5,1},{9,13},{13,9},{2,6},{6,2},{1... | collective-permute-start | bytes 442376 | tf_op jit(solution)/shard_map/ppermute | solution.py:239
  2.9 1.5 %collective-permute-start.2 = (bf16[576,128]{1,0:T(8,128)(2,1)}, bf16[576,128]{1,0:T(8,128)(2,1)S(1)}, u32[]{:S(2)}, u32[]{:S(2)}) collective-permute-start(bf16[576,128]{1,0:T(8,128)(2,1)} %bitcast.14), channel_id=1, source_target_pairs={{0,8},{4,12},{8,0},{12,4},{1,9},{5,13},{9,1},{13,5},{2,10},{6,14},... | collective-permute-start | bytes 442376 | tf_op jit(solution)/shard_map/ppermute | solution.py:239
  4.5 0.7 %copy-done.10 = s32[4,4]{1,0:T(4,128)S(1)} copy-done((s32[4,4]{1,0:T(4,128)S(1)}, s32[4,4]{1,0:T(4,128)}, u32[]{:S(2)}) %copy-start.10) | copy-done | bytes 88
  5.8 0.6 %copy-done.11 = bf16[128,4]{0,1:T(4,128)(2,1)S(1)} copy-done((bf16[128,4]{0,1:T(4,128)(2,1)S(1)}, bf16[128,4]{0,1:T(4,128)(2,1)}, u32[]{:S(2)}) %copy-start.11) | copy-done | bytes 1048
  6.8 0.6 %copy-done.7 = f32[128]{0:T(128)S(1)} copy-done((f32[128]{0:T(128)S(1)}, f32[128]{0:T(128)}, u32[]{:S(2)}) %copy-start.7) | copy-done | bytes 536
  7.4 1.1 %shard_map.127 = (f32[576,128]{1,0:T(8,128)S(1)}, f32[576,128]{1,0:T(8,128)S(1)}, bf16[576,128]{1,0:T(8,128)(2,1)S(1)}, f32[1,128]{1,0:T(1,128)S(1)}, bf16[128,1...) custom-call(bf16[576,128]{1,0:T(8,128)(2,1)S(1)} %bitcast.16, ...), custom_call_target="tpu_custom_call" | custom-call | tf_op jit(solution)/shard_map/pallas_call | solution.py:227
  8.5 0.9 %shard_map.128.refs_7_ = bf16[576,128]{1,0:T(8,128)(2,1)S(1)} custom-call(f32[96,1,128]{2,1,0:T(1,128)S(1)} %broadcast_in_dim.31.row_mask.refs_1_, f32[96,128]{1,0:T(8,128)S(1)} %broadcast_in_dim.32.column_mask.refs_2_, f32[1,128]{1,0:T(1,128)S(1)} %bitcast.21, bf16[128,512]{1,0:T(8,128)(2,1)S(1)} %copy-done, f32[576,128]{1,0:T(8,128)S(1)} %get-tuple-element.32.left.refs_5_, ...), custom_call_target="tpu_custom_call" | custom-call | tf_op jit(solution)/shard_map/pallas_call | solution.py:227
  9.5 2.1 %collective-permute-done.2.refs_0_ = bf16[576,128]{1,0:T(8,128)(2,1)S(1)} collective-permute-done((bf16[576,128]{1,0:T(8,128)(2,1)}, bf16[576,128]{1,0:T(8,128)(2,1)S(1)}, u32[]{:S(2)}, u32[]{:S(2)}) %collective-permute-start.2) | collective-permute-done | bytes 147488 | tf_op jit(solution)/shard_map/ppermute | solution.py:239
  11.6 0.9 %shard_map.129.refs_8_ = bf16[576,128]{1,0:T(8,128)(2,1)S(1)} custom-call(f32[96,1,128]{2,1,0:T(1,128)S(1)} %broadcast_in_dim.31.row_mask.refs_1_, f32[96,128]{1,0:T(8,128)S(1)} %broadcast_in_dim.32.column_mask.refs_2_, f32[1,128]{1,0:T(1,128)S(1)} %bitcast.22, bf16[128,512]{1,0:T(8,128)(2,1)S(1)} %copy-done, f32[576,128]{1,0:T(8,128)S(1)} %get-tuple-element.32.left.refs_5_, ...), custom_call_target="tpu_custom_call" | custom-call | tf_op jit(solution)/shard_map/pallas_call | solution.py:227
  12.6 1.1 %shard_map.130 = (bf16[576,128]{1,0:T(8,128)(2,1)S(1)}, bf16[576,128]{1,0:T(8,128)(2,1)S(1)}, bf16[576,128]{1,0:T(8,128)(2,1)S(1)}, bf16[576,128]{1,0:T(8,128)(2,1)S(1)}) custom-call(bf16[576,128]{1,0:T(8,128)(2,1)S(1)} %collective-permute-done.refs_0_, f32[96,1,128]{2,1,0:T(1,128)S(1)} %broadcast_in_dim.31.row_mask.refs_1_, ...), custom_call_target="tpu_custom_call" | custom-call | tf_op jit(solution)/shard_map/pallas_call | solution.py:227
  13.7 3.7 %collective-permute-start.3 = (bf16[576,128]{1,0:T(8,128)(2,1)S(1)}, bf16[576,128]{1,0:T(8,128)(2,1)S(1)}, u32[]{:S(2)}, u32[]{:S(2)}) collective-permute-start(bf16[576,128]{1,0:T(8,128)(2,1)S(1)} %get-tuple-element.35), channel_id=1, source_target_pairs={{0,3},{1,2},{2,1},{3,0},{4,7},{5,6},{6,5},{7,4},{8,11},{9,10},{10,... | collective-permute-start | bytes 442376 | tf_op jit(solution)/shard_map/ppermute | solution.py:239
  17.3 0.8 %collective-permute-start.5 = (bf16[576,128]{1,0:T(8,128)(2,1)S(1)}, bf16[576,128]{1,0:T(8,128)(2,1)S(1)}, u32[]{:S(2)}, u32[]{:S(2)}) collective-permute-start(bf16[576,128]{1,0:T(8,128)(2,1)S(1)} %get-tuple-element.37), channel_id=1, source_target_pairs={{0,2},{1,3},{2,0},{3,1},{4,6},{5,7},{6,4},{7,5},{8,10},{9,11},{10,... | collective-permute-start | bytes 442376 | tf_op jit(solution)/shard_map/ppermute | solution.py:239
  18.1 4.1 %collective-permute-done.3.refs_1_ = bf16[576,128]{1,0:T(8,128)(2,1)S(1)} collective-permute-done((bf16[576,128]{1,0:T(8,128)(2,1)S(1)}, bf16[576,128]{1,0:T(8,128)(2,1)S(1)}, u32[]{:S(2)}, u32[]{:S(2)}) %collective-permute-start.3) | collective-permute-done | bytes 147488 | tf_op jit(solution)/shard_map/ppermute | solution.py:239
  22.3 1.5 %collective-permute-done.4.refs_2_ = bf16[576,128]{1,0:T(8,128)(2,1)S(1)} collective-permute-done((bf16[576,128]{1,0:T(8,128)(2,1)S(1)}, bf16[576,128]{1,0:T(8,128)(2,1)S(1)}, u32[]{:S(2)}, u32[]{:S(2)}) %collective-permute-start.4) | collective-permute-done | bytes 147488 | tf_op jit(solution)/shard_map/ppermute | solution.py:239
  23.7 4.2 %collective-permute-done.5.refs_3_ = bf16[576,128]{1,0:T(8,128)(2,1)S(1)} collective-permute-done((bf16[576,128]{1,0:T(8,128)(2,1)S(1)}, bf16[576,128]{1,0:T(8,128)(2,1)S(1)}, u32[]{:S(2)}, u32[]{:S(2)}) %collective-permute-start.5) | collective-permute-done | bytes 147488 | tf_op jit(solution)/shard_map/ppermute | solution.py:239
  27.9 0.7 %shard_map.131 = (bf16[576,128]{1,0:T(8,128)(2,1)S(1)}, bf16[576,128]{1,0:T(8,128)(2,1)S(1)}, bf16[1,24,96]{2,1,0:T(8,128)(2,1)S(1)}) custom-call(bf16[576,128]{1,0:T(8,128)(2,1)S(1)} %bitcast.17, f32[576,128]{1,0:T(8,128)S(1)} %get-tuple-element.27.gate, f32[1,128]{1,0:T(1,128)S(1)} %get-tuple-element.28.product_gain, ...), custom_call_target="tpu_custom_call" | custom-call | tf_op jit(solution)/shard_map/pallas_call | solution.py:227
  28.7 3.4 %collective-permute-start.7 = (bf16[576,128]{1,0:T(8,128)(2,1)S(1)}, bf16[576,128]{1,0:T(8,128)(2,1)S(1)}, u32[]{:S(2)}, u32[]{:S(2)}) collective-permute-start(bf16[576,128]{1,0:T(8,128)(2,1)S(1)} %get-tuple-element.43.refs_0_), channel_id=1, source_target_pairs={{0,2},{1,3},{2,0},{3,1},{4,6},{5,7},{6,4},{7,5},{8,10},{9,11},{10,... | collective-permute-start | bytes 442376 | tf_op jit(solution)/shard_map/ppermute | solution.py:239
  32.1 1.0 %collective-permute-start.8 = (bf16[576,128]{1,0:T(8,128)(2,1)S(1)}, bf16[576,128]{1,0:T(8,128)(2,1)S(1)}, u32[]{:S(2)}, u32[]{:S(2)}) collective-permute-start(bf16[576,128]{1,0:T(8,128)(2,1)S(1)} %get-tuple-element.43.refs_0_), channel_id=1, source_target_pairs={{0,3},{1,2},{2,1},{3,0},{4,7},{5,6},{6,5},{7,4},{8,11},{9,10},{10,... | collective-permute-start | bytes 442376 | tf_op jit(solution)/shard_map/ppermute | solution.py:239
  33.1 3.5 %collective-permute-done.6.refs_1_.attend = bf16[576,128]{1,0:T(8,128)(2,1)S(1)} collective-permute-done((bf16[576,128]{1,0:T(8,128)(2,1)S(1)}, bf16[576,128]{1,0:T(8,128)(2,1)S(1)}, u32[]{:S(2)}, u32[]{:S(2)}) %collective-permute-start.6) | collective-permute-done | bytes 147488 | tf_op jit(solution)/shard_map/ppermute | solution.py:239
  36.8 1.7 %collective-permute-start.10 = (bf16[48,96]{1,0:T(8,128)(2,1)S(1)}, bf16[48,96]{1,0:T(8,128)(2,1)S(1)}, u32[]{:S(2)}, u32[]{:S(2)}) collective-permute-start(bf16[48,96]{1,0:T(8,128)(2,1)S(1)} %bitcast.18), channel_id=1, source_target_pairs={{0,12},{1,8},{2,4},{3,0},{4,13},{5,9},{6,5},{7,1},{8,14},{9,10},{1... | collective-permute-start | bytes 27656 | tf_op jit(solution)/shard_map/ppermute | solution.py:345
  38.5 0.4 shard_map.132
  38.8 3.2 %collective-permute-done.7.refs_0_ = bf16[576,128]{1,0:T(8,128)(2,1)S(1)} collective-permute-done((bf16[576,128]{1,0:T(8,128)(2,1)S(1)}, bf16[576,128]{1,0:T(8,128)(2,1)S(1)}, u32[]{:S(2)}, u32[]{:S(2)}) %collective-permute-start.7) | collective-permute-done | bytes 147488 | tf_op jit(solution)/shard_map/ppermute | solution.py:239
  42.1 0.4 collective-permute-done.10.refs_3_
  42.5 1.8 %shard_map.134 = bf16[576,128]{1,0:T(8,128)(2,1)} custom-call(bf16[576,128]{1,0:T(8,128)(2,1)S(1)} %get-tuple-element.38.middle, f32[96,96]{1,0:T(8,128)S(1)} %get-tuple-element.39.allowed, bf16[128,384]{1,0:T(8,128)(2,1)S(1)} %get-tuple-element.40.w_inputs, bf16[128,128]{1,0:T(8,128)(2,1)S(1)} %get-tuple-element.41.w_out, ...), custom_call_target="tpu_custom_call" | custom-call | tf_op jit(solution)/shard_map/pallas_call | solution.py:227
  (46 shorter events, 1.2 us)
Async XLA Ops:
  0.0 4.5 %copy-start.12 = (s32[96]{0:T(128)S(1)}, s32[96]{0:T(128)}, u32[]{:S(2)}) copy-start(s32[96]{0:T(128)} %param.14) | copy-start | bytes 1156
  0.0 8.5 %collective-permute-start.1 = (bf16[576,128]{1,0:T(8,128)(2,1)}, bf16[576,128]{1,0:T(8,128)(2,1)S(1)}, u32[]{:S(2)}, u32[]{:S(2)}) collective-permute-start(bf16[576,128]{1,0:T(8,128)(2,1)} %bitcast.13), channel_id=1, source_target_pairs={{0,4},{4,0},{8,12},{12,8},{1,5},{5,1},{9,13},{13,9},{2,6},{6,2},{1... | collective-permute-start | bytes 442376 | tf_op jit(solution)/shard_map/ppermute | solution.py:239
  2.9 8.7 %collective-permute-start.2 = (bf16[576,128]{1,0:T(8,128)(2,1)}, bf16[576,128]{1,0:T(8,128)(2,1)S(1)}, u32[]{:S(2)}, u32[]{:S(2)}) collective-permute-start(bf16[576,128]{1,0:T(8,128)(2,1)} %bitcast.14), channel_id=1, source_target_pairs={{0,8},{4,12},{8,0},{12,4},{1,9},{5,13},{9,1},{13,5},{2,10},{6,14},... | collective-permute-start | bytes 442376 | tf_op jit(solution)/shard_map/ppermute | solution.py:239
  4.5 8.1 %collective-permute-start = (bf16[576,128]{1,0:T(8,128)(2,1)}, bf16[576,128]{1,0:T(8,128)(2,1)S(1)}, u32[]{:S(2)}, u32[]{:S(2)}) collective-permute-start(bf16[576,128]{1,0:T(8,128)(2,1)} %bitcast.15), channel_id=1, source_target_pairs={{0,12},{4,8},{8,4},{12,0},{1,13},{5,9},{9,5},{13,1},{2,14},{6,10},... | collective-permute-start | bytes 442376 | tf_op jit(solution)/shard_map/ppermute | solution.py:239
  4.5 0.7 %copy-start.10 = (s32[4,4]{1,0:T(4,128)S(1)}, s32[4,4]{1,0:T(4,128)}, u32[]{:S(2)}) copy-start(s32[4,4]{1,0:T(4,128)} %param.15) | copy-start | bytes 196
  5.4 1.3 %copy-start.4 = (bf16[128,128]{1,0:T(8,128)(2,1)S(1)}, bf16[128,128]{1,0:T(8,128)(2,1)}, u32[]{:S(2)}) copy-start(bf16[128,128]{1,0:T(8,128)(2,1)} %refs_1_.1) | copy-start | bytes 98308
  5.4 1.3 %copy-start.5 = (bf16[128,128]{1,0:T(8,128)(2,1)S(1)}, bf16[128,128]{1,0:T(8,128)(2,1)}, u32[]{:S(2)}) copy-start(bf16[128,128]{1,0:T(8,128)(2,1)} %refs_6_.1) | copy-start | bytes 98308
  5.4 1.3 %copy-start.6 = (bf16[128,128]{1,0:T(8,128)(2,1)S(1)}, bf16[128,128]{1,0:T(8,128)(2,1)}, u32[]{:S(2)}) copy-start(bf16[128,128]{1,0:T(8,128)(2,1)} %refs_7_.1) | copy-start | bytes 98308
  5.6 1.2 %copy-start.2 = (bf16[128,384]{1,0:T(8,128)(2,1)S(1)}, bf16[128,384]{1,0:T(8,128)(2,1)}, u32[]{:S(2)}) copy-start(bf16[128,384]{1,0:T(8,128)(2,1)} %refs_5_.1) | copy-start | bytes 294916
  5.6 0.7 %copy-start.11 = (bf16[128,4]{0,1:T(4,128)(2,1)S(1)}, bf16[128,4]{0,1:T(4,128)(2,1)}, u32[]{:S(2)}) copy-start(bf16[128,4]{0,1:T(4,128)(2,1)} %param.24) | copy-start | bytes 3076
  5.6 1.1 %copy-start.3 = (bf16[128,128]{1,0:T(8,128)(2,1)S(1)}, bf16[128,128]{1,0:T(8,128)(2,1)}, u32[]{:S(2)}) copy-start(bf16[128,128]{1,0:T(8,128)(2,1)} %w_gate.1) | copy-start | bytes 98308
  5.7 1.1 %copy-start.1 = (bf16[24,24,128]{2,1,0:T(8,128)(2,1)S(1)}, bf16[24,24,128]{2,1,0:T(8,128)(2,1)}, u32[]{:S(2)}) copy-start(bf16[24,24,128]{2,1,0:T(8,128)(2,1)} %param.13) | copy-start | bytes 442372
  5.7 1.1 %copy-start = (bf16[128,512]{1,0:T(8,128)(2,1)S(1)}, bf16[128,512]{1,0:T(8,128)(2,1)}, u32[]{:S(2)}) copy-start(bf16[128,512]{1,0:T(8,128)(2,1)} %refs_4_.1) | copy-start | bytes 393220
  6.7 0.7 %copy-start.7 = (f32[128]{0:T(128)S(1)}, f32[128]{0:T(128)}, u32[]{:S(2)}) copy-start(f32[128]{0:T(128)} %param.16) | copy-start | bytes 1540
  6.7 0.7 %copy-start.8 = (f32[128]{0:T(128)S(1)}, f32[128]{0:T(128)}, u32[]{:S(2)}) copy-start(f32[128]{0:T(128)} %param.19) | copy-start | bytes 1540
  6.7 0.7 %copy-start.9 = (f32[128]{0:T(128)S(1)}, f32[128]{0:T(128)}, u32[]{:S(2)}) copy-start(f32[128]{0:T(128)} %param.21) | copy-start | bytes 1540
  13.7 8.6 %collective-permute-start.3 = (bf16[576,128]{1,0:T(8,128)(2,1)S(1)}, bf16[576,128]{1,0:T(8,128)(2,1)S(1)}, u32[]{:S(2)}, u32[]{:S(2)}) collective-permute-start(bf16[576,128]{1,0:T(8,128)(2,1)S(1)} %get-tuple-element.35), channel_id=1, source_target_pairs={{0,3},{1,2},{2,1},{3,0},{4,7},{5,6},{6,5},{7,4},{8,11},{9,10},{10,... | collective-permute-start | bytes 442376 | tf_op jit(solution)/shard_map/ppermute | solution.py:239
  17.3 6.4 %collective-permute-start.4 = (bf16[576,128]{1,0:T(8,128)(2,1)S(1)}, bf16[576,128]{1,0:T(8,128)(2,1)S(1)}, u32[]{:S(2)}, u32[]{:S(2)}) collective-permute-start(bf16[576,128]{1,0:T(8,128)(2,1)S(1)} %get-tuple-element.36), channel_id=1, source_target_pairs={{0,1},{1,0},{2,3},{3,2},{4,5},{5,4},{6,7},{7,6},{8,9},{9,8},{10,11... | collective-permute-start | bytes 442376 | tf_op jit(solution)/shard_map/ppermute | solution.py:239
  17.3 10.6 %collective-permute-start.5 = (bf16[576,128]{1,0:T(8,128)(2,1)S(1)}, bf16[576,128]{1,0:T(8,128)(2,1)S(1)}, u32[]{:S(2)}, u32[]{:S(2)}) collective-permute-start(bf16[576,128]{1,0:T(8,128)(2,1)S(1)} %get-tuple-element.37), channel_id=1, source_target_pairs={{0,2},{1,3},{2,0},{3,1},{4,6},{5,7},{6,4},{7,5},{8,10},{9,11},{10,... | collective-permute-start | bytes 442376 | tf_op jit(solution)/shard_map/ppermute | solution.py:239
  28.7 8.0 %collective-permute-start.6 = (bf16[576,128]{1,0:T(8,128)(2,1)S(1)}, bf16[576,128]{1,0:T(8,128)(2,1)S(1)}, u32[]{:S(2)}, u32[]{:S(2)}) collective-permute-start(bf16[576,128]{1,0:T(8,128)(2,1)S(1)} %get-tuple-element.43.refs_0_), channel_id=1, source_target_pairs={{0,1},{1,0},{2,3},{3,2},{4,5},{5,4},{6,7},{7,6},{8,9},{9,8},{10,11... | collective-permute-start | bytes 442376 | tf_op jit(solution)/shard_map/ppermute | solution.py:239
  28.7 13.4 %collective-permute-start.7 = (bf16[576,128]{1,0:T(8,128)(2,1)S(1)}, bf16[576,128]{1,0:T(8,128)(2,1)S(1)}, u32[]{:S(2)}, u32[]{:S(2)}) collective-permute-start(bf16[576,128]{1,0:T(8,128)(2,1)S(1)} %get-tuple-element.43.refs_0_), channel_id=1, source_target_pairs={{0,2},{1,3},{2,0},{3,1},{4,6},{5,7},{6,4},{7,5},{8,10},{9,11},{10,... | collective-permute-start | bytes 442376 | tf_op jit(solution)/shard_map/ppermute | solution.py:239
  32.1 10.0 %collective-permute-start.8 = (bf16[576,128]{1,0:T(8,128)(2,1)S(1)}, bf16[576,128]{1,0:T(8,128)(2,1)S(1)}, u32[]{:S(2)}, u32[]{:S(2)}) collective-permute-start(bf16[576,128]{1,0:T(8,128)(2,1)S(1)} %get-tuple-element.43.refs_0_), channel_id=1, source_target_pairs={{0,3},{1,2},{2,1},{3,0},{4,7},{5,6},{6,5},{7,4},{8,11},{9,10},{10,... | collective-permute-start | bytes 442376 | tf_op jit(solution)/shard_map/ppermute | solution.py:239
  36.8 5.7 %collective-permute-start.10 = (bf16[48,96]{1,0:T(8,128)(2,1)S(1)}, bf16[48,96]{1,0:T(8,128)(2,1)S(1)}, u32[]{:S(2)}, u32[]{:S(2)}) collective-permute-start(bf16[48,96]{1,0:T(8,128)(2,1)S(1)} %bitcast.18), channel_id=1, source_target_pairs={{0,12},{1,8},{2,4},{3,0},{4,13},{5,9},{6,5},{7,1},{8,14},{9,10},{1... | collective-permute-start | bytes 27656 | tf_op jit(solution)/shard_map/ppermute | solution.py:345
  38.5 4.0 %collective-permute-start.9 = (bf16[48,96]{1,0:T(8,128)(2,1)S(1)}, bf16[48,96]{1,0:T(8,128)(2,1)S(1)}, u32[]{:S(2)}, u32[]{:S(2)}) collective-permute-start(bf16[48,96]{1,0:T(8,128)(2,1)S(1)} %bitcast.19), channel_id=1, source_target_pairs={{0,4},{1,0},{2,12},{3,8},{4,5},{5,1},{6,13},{7,9},{8,6},{9,2},{10,... | collective-permute-start | bytes 27656 | tf_op jit(solution)/shard_map/ppermute | solution.py:345

commit v7 on v6

--- a/solution.py
+++ b/solution.py
@@ -40,7 +40,7 @@
 
 def multiply(rows, columns, left, right, base, out, out_base):
     channels = left.shape[1]
-    group = 4 if rows % 4 == 0 else 2
+    group = 12 if rows % 12 == 0 else 2
     for at in range(rows // group):
         sums = [jnp.zeros((columns, channels), jnp.float32) for _ in range(group)]
         for k in range(columns):
@@ -83,28 +83,32 @@
             multiply(rows, columns, left, right, part * columns * columns, part_out, (at * split + part) * size)
 
 
-def late_kernel(rows, columns, steps, column_devices, early_groups, *refs):
-    states, refs = refs[: len(steps)], refs[len(steps) :]
-    row_mask, column_mask, gain, w_in, left, own, *refs = refs
-    early, refs = refs[: len(early_groups)], refs[len(early_groups) :]
-    outs, late, right = refs[:column_devices], refs[column_devices], refs[column_devices + 1]
-    size = rows * columns
-    split = rows // columns
-    early_kernel(rows, columns, steps, row_mask, column_mask, gain, w_in, left, *states, late, right)
+def fill(columns, split, source, first, last, outs):
+    section = outs[0].shape[0]
     row_index, column_index = lax.axis_index("row"), lax.axis_index("col")
     for step, out in enumerate(outs):
         target = lax.bitwise_xor(column_index, step)
         place = lax.bitwise_xor(row_index, target // split) * split + target % split
 
-        def fill(source, first, last, out=out, place=place):
-            @pl.when((place >= first) & (place < last))
-            def _():
-                out[...] = source[pl.ds(pl.multiple_of((place - first) * size, 16), size), :]
-
-        fill(own, 0, split)
-        for group, source in zip(early_groups, early):
-            fill(source, group[0] * split, (group[-1] + 1) * split)
-        fill(late, steps[0] * split, (steps[-1] + 1) * split)
+        @pl.when((place >= first) & (place < last))
+        def _(out=out, place=place):
+            out[...] = source[pl.ds(pl.multiple_of((place - first) * section, 16), section), :]
+
+
+def place_kernel(columns, split, early_groups, own, *refs):
+    early, outs = refs[: len(early_groups)], refs[len(early_groups) :]
+    fill(columns, split, own, 0, split, outs)
+    for group, source in zip(early_groups, early):
+        fill(columns, split, source, group[0] * split, (group[-1] + 1) * split, outs)
+
+
+def late_kernel(rows, columns, steps, column_devices, *refs):
+    states, refs = refs[: len(steps)], refs[len(steps) :]
+    row_mask, column_mask, gain, w_in, left, *refs = refs
+    outs, late, right = refs[column_devices:-2], refs[-2], refs[-1]
+    split = rows // columns
+    early_kernel(rows, columns, steps, row_mask, column_mask, gain, w_in, left, *states, late, right)
+    fill(columns, split, late, steps[0] * split, (steps[-1] + 1) * split, outs)
 
 
 def middle_kernel(rows, columns, split, state, gate, product_gain, w_out, attend_gain, w_bias, *refs):
@@ -148,12 +152,18 @@
         values[:, here, :] = part[..., channels:]
 
 
-def near_kernel(rows, columns, count, w_inputs, w_gate, *refs):
+def near_kernel(rows, columns, heads, count, w_inputs, w_gate, *refs):
     tiles, (keys, values, queries, gates) = refs[:count], refs[count:]
     own = tiles[0][...]
-    queries[...] = dot(own, w_inputs[:, : own.shape[1]])
+    channels = own.shape[1]
     gates[...] = jax.nn.sigmoid(dot(own, w_gate[...]))
-    project(rows, columns, w_inputs, tiles, keys, values)
+    query = dot(own, w_inputs[:, :channels]).reshape(rows, columns, channels)
+    head_of_lane = lax.broadcasted_iota(jnp.int32, (1, 1, channels), 2) // (channels // heads)
+    queries[...] = jnp.concatenate([jnp.where(head_of_lane == h, query, 0.0) for h in range(heads)], 1).astype(jnp.bfloat16)
+    parts = [dot(tile[...], w_inputs[:, channels:]).reshape(rows, columns, 2 * channels) for tile in tiles]
+    both = jnp.concatenate(parts, 1).astype(jnp.bfloat16)
+    keys[...] = both[..., :channels]
+    values[...] = both[..., channels:]
 
 
 def attend_kernel(rows, columns, heads, split, column_devices, arrival, middle, allowed, w_inputs, w_out, near_keys, near_values, queries, gates, *refs):
@@ -192,15 +202,13 @@
         places = [first * group + g for g in range(group)]
         starts = [pl.multiple_of(at * columns, 8) for at in places]
         scores = []
-        for at, start in zip(places, starts):
-            query = queries[pl.ds(start, columns), :]
-            stacked = jnp.concatenate([jnp.where(pick[:, :channels], query, 0.0) for pick in picks], 0).astype(jnp.bfloat16)
-            key = jnp.concatenate([near_keys[at], far_keys[at]], 0).astype(jnp.bfloat16)
-            scores.append(lax.dot_general(stacked, key, (((1,), (1,)), ((), ())), preferred_element_type=jnp.float32))
+        for at in places:
+            key = jnp.concatenate([near_keys[at], far_keys[at].astype(jnp.bfloat16)], 0)
+            scores.append(lax.dot_general(queries[at], key, (((1,), (1,)), ((), ())), preferred_element_type=jnp.float32))
         scores = [score * scale + added for score in scores]
         tops = [jnp.max(score, axis=-1, keepdims=True) for score in scores]
         weights = [jnp.exp(score - top).astype(jnp.bfloat16) for score, top in zip(scores, tops)]
-        held = [jnp.concatenate([near_values[at], far_values[at]], 0).astype(jnp.bfloat16) for at in places]
+        held = [jnp.concatenate([near_values[at], far_values[at].astype(jnp.bfloat16)], 0) for at in places]
         mixed = [
             dot(weight, jnp.concatenate([value, ones], 1))
             for weight, value in zip(weights, held)
@@ -221,7 +229,7 @@
     out[...] = (middle[...].astype(jnp.float32) + update).astype(jnp.bfloat16)
 
 
-def call(kernel, outs, args, scratch=()):
+def call(kernel, outs, args, scratch=(), aliases=None):
     arrays = jax.tree.leaves(outs) + list(args) + list(scratch)
     held = sum(math.prod(array.shape) * jnp.dtype(array.dtype).itemsize for array in arrays)
     return pl.pallas_call(
@@ -230,6 +238,7 @@
         in_specs=[VMEM] * len(args),
         out_specs=jax.tree.map(lambda _: VMEM, outs),
         scratch_shapes=scratch,
+        input_output_aliases=aliases or {},
         compiler_params=pltpu.CompilerParams(vmem_limit_bytes=min(56, 12 + 2 * held // 2**20) * 2**20),
     )(*args)
 
@@ -311,11 +320,19 @@
         )
         for group in early_groups
     ]
+    placed = call(
+        functools.partial(place_kernel, columns, split, early_groups),
+        [tile] * column_devices,
+        [own] + early,
+    )
+    late_states = [others[step - 1] for step in late_steps]
+    start = len(late_states) + len(common)
     parts = call(
-        functools.partial(late_kernel, rows, columns, late_steps, column_devices, early_groups),
+        functools.partial(late_kernel, rows, columns, late_steps, column_devices),
         [tile] * column_devices,
-        [others[step - 1] for step in late_steps] + common + [own] + early,
+        late_states + common + list(placed),
         [pltpu.VMEM((len(late_steps) * split * size, channels), jnp.bfloat16), padded],
+        {start + at: at for at in range(column_devices)},
     )
     order = list(range(column_devices - 1, 2, -1)) + [1, 2]
     parts = [parts[0]] + [exchange(parts[step], "col", step) for step in order]
@@ -344,10 +361,10 @@
                 pairs.append((a * column_devices + b, (turn // split) * column_devices + split * a + turn % split))
         biases.append(lax.ppermute(piece, ("row", "col"), pairs))
     near = 2
-    near_stack = jax.ShapeDtypeStruct((rows, near * columns, channels), jnp.float32)
+    near_stack = jax.ShapeDtypeStruct((rows, near * columns, channels), jnp.bfloat16)
     held = call(
-        functools.partial(near_kernel, rows, columns, near),
-        [near_stack, near_stack, wide, wide],
+        functools.partial(near_kernel, rows, columns, heads, near),
+        [near_stack, near_stack, jax.ShapeDtypeStruct((rows, heads * columns, channels), jnp.bfloat16), wide],
         [w_inputs, w_gate] + tiles[:near],
     )
     far_stack = pltpu.VMEM((rows, tokens - near * columns, channels), jnp.float32)

time: 45 us -> 44.8 us (level)
    pallas_call x8 -> x9, Pallas kernels: 7.19 us -> 7.03 us  [call(): pl.pallas_call(kernel, out_shape=outs, in_specs=[VMEM] * len(args), out_s...]
where the time goes in v7:
time: 44.8 us; the launch traced here: 44.1 us
  waiting for transfers between devices  19 us (42%)
  starting transfers between devices  15 us (33%)
  Pallas kernels  7.03 us (16%)
  local copies, waits for them, and re-layouts  2.66 us (6%)
    ppermute x9, waiting for transfers between devices, exchange(): return lax.ppermute(value, axis, [(at, at ^ step) for at in range(size)])  18.6 us
    ppermute x9, starting transfers between devices, exchange(): return lax.ppermute(value, axis, [(at, at ^ step) for at in range(size)])  13.3 us
    pallas_call x9, Pallas kernels, call(): pl.pallas_call(kernel, out_shape=outs, in_specs=[VMEM] * len(args), out_s...  7.03 us
    unnamed x27, local copies, waits for them, and re-layouts  1.98 us
    ppermute x2, starting transfers between devices, shards(): biases.append(lax.ppermute(piece, ('row', 'col'), pairs))  1.69 us
  transfers between devices with their start and end apart: 11, of which 7 were waited for; matrix products, arithmetic and copies ran while one was open for 2% of the time, Pallas kernels for 8%

profile of v7, /device:TPU:0, one launch (start us, length us, event | category | flops | bytes accessed | tf_op | source)
XLA Modules:
  0.0 44.1 jit_solution(15666188364354646897)
XLA Ops:
  0.0 2.9 %collective-permute-start.1 = (bf16[576,128]{1,0:T(8,128)(2,1)}, bf16[576,128]{1,0:T(8,128)(2,1)S(1)}, u32[]{:S(2)}, u32[]{:S(2)}) collective-permute-start(bf16[576,128]{1,0:T(8,128)(2,1)} %bitcast.13), channel_id=1, source_target_pairs={{0,4},{4,0},{8,12},{12,8},{1,5},{5,1},{9,13},{13,9},{2,6},{6,2},{1... | collective-permute-start | bytes 442376 | tf_op jit(solution)/shard_map/ppermute | solution.py:248
  2.9 1.5 %collective-permute-start.2 = (bf16[576,128]{1,0:T(8,128)(2,1)}, bf16[576,128]{1,0:T(8,128)(2,1)S(1)}, u32[]{:S(2)}, u32[]{:S(2)}) collective-permute-start(bf16[576,128]{1,0:T(8,128)(2,1)} %bitcast.14), channel_id=1, source_target_pairs={{0,8},{4,12},{8,0},{12,4},{1,9},{5,13},{9,1},{13,5},{2,10},{6,14},... | collective-permute-start | bytes 442376 | tf_op jit(solution)/shard_map/ppermute | solution.py:248
  4.5 0.7 %copy-done.10 = s32[4,4]{1,0:T(4,128)S(1)} copy-done((s32[4,4]{1,0:T(4,128)S(1)}, s32[4,4]{1,0:T(4,128)}, u32[]{:S(2)}) %copy-start.10) | copy-done | bytes 88
  5.8 0.6 %copy-done.11 = bf16[128,4]{0,1:T(4,128)(2,1)S(1)} copy-done((bf16[128,4]{0,1:T(4,128)(2,1)S(1)}, bf16[128,4]{0,1:T(4,128)(2,1)}, u32[]{:S(2)}) %copy-start.11) | copy-done | bytes 1048
  6.8 0.6 %copy-done.7 = f32[128]{0:T(128)S(1)} copy-done((f32[128]{0:T(128)S(1)}, f32[128]{0:T(128)}, u32[]{:S(2)}) %copy-start.7) | copy-done | bytes 536
  7.4 1.1 %shard_map.127 = (f32[576,128]{1,0:T(8,128)S(1)}, f32[576,128]{1,0:T(8,128)S(1)}, bf16[576,128]{1,0:T(8,128)(2,1)S(1)}, f32[1,128]{1,0:T(1,128)S(1)}, bf16[128,1...) custom-call(bf16[576,128]{1,0:T(8,128)(2,1)S(1)} %bitcast.16, ...), custom_call_target="tpu_custom_call" | custom-call | tf_op jit(solution)/shard_map/pallas_call | solution.py:235
  8.5 0.9 %shard_map.128.refs_0_ = bf16[576,128]{1,0:T(8,128)(2,1)S(1)} custom-call(f32[96,1,128]{2,1,0:T(1,128)S(1)} %broadcast_in_dim.31.row_mask.refs_1_, f32[96,128]{1,0:T(8,128)S(1)} %broadcast_in_dim.32.column_mask.refs_2_, f32[1,128]{1,0:T(1,128)S(1)} %bitcast.21, bf16[128,512]{1,0:T(8,128)(2,1)S(1)} %copy-done, f32[576,128]{1,0:T(8,128)S(1)} %get-tuple-element.36.left.refs_5_, ...), custom_call_target="tpu_custom_call" | custom-call | tf_op jit(solution)/shard_map/pallas_call | solution.py:235
  9.4 2.2 %collective-permute-done.2.refs_0_ = bf16[576,128]{1,0:T(8,128)(2,1)S(1)} collective-permute-done((bf16[576,128]{1,0:T(8,128)(2,1)}, bf16[576,128]{1,0:T(8,128)(2,1)S(1)}, u32[]{:S(2)}, u32[]{:S(2)}) %collective-permute-start.2) | collective-permute-done | bytes 147488 | tf_op jit(solution)/shard_map/ppermute | solution.py:248
  11.6 0.9 %shard_map.129.refs_1_ = bf16[576,128]{1,0:T(8,128)(2,1)S(1)} custom-call(f32[96,1,128]{2,1,0:T(1,128)S(1)} %broadcast_in_dim.31.row_mask.refs_1_, f32[96,128]{1,0:T(8,128)S(1)} %broadcast_in_dim.32.column_mask.refs_2_, f32[1,128]{1,0:T(1,128)S(1)} %bitcast.22, bf16[128,512]{1,0:T(8,128)(2,1)S(1)} %copy-done, f32[576,128]{1,0:T(8,128)S(1)} %get-tuple-element.36.left.refs_5_, ...), custom_call_target="tpu_custom_call" | custom-call | tf_op jit(solution)/shard_map/pallas_call | solution.py:235
  12.7 0.9 %shard_map.131 = (bf16[576,128]{1,0:T(8,128)(2,1)S(1)}, bf16[576,128]{1,0:T(8,128)(2,1)S(1)}, bf16[576,128]{1,0:T(8,128)(2,1)S(1)}, bf16[576,128]{1,0:T(8,128)(2,1)S(1)}) custom-call(bf16[576,128]{1,0:T(8,128)(2,1)S(1)} %collective-permute-done.refs_0_, ...), custom_call_target="tpu_custom_call", output_to_operand_aliasing={{0}: (6, {}), {1}: (7, {}), {2}: (8, {}), {3}: (9, {})} | custom-call | tf_op jit(solution)/shard_map/pallas_call | solution.py:235
  13.6 3.7 %collective-permute-start.3 = (bf16[576,128]{1,0:T(8,128)(2,1)S(1)}, bf16[576,128]{1,0:T(8,128)(2,1)S(1)}, u32[]{:S(2)}, u32[]{:S(2)}) collective-permute-start(bf16[576,128]{1,0:T(8,128)(2,1)S(1)} %get-tuple-element.43), channel_id=1, source_target_pairs={{0,3},{1,2},{2,1},{3,0},{4,7},{5,6},{6,5},{7,4},{8,11},{9,10},{10,... | collective-permute-start | bytes 442376 | tf_op jit(solution)/shard_map/ppermute | solution.py:248
  17.3 0.8 %collective-permute-start.5 = (bf16[576,128]{1,0:T(8,128)(2,1)S(1)}, bf16[576,128]{1,0:T(8,128)(2,1)S(1)}, u32[]{:S(2)}, u32[]{:S(2)}) collective-permute-start(bf16[576,128]{1,0:T(8,128)(2,1)S(1)} %get-tuple-element.45), channel_id=1, source_target_pairs={{0,2},{1,3},{2,0},{3,1},{4,6},{5,7},{6,4},{7,5},{8,10},{9,11},{10,... | collective-permute-start | bytes 442376 | tf_op jit(solution)/shard_map/ppermute | solution.py:248
  18.1 4.1 %collective-permute-done.3.refs_1_ = bf16[576,128]{1,0:T(8,128)(2,1)S(1)} collective-permute-done((bf16[576,128]{1,0:T(8,128)(2,1)S(1)}, bf16[576,128]{1,0:T(8,128)(2,1)S(1)}, u32[]{:S(2)}, u32[]{:S(2)}) %collective-permute-start.3) | collective-permute-done | bytes 147488 | tf_op jit(solution)/shard_map/ppermute | solution.py:248
  22.1 1.5 %collective-permute-done.4.refs_2_ = bf16[576,128]{1,0:T(8,128)(2,1)S(1)} collective-permute-done((bf16[576,128]{1,0:T(8,128)(2,1)S(1)}, bf16[576,128]{1,0:T(8,128)(2,1)S(1)}, u32[]{:S(2)}, u32[]{:S(2)}) %collective-permute-start.4) | collective-permute-done | bytes 147488 | tf_op jit(solution)/shard_map/ppermute | solution.py:248
  23.7 4.1 %collective-permute-done.5.refs_3_ = bf16[576,128]{1,0:T(8,128)(2,1)S(1)} collective-permute-done((bf16[576,128]{1,0:T(8,128)(2,1)S(1)}, bf16[576,128]{1,0:T(8,128)(2,1)S(1)}, u32[]{:S(2)}, u32[]{:S(2)}) %collective-permute-start.5) | collective-permute-done | bytes 147488 | tf_op jit(solution)/shard_map/ppermute | solution.py:248
  27.8 0.7 %shard_map.132 = (bf16[576,128]{1,0:T(8,128)(2,1)S(1)}, bf16[576,128]{1,0:T(8,128)(2,1)S(1)}, bf16[1,24,96]{2,1,0:T(8,128)(2,1)S(1)}) custom-call(bf16[576,128]{1,0:T(8,128)(2,1)S(1)} %bitcast.17, f32[576,128]{1,0:T(8,128)S(1)} %get-tuple-element.31.gate, f32[1,128]{1,0:T(1,128)S(1)} %get-tuple-element.32.product_gain, ...), custom_call_target="tpu_custom_call" | custom-call | tf_op jit(solution)/shard_map/pallas_call | solution.py:235
  28.6 3.4 %collective-permute-start.7 = (bf16[576,128]{1,0:T(8,128)(2,1)S(1)}, bf16[576,128]{1,0:T(8,128)(2,1)S(1)}, u32[]{:S(2)}, u32[]{:S(2)}) collective-permute-start(bf16[576,128]{1,0:T(8,128)(2,1)S(1)} %get-tuple-element.51.refs_0_), channel_id=1, source_target_pairs={{0,2},{1,3},{2,0},{3,1},{4,6},{5,7},{6,4},{7,5},{8,10},{9,11},{10,... | collective-permute-start | bytes 442376 | tf_op jit(solution)/shard_map/ppermute | solution.py:248
  31.9 1.0 %collective-permute-start.8 = (bf16[576,128]{1,0:T(8,128)(2,1)S(1)}, bf16[576,128]{1,0:T(8,128)(2,1)S(1)}, u32[]{:S(2)}, u32[]{:S(2)}) collective-permute-start(bf16[576,128]{1,0:T(8,128)(2,1)S(1)} %get-tuple-element.51.refs_0_), channel_id=1, source_target_pairs={{0,3},{1,2},{2,1},{3,0},{4,7},{5,6},{6,5},{7,4},{8,11},{9,10},{10,... | collective-permute-start | bytes 442376 | tf_op jit(solution)/shard_map/ppermute | solution.py:248
  32.9 3.5 %collective-permute-done.6.refs_1_.attend = bf16[576,128]{1,0:T(8,128)(2,1)S(1)} collective-permute-done((bf16[576,128]{1,0:T(8,128)(2,1)S(1)}, bf16[576,128]{1,0:T(8,128)(2,1)S(1)}, u32[]{:S(2)}, u32[]{:S(2)}) %collective-permute-start.6) | collective-permute-done | bytes 147488 | tf_op jit(solution)/shard_map/ppermute | solution.py:248
  36.7 1.7 %collective-permute-start.10 = (bf16[48,96]{1,0:T(8,128)(2,1)S(1)}, bf16[48,96]{1,0:T(8,128)(2,1)S(1)}, u32[]{:S(2)}, u32[]{:S(2)}) collective-permute-start(bf16[48,96]{1,0:T(8,128)(2,1)S(1)} %bitcast.18), channel_id=1, source_target_pairs={{0,12},{1,8},{2,4},{3,0},{4,13},{5,9},{6,5},{7,1},{8,14},{9,10},{1... | collective-permute-start | bytes 27656 | tf_op jit(solution)/shard_map/ppermute | solution.py:362
  38.4 0.4 shard_map.133
  38.7 3.2 %collective-permute-done.7.refs_0_ = bf16[576,128]{1,0:T(8,128)(2,1)S(1)} collective-permute-done((bf16[576,128]{1,0:T(8,128)(2,1)S(1)}, bf16[576,128]{1,0:T(8,128)(2,1)S(1)}, u32[]{:S(2)}, u32[]{:S(2)}) %collective-permute-start.7) | collective-permute-done | bytes 147488 | tf_op jit(solution)/shard_map/ppermute | solution.py:248
  41.9 0.4 collective-permute-done.10.refs_3_
  42.3 1.8 %shard_map.135 = bf16[576,128]{1,0:T(8,128)(2,1)} custom-call(bf16[576,128]{1,0:T(8,128)(2,1)S(1)} %get-tuple-element.46.middle, f32[96,96]{1,0:T(8,128)S(1)} %get-tuple-element.47.allowed, bf16[128,384]{1,0:T(8,128)(2,1)S(1)} %get-tuple-element.48.w_inputs, bf16[128,128]{1,0:T(8,128)(2,1)S(1)} %get-tuple-element.49.w_out, ...), custom_call_target="tpu_custom_call" | custom-call | tf_op jit(solution)/shard_map/pallas_call | solution.py:235
  (47 shorter events, 1.3 us)
Async XLA Ops:
  0.0 4.5 %copy-start.12 = (s32[96]{0:T(128)S(1)}, s32[96]{0:T(128)}, u32[]{:S(2)}) copy-start(s32[96]{0:T(128)} %param.14) | copy-start | bytes 1156
  0.0 8.5 %collective-permute-start.1 = (bf16[576,128]{1,0:T(8,128)(2,1)}, bf16[576,128]{1,0:T(8,128)(2,1)S(1)}, u32[]{:S(2)}, u32[]{:S(2)}) collective-permute-start(bf16[576,128]{1,0:T(8,128)(2,1)} %bitcast.13), channel_id=1, source_target_pairs={{0,4},{4,0},{8,12},{12,8},{1,5},{5,1},{9,13},{13,9},{2,6},{6,2},{1... | collective-permute-start | bytes 442376 | tf_op jit(solution)/shard_map/ppermute | solution.py:248
  2.9 8.7 %collective-permute-start.2 = (bf16[576,128]{1,0:T(8,128)(2,1)}, bf16[576,128]{1,0:T(8,128)(2,1)S(1)}, u32[]{:S(2)}, u32[]{:S(2)}) collective-permute-start(bf16[576,128]{1,0:T(8,128)(2,1)} %bitcast.14), channel_id=1, source_target_pairs={{0,8},{4,12},{8,0},{12,4},{1,9},{5,13},{9,1},{13,5},{2,10},{6,14},... | collective-permute-start | bytes 442376 | tf_op jit(solution)/shard_map/ppermute | solution.py:248
  4.5 8.2 %collective-permute-start = (bf16[576,128]{1,0:T(8,128)(2,1)}, bf16[576,128]{1,0:T(8,128)(2,1)S(1)}, u32[]{:S(2)}, u32[]{:S(2)}) collective-permute-start(bf16[576,128]{1,0:T(8,128)(2,1)} %bitcast.15), channel_id=1, source_target_pairs={{0,12},{4,8},{8,4},{12,0},{1,13},{5,9},{9,5},{13,1},{2,14},{6,10},... | collective-permute-start | bytes 442376 | tf_op jit(solution)/shard_map/ppermute | solution.py:248
  4.5 0.7 %copy-start.10 = (s32[4,4]{1,0:T(4,128)S(1)}, s32[4,4]{1,0:T(4,128)}, u32[]{:S(2)}) copy-start(s32[4,4]{1,0:T(4,128)} %param.15) | copy-start | bytes 196
  5.4 1.3 %copy-start.4 = (bf16[128,128]{1,0:T(8,128)(2,1)S(1)}, bf16[128,128]{1,0:T(8,128)(2,1)}, u32[]{:S(2)}) copy-start(bf16[128,128]{1,0:T(8,128)(2,1)} %refs_1_.1) | copy-start | bytes 98308
  5.4 1.3 %copy-start.5 = (bf16[128,128]{1,0:T(8,128)(2,1)S(1)}, bf16[128,128]{1,0:T(8,128)(2,1)}, u32[]{:S(2)}) copy-start(bf16[128,128]{1,0:T(8,128)(2,1)} %refs_6_.1) | copy-start | bytes 98308
  5.4 1.3 %copy-start.6 = (bf16[128,128]{1,0:T(8,128)(2,1)S(1)}, bf16[128,128]{1,0:T(8,128)(2,1)}, u32[]{:S(2)}) copy-start(bf16[128,128]{1,0:T(8,128)(2,1)} %refs_7_.1) | copy-start | bytes 98308
  5.6 1.2 %copy-start.2 = (bf16[128,384]{1,0:T(8,128)(2,1)S(1)}, bf16[128,384]{1,0:T(8,128)(2,1)}, u32[]{:S(2)}) copy-start(bf16[128,384]{1,0:T(8,128)(2,1)} %refs_5_.1) | copy-start | bytes 294916
  5.6 0.7 %copy-start.11 = (bf16[128,4]{0,1:T(4,128)(2,1)S(1)}, bf16[128,4]{0,1:T(4,128)(2,1)}, u32[]{:S(2)}) copy-start(bf16[128,4]{0,1:T(4,128)(2,1)} %param.24) | copy-start | bytes 3076
  5.6 1.1 %copy-start.3 = (bf16[128,128]{1,0:T(8,128)(2,1)S(1)}, bf16[128,128]{1,0:T(8,128)(2,1)}, u32[]{:S(2)}) copy-start(bf16[128,128]{1,0:T(8,128)(2,1)} %w_gate.1) | copy-start | bytes 98308
  5.7 1.1 %copy-start.1 = (bf16[24,24,128]{2,1,0:T(8,128)(2,1)S(1)}, bf16[24,24,128]{2,1,0:T(8,128)(2,1)}, u32[]{:S(2)}) copy-start(bf16[24,24,128]{2,1,0:T(8,128)(2,1)} %param.13) | copy-start | bytes 442372
  5.7 1.1 %copy-start = (bf16[128,512]{1,0:T(8,128)(2,1)S(1)}, bf16[128,512]{1,0:T(8,128)(2,1)}, u32[]{:S(2)}) copy-start(bf16[128,512]{1,0:T(8,128)(2,1)} %refs_4_.1) | copy-start | bytes 393220
  6.7 0.7 %copy-start.7 = (f32[128]{0:T(128)S(1)}, f32[128]{0:T(128)}, u32[]{:S(2)}) copy-start(f32[128]{0:T(128)} %param.16) | copy-start | bytes 1540
  6.7 0.7 %copy-start.8 = (f32[128]{0:T(128)S(1)}, f32[128]{0:T(128)}, u32[]{:S(2)}) copy-start(f32[128]{0:T(128)} %param.19) | copy-start | bytes 1540
  6.7 0.7 %copy-start.9 = (f32[128]{0:T(128)S(1)}, f32[128]{0:T(128)}, u32[]{:S(2)}) copy-start(f32[128]{0:T(128)} %param.21) | copy-start | bytes 1540
  13.6 8.5 %collective-permute-start.3 = (bf16[576,128]{1,0:T(8,128)(2,1)S(1)}, bf16[576,128]{1,0:T(8,128)(2,1)S(1)}, u32[]{:S(2)}, u32[]{:S(2)}) collective-permute-start(bf16[576,128]{1,0:T(8,128)(2,1)S(1)} %get-tuple-element.43), channel_id=1, source_target_pairs={{0,3},{1,2},{2,1},{3,0},{4,7},{5,6},{6,5},{7,4},{8,11},{9,10},{10,... | collective-permute-start | bytes 442376 | tf_op jit(solution)/shard_map/ppermute | solution.py:248
  17.3 6.4 %collective-permute-start.4 = (bf16[576,128]{1,0:T(8,128)(2,1)S(1)}, bf16[576,128]{1,0:T(8,128)(2,1)S(1)}, u32[]{:S(2)}, u32[]{:S(2)}) collective-permute-start(bf16[576,128]{1,0:T(8,128)(2,1)S(1)} %get-tuple-element.44), channel_id=1, source_target_pairs={{0,1},{1,0},{2,3},{3,2},{4,5},{5,4},{6,7},{7,6},{8,9},{9,8},{10,11... | collective-permute-start | bytes 442376 | tf_op jit(solution)/shard_map/ppermute | solution.py:248
  17.3 10.5 %collective-permute-start.5 = (bf16[576,128]{1,0:T(8,128)(2,1)S(1)}, bf16[576,128]{1,0:T(8,128)(2,1)S(1)}, u32[]{:S(2)}, u32[]{:S(2)}) collective-permute-start(bf16[576,128]{1,0:T(8,128)(2,1)S(1)} %get-tuple-element.45), channel_id=1, source_target_pairs={{0,2},{1,3},{2,0},{3,1},{4,6},{5,7},{6,4},{7,5},{8,10},{9,11},{10,... | collective-permute-start | bytes 442376 | tf_op jit(solution)/shard_map/ppermute | solution.py:248
  28.5 8.0 %collective-permute-start.6 = (bf16[576,128]{1,0:T(8,128)(2,1)S(1)}, bf16[576,128]{1,0:T(8,128)(2,1)S(1)}, u32[]{:S(2)}, u32[]{:S(2)}) collective-permute-start(bf16[576,128]{1,0:T(8,128)(2,1)S(1)} %get-tuple-element.51.refs_0_), channel_id=1, source_target_pairs={{0,1},{1,0},{2,3},{3,2},{4,5},{5,4},{6,7},{7,6},{8,9},{9,8},{10,11... | collective-permute-start | bytes 442376 | tf_op jit(solution)/shard_map/ppermute | solution.py:248
  28.6 13.4 %collective-permute-start.7 = (bf16[576,128]{1,0:T(8,128)(2,1)S(1)}, bf16[576,128]{1,0:T(8,128)(2,1)S(1)}, u32[]{:S(2)}, u32[]{:S(2)}) collective-permute-start(bf16[576,128]{1,0:T(8,128)(2,1)S(1)} %get-tuple-element.51.refs_0_), channel_id=1, source_target_pairs={{0,2},{1,3},{2,0},{3,1},{4,6},{5,7},{6,4},{7,5},{8,10},{9,11},{10,... | collective-permute-start | bytes 442376 | tf_op jit(solution)/shard_map/ppermute | solution.py:248
  31.9 10.0 %collective-permute-start.8 = (bf16[576,128]{1,0:T(8,128)(2,1)S(1)}, bf16[576,128]{1,0:T(8,128)(2,1)S(1)}, u32[]{:S(2)}, u32[]{:S(2)}) collective-permute-start(bf16[576,128]{1,0:T(8,128)(2,1)S(1)} %get-tuple-element.51.refs_0_), channel_id=1, source_target_pairs={{0,3},{1,2},{2,1},{3,0},{4,7},{5,6},{6,5},{7,4},{8,11},{9,10},{10,... | collective-permute-start | bytes 442376 | tf_op jit(solution)/shard_map/ppermute | solution.py:248
  36.7 5.7 %collective-permute-start.10 = (bf16[48,96]{1,0:T(8,128)(2,1)S(1)}, bf16[48,96]{1,0:T(8,128)(2,1)S(1)}, u32[]{:S(2)}, u32[]{:S(2)}) collective-permute-start(bf16[48,96]{1,0:T(8,128)(2,1)S(1)} %bitcast.18), channel_id=1, source_target_pairs={{0,12},{1,8},{2,4},{3,0},{4,13},{5,9},{6,5},{7,1},{8,14},{9,10},{1... | collective-permute-start | bytes 27656 | tf_op jit(solution)/shard_map/ppermute | solution.py:362
  38.4 4.0 %collective-permute-start.9 = (bf16[48,96]{1,0:T(8,128)(2,1)S(1)}, bf16[48,96]{1,0:T(8,128)(2,1)S(1)}, u32[]{:S(2)}, u32[]{:S(2)}) collective-permute-start(bf16[48,96]{1,0:T(8,128)(2,1)S(1)} %bitcast.19), channel_id=1, source_target_pairs={{0,4},{1,0},{2,12},{3,8},{4,5},{5,1},{6,13},{7,9},{8,6},{9,2},{10,... | collective-permute-start | bytes 27656 | tf_op jit(solution)/shard_map/ppermute | solution.py:362
